TPU v7x, 256 devices: a whole 4x4x8 slice. The times are simulated.
256 devices in a mesh: gx: 64 (over y_hi, x, z), gy: 4 (over y_lo, core).
Axes of the slice: x: 4, y: 4 (y_hi: 2, y_lo: 2; y = y_hi * 2 + y_lo), z: 8, core: 2. Of those that a mesh axis runs over, the one named last changes fastest.
Arguments:
- acid_field: float32 [8, 1024, 16384], P(None, 'gy', 'gx'), may hold values from 0 to 1
- quencher_field: float32 [8, 1024, 16384], P(None, 'gy', 'gx'), may hold values from 0.1 to 0.5
Outputs:
- acid_after: float32 [8, 1024, 16384], P(None, 'gy', 'gx')
- inhibitor: float32 [8, 1024, 16384], P(None, 'gy', 'gx')
- etch_rate: float32 [1024, 16384], P('gy', 'gx')
All inputs are finite; a program needn't handle non-finite values.
Results may differ from a plain program's by a relative error of at most 0.00005.
Values sent between devices are 32-bit elements; how exact they have to be, the bound alone decides.
No kernel may reach another device: no remote copies, remote signals or barrier semaphores. Data moves between devices by JAX's collectives and lax.ppermute only.
A program may use at most 128 MiB of HBM per device.

v0:
```python
import jax
import jax.numpy as jnp
from jax import lax
from jax.sharding import PartitionSpec as P

STEPS = 4
COARSEN = 8


RATE_ACID = 0.15
RATE_QUENCH = 0.05
NEUTRAL = 0.1
DEPROTECT = 0.35
LOADING = 0.8


def padded(block, sides, width):
    for axis, dim in sides:
        count = lax.axis_size(axis)
        forward = [(i, i + 1) for i in range(count - 1)]
        backward = [(target, source) for source, target in forward]
        low = lax.ppermute(
            lax.slice_in_dim(block, block.shape[dim] - width, None, axis=dim), axis, forward
        )
        high = lax.ppermute(lax.slice_in_dim(block, 0, width, axis=dim), axis, backward)
        block = jnp.concatenate([low, block, high], axis=dim)
    return block


def from_behind(block, axis, distance):
    devices = range(lax.axis_size(axis))
    route = [(i - distance, i) for i in devices if i - distance in devices]
    return lax.ppermute(block, axis, route)


def kernel(distance, coarse_tile):
    spread = 25.0 * coarse_tile / 32.0
    offset_float = distance.astype(jnp.float32)
    return jnp.where(
        jnp.abs(distance) <= 2 * coarse_tile,
        jnp.exp(-offset_float * offset_float / (2.0 * spread * spread)),
        0.0,
    )


def advance(extended):
    center = extended[:, :, 1:-1, 1:-1]
    lateral = (
        extended[:, :, 2:, 1:-1]
        + extended[:, :, :-2, 1:-1]
        + extended[:, :, 1:-1, 2:]
        + extended[:, :, 1:-1, :-2]
    )
    edged = jnp.pad(center, ((0, 0), (1, 1), (0, 0), (0, 0)), mode="edge")
    vertical = edged[:, 2:] + edged[:, :-2]
    rates = jnp.array([RATE_ACID, RATE_QUENCH], jnp.float32)[:, None, None, None]
    reaction = NEUTRAL * center[0] * center[1]
    updated = center + rates * (lateral + vertical - 6.0 * center) - reaction[None]
    return (updated, center[0])


def pooling(fine_count):
    return (
        jnp.arange(fine_count)[:, None] // COARSEN == jnp.arange(fine_count // COARSEN)[None, :]
    ).astype(jnp.float32)


def shards(acid_field, quencher_field):
    layers = acid_field.shape[0]
    tile_rows = acid_field.shape[1]
    tile_cols = acid_field.shape[2]
    stacked = jnp.stack([acid_field, quencher_field], 0)
    protect = jnp.ones_like(acid_field)

    def single(turn_index, state_pair):
        fields, guarded = state_pair
        widened = padded(fields, (("gx", 3), ("gy", 2)), 1)
        fields, acid_now = advance(widened)
        return (fields, guarded * jnp.exp(-DEPROTECT * acid_now))

    stacked, protect = lax.fori_loop(0, STEPS, single, (stacked, protect))
    coarse_cols = tile_cols // COARSEN
    coarse_rows = tile_rows // COARSEN
    pool_rows = pooling(tile_rows)
    pool_cols = pooling(tile_cols)
    layer_sum = jnp.sum(1.0 - protect, axis=0)
    col_pooled = jnp.dot(layer_sum, pool_cols, precision=lax.Precision.HIGHEST)
    density = jnp.dot(pool_rows.T, col_pooled, precision=lax.Precision.HIGHEST) / (
        layers * COARSEN * COARSEN
    )
    kernel_total = jnp.sum(kernel(jnp.arange(-2 * coarse_cols, 2 * coarse_cols + 1), coarse_cols))
    col_pieces = []
    for offset in (2, 1, 0, -1, -2):
        col_pieces.append(density if offset == 0 else from_behind(density, "gx", offset))
    stacked_cols = jnp.concatenate(col_pieces, 1)
    weights_band = kernel(
        jnp.arange(5 * coarse_cols)[:, None] - 2 * coarse_cols - jnp.arange(coarse_cols)[None, :],
        coarse_cols,
    )
    across = jnp.dot(stacked_cols, weights_band, precision=lax.Precision.HIGHEST)
    across = across / kernel_total
    row_pieces = []
    for offset in (2, 1, 0, -1, -2):
        row_pieces.append(across if offset == 0 else from_behind(across, "gy", offset))
    stacked_rows = jnp.concatenate(row_pieces, 0)
    row_band = kernel(
        jnp.arange(5 * coarse_rows)[None, :] - 2 * coarse_rows - jnp.arange(coarse_rows)[:, None],
        coarse_cols,
    )
    smoothed = jnp.dot(row_band, stacked_rows, precision=lax.Precision.HIGHEST) / kernel_total
    wide_cols = jnp.dot(smoothed, pool_cols.T, precision=lax.Precision.HIGHEST)
    fine_map = jnp.dot(pool_rows, wide_cols, precision=lax.Precision.HIGHEST)
    etch_rate = (1.0 - protect[0]) * (1.0 - LOADING * fine_map)
    return (stacked[0], protect, etch_rate)


def solution(mesh):
    in_specs = (P(None, "gy", "gx"), P(None, "gy", "gx"))
    out_specs = (P(None, "gy", "gx"), P(None, "gy", "gx"), P("gy", "gx"))
    return jax.shard_map(shards, mesh=mesh, in_specs=in_specs, out_specs=out_specs, check_vma=False)
```

profile of v0, /device:TPU:24, one launch (start us, length us, event | category | flops | bytes accessed | tf_op | source)
XLA Modules:
  0.0 302.1 jit_solution(9903799315966541648)
XLA Ops:
  0.6 3.0 %copy.27 = f32[8,256,256]{1,0,2:T(8,128)} copy(f32[8,256,256]{2,1,0:T(8,128)} %param.6) | data formatting | bytes 4194304 | tf_op args[1]
  3.7 3.0 %copy.26 = f32[8,256,256]{1,0,2:T(8,128)} copy(f32[8,256,256]{2,1,0:T(8,128)} %param.5) | data formatting | bytes 4194304 | tf_op args[0]
  6.7 4.5 %pad_maximum_fusion.13 = f32[2,8,256,256]{2,1,3,0:T(8,128)} fusion(f32[1,8,256,256]{2,1,3,0:T(8,128)} %bitcast.22, f32[1,8,256,256]{2,1,3,0:T(8,128)} %bitcast.23), kind=kLoop, calls=%fused_computation.24 | loop fusion | flops 1048576 | bytes 8388608 | tf_op jit(solution)/shard_map/stack | solution.py:72
  11.2 247.6 %while.14 = (s32[]{:T(128)}, f32[2,8,256,256]{2,1,3,0:T(8,128)}, f32[8,256,256]{1,0,2:T(8,128)S(1)}, s32[]{:T(128)}, f32[2]{0:T(128)S(1)}, /*index=5*/s32[]{:T(128)}) while((s32[]{:T(128)}, f32[2,8,256,256]{2,1,3,0:T(8,128)}, f32[8,256,256]{1,0,2:T(8,128)S(1)}, s32[]{:T(128)}, f32[2]{0:T(128)S(1)}, ...), condition=%wide.region_1.2_spmd.clone.clone, body=%wide.region_0.1_spmd.sunk.clone.clone.sunk | while | flops 23609472 | bytes 85460816 | solution.py:81
  11.9 3.8 %collective-permute-start = (f32[2,8,256,1]{2,1,3,0:T(8,128)S(1)}, f32[2,8,256,1]{2,1,3,0:T(8,128)S(1)}, u32[]{:S(2)}, u32[]{:S(2)}) collective-permute-start(f32[2,8,256,1]{2,1,3,0:T(8,128)S(1)} %get-tuple-element.100), channel_id=1, source_target_pairs={{0,4},{4,8},{8,12},{12,16},{16,20},{20,24},{24,28},{28,32},{32,36}... | collective-permute-start | bytes 49160 | tf_op jit(solution)/shard_map/while/body/eval_jaxpr/ppermute | solution.py:22
  15.8 8.7 %collective-permute-start.1 = (f32[2,8,256,1]{2,1,3,0:T(8,128)S(1)}, f32[2,8,256,1]{2,1,3,0:T(8,128)S(1)}, u32[]{:S(2)}, u32[]{:S(2)}) collective-permute-start(f32[2,8,256,1]{2,1,3,0:T(8,128)S(1)} %get-tuple-element.101), channel_id=1, source_target_pairs={{4,0},{8,4},{12,8},{16,12},{20,16},{24,20},{28,24},{32,28},{36,32}... | collective-permute-start | bytes 49160 | tf_op jit(solution)/shard_map/while/body/eval_jaxpr/ppermute | solution.py:25
  24.5 5.6 %copy.38 = f32[2,8,256,256]{3,1,2,0:T(8,128)} copy(f32[2,8,256,256]{2,1,3,0:T(8,128)} %get-tuple-element.111) | data formatting | bytes 8388608 | tf_op jit(solution)/shard_map/while
  30.1 4.2 %fusion.62 = (f32[2,1,256,256]{3,1,2,0:T(1,128)S(1)}, f32[2,1,256,256]{3,1,2,0:T(1,128)S(1)}) fusion(f32[2,8,256,256]{3,1,2,0:T(8,128)} %copy.38), kind=kLoop, calls=%fused_computation.84.clone.1 | loop fusion | bytes 2097152 | tf_op jit(solution)/shard_map/while/body/eval_jaxpr/jit(_pad)/slice | solution.py:54
  34.3 2.6 bitcast_multiply_fusion.2
  39.0 2.0 copy.40
  41.9 2.1 collective-permute-start.2
  44.0 3.6 %collective-permute-start.3 = (f32[2,8,1,258]{3,1,2,0:T(8,128)S(1)}, f32[2,8,1,258]{3,1,2,0:T(8,128)S(1)}, u32[]{:S(2)}, u32[]{:S(2)}) collective-permute-start(f32[2,8,1,258]{3,1,2,0:T(8,128)S(1)} %get-tuple-element.103), channel_id=1, source_target_pairs={{1,0},{2,1},{3,2},{5,4},{6,5},{7,6},{9,8},{10,9},{11,10},{13,12},{... | collective-permute-start | bytes 49544 | tf_op jit(solution)/shard_map/while/body/eval_jaxpr/ppermute | solution.py:25
  49.2 3.1 %copy.41 = f32[8,256,256]{2,0,1:T(8,128)} copy(f32[8,256,256]{1,0,2:T(8,128)} %multiply_bitcast_fusion.2) | data formatting | bytes 4194304 | tf_op jit(solution)/shard_map/while/body/eval_jaxpr/sub | solution.py:58
  52.4 15.7 %fusion.64 = f32[2,8,256,256]{3,1,2,0:T(8,128)} fusion(f32[2,8,256,256]{3,1,2,0:T(8,128)} %copy.38, f32[2,1,256,256]{3,1,2,0:T(1,128)S(1)} %get-tuple-element.98, f32[2,1,256,256]{3,1,2,0:T(1,128)S(1)} %get-tuple-element.99, f32[2,8,256,1]{3,1,2,0:T(8,128)S(1)} %copy.39, f32[2,8,256,1]{3,1,2,0:T(8,128)} %copy.40, ...), kind=kLoop, calls=%fused_computation.6.clone.1 | loop fusion | flops 20971520 | bytes 11600136 | tf_op jit(solution)/shard_map/while/body/eval_jaxpr/sub | solution.py:58
  68.1 5.7 %copy.42 = f32[2,8,256,256]{2,1,3,0:T(8,128)} copy(f32[2,8,256,256]{3,1,2,0:T(8,128)} %fusion.64) | data formatting | bytes 8388608 | tf_op jit(solution)/shard_map/while
  76.5 9.6 %collective-permute-start.1 = (f32[2,8,256,1]{2,1,3,0:T(8,128)S(1)}, f32[2,8,256,1]{2,1,3,0:T(8,128)S(1)}, u32[]{:S(2)}, u32[]{:S(2)}) collective-permute-start(f32[2,8,256,1]{2,1,3,0:T(8,128)S(1)} %get-tuple-element.101), channel_id=1, source_target_pairs={{4,0},{8,4},{12,8},{16,12},{20,16},{24,20},{28,24},{32,28},{36,32}... | collective-permute-start | bytes 49160 | tf_op jit(solution)/shard_map/while/body/eval_jaxpr/ppermute | solution.py:25
  86.1 5.6 %copy.38 = f32[2,8,256,256]{3,1,2,0:T(8,128)} copy(f32[2,8,256,256]{2,1,3,0:T(8,128)} %get-tuple-element.111) | data formatting | bytes 8388608 | tf_op jit(solution)/shard_map/while
  91.7 4.2 %fusion.62 = (f32[2,1,256,256]{3,1,2,0:T(1,128)S(1)}, f32[2,1,256,256]{3,1,2,0:T(1,128)S(1)}) fusion(f32[2,8,256,256]{3,1,2,0:T(8,128)} %copy.38), kind=kLoop, calls=%fused_computation.84.clone.1 | loop fusion | bytes 2097152 | tf_op jit(solution)/shard_map/while/body/eval_jaxpr/jit(_pad)/slice | solution.py:54
  95.9 2.6 bitcast_multiply_fusion.2
  103.6 2.1 collective-permute-start.2
  105.7 3.6 %collective-permute-start.3 = (f32[2,8,1,258]{3,1,2,0:T(8,128)S(1)}, f32[2,8,1,258]{3,1,2,0:T(8,128)S(1)}, u32[]{:S(2)}, u32[]{:S(2)}) collective-permute-start(f32[2,8,1,258]{3,1,2,0:T(8,128)S(1)} %get-tuple-element.103), channel_id=1, source_target_pairs={{1,0},{2,1},{3,2},{5,4},{6,5},{7,6},{9,8},{10,9},{11,10},{13,12},{... | collective-permute-start | bytes 49544 | tf_op jit(solution)/shard_map/while/body/eval_jaxpr/ppermute | solution.py:25
  110.9 3.1 %copy.41 = f32[8,256,256]{2,0,1:T(8,128)} copy(f32[8,256,256]{1,0,2:T(8,128)} %multiply_bitcast_fusion.2) | data formatting | bytes 4194304 | tf_op jit(solution)/shard_map/while/body/eval_jaxpr/sub | solution.py:58
  114.0 15.7 %fusion.64 = f32[2,8,256,256]{3,1,2,0:T(8,128)} fusion(f32[2,8,256,256]{3,1,2,0:T(8,128)} %copy.38, f32[2,1,256,256]{3,1,2,0:T(1,128)S(1)} %get-tuple-element.98, f32[2,1,256,256]{3,1,2,0:T(1,128)S(1)} %get-tuple-element.99, f32[2,8,256,1]{3,1,2,0:T(8,128)S(1)} %copy.39, f32[2,8,256,1]{3,1,2,0:T(8,128)} %copy.40, ...), kind=kLoop, calls=%fused_computation.6.clone.1 | loop fusion | flops 20971520 | bytes 11600136 | tf_op jit(solution)/shard_map/while/body/eval_jaxpr/sub | solution.py:58
  129.8 5.7 %copy.42 = f32[2,8,256,256]{2,1,3,0:T(8,128)} copy(f32[2,8,256,256]{3,1,2,0:T(8,128)} %fusion.64) | data formatting | bytes 8388608 | tf_op jit(solution)/shard_map/while
  138.2 9.6 %collective-permute-start.1 = (f32[2,8,256,1]{2,1,3,0:T(8,128)S(1)}, f32[2,8,256,1]{2,1,3,0:T(8,128)S(1)}, u32[]{:S(2)}, u32[]{:S(2)}) collective-permute-start(f32[2,8,256,1]{2,1,3,0:T(8,128)S(1)} %get-tuple-element.101), channel_id=1, source_target_pairs={{4,0},{8,4},{12,8},{16,12},{20,16},{24,20},{28,24},{32,28},{36,32}... | collective-permute-start | bytes 49160 | tf_op jit(solution)/shard_map/while/body/eval_jaxpr/ppermute | solution.py:25
  147.8 5.6 %copy.38 = f32[2,8,256,256]{3,1,2,0:T(8,128)} copy(f32[2,8,256,256]{2,1,3,0:T(8,128)} %get-tuple-element.111) | data formatting | bytes 8388608 | tf_op jit(solution)/shard_map/while
  153.4 4.2 %fusion.62 = (f32[2,1,256,256]{3,1,2,0:T(1,128)S(1)}, f32[2,1,256,256]{3,1,2,0:T(1,128)S(1)}) fusion(f32[2,8,256,256]{3,1,2,0:T(8,128)} %copy.38), kind=kLoop, calls=%fused_computation.84.clone.1 | loop fusion | bytes 2097152 | tf_op jit(solution)/shard_map/while/body/eval_jaxpr/jit(_pad)/slice | solution.py:54
  157.6 2.6 bitcast_multiply_fusion.2
  162.3 2.0 copy.40
  165.2 2.1 collective-permute-start.2
  167.3 3.6 %collective-permute-start.3 = (f32[2,8,1,258]{3,1,2,0:T(8,128)S(1)}, f32[2,8,1,258]{3,1,2,0:T(8,128)S(1)}, u32[]{:S(2)}, u32[]{:S(2)}) collective-permute-start(f32[2,8,1,258]{3,1,2,0:T(8,128)S(1)} %get-tuple-element.103), channel_id=1, source_target_pairs={{1,0},{2,1},{3,2},{5,4},{6,5},{7,6},{9,8},{10,9},{11,10},{13,12},{... | collective-permute-start | bytes 49544 | tf_op jit(solution)/shard_map/while/body/eval_jaxpr/ppermute | solution.py:25
  172.6 3.1 %copy.41 = f32[8,256,256]{2,0,1:T(8,128)} copy(f32[8,256,256]{1,0,2:T(8,128)} %multiply_bitcast_fusion.2) | data formatting | bytes 4194304 | tf_op jit(solution)/shard_map/while/body/eval_jaxpr/sub | solution.py:58
  175.7 15.7 %fusion.64 = f32[2,8,256,256]{3,1,2,0:T(8,128)} fusion(f32[2,8,256,256]{3,1,2,0:T(8,128)} %copy.38, f32[2,1,256,256]{3,1,2,0:T(1,128)S(1)} %get-tuple-element.98, f32[2,1,256,256]{3,1,2,0:T(1,128)S(1)} %get-tuple-element.99, f32[2,8,256,1]{3,1,2,0:T(8,128)S(1)} %copy.39, f32[2,8,256,1]{3,1,2,0:T(8,128)} %copy.40, ...), kind=kLoop, calls=%fused_computation.6.clone.1 | loop fusion | flops 20971520 | bytes 11600136 | tf_op jit(solution)/shard_map/while/body/eval_jaxpr/sub | solution.py:58
  191.4 5.7 %copy.42 = f32[2,8,256,256]{2,1,3,0:T(8,128)} copy(f32[2,8,256,256]{3,1,2,0:T(8,128)} %fusion.64) | data formatting | bytes 8388608 | tf_op jit(solution)/shard_map/while
  199.8 9.6 %collective-permute-start.1 = (f32[2,8,256,1]{2,1,3,0:T(8,128)S(1)}, f32[2,8,256,1]{2,1,3,0:T(8,128)S(1)}, u32[]{:S(2)}, u32[]{:S(2)}) collective-permute-start(f32[2,8,256,1]{2,1,3,0:T(8,128)S(1)} %get-tuple-element.101), channel_id=1, source_target_pairs={{4,0},{8,4},{12,8},{16,12},{20,16},{24,20},{28,24},{32,28},{36,32}... | collective-permute-start | bytes 49160 | tf_op jit(solution)/shard_map/while/body/eval_jaxpr/ppermute | solution.py:25
  209.5 5.6 %copy.38 = f32[2,8,256,256]{3,1,2,0:T(8,128)} copy(f32[2,8,256,256]{2,1,3,0:T(8,128)} %get-tuple-element.111) | data formatting | bytes 8388608 | tf_op jit(solution)/shard_map/while
  215.0 4.2 %fusion.62 = (f32[2,1,256,256]{3,1,2,0:T(1,128)S(1)}, f32[2,1,256,256]{3,1,2,0:T(1,128)S(1)}) fusion(f32[2,8,256,256]{3,1,2,0:T(8,128)} %copy.38), kind=kLoop, calls=%fused_computation.84.clone.1 | loop fusion | bytes 2097152 | tf_op jit(solution)/shard_map/while/body/eval_jaxpr/jit(_pad)/slice | solution.py:54
  219.2 2.6 bitcast_multiply_fusion.2
  226.9 2.1 collective-permute-start.2
  229.0 3.6 %collective-permute-start.3 = (f32[2,8,1,258]{3,1,2,0:T(8,128)S(1)}, f32[2,8,1,258]{3,1,2,0:T(8,128)S(1)}, u32[]{:S(2)}, u32[]{:S(2)}) collective-permute-start(f32[2,8,1,258]{3,1,2,0:T(8,128)S(1)} %get-tuple-element.103), channel_id=1, source_target_pairs={{1,0},{2,1},{3,2},{5,4},{6,5},{7,6},{9,8},{10,9},{11,10},{13,12},{... | collective-permute-start | bytes 49544 | tf_op jit(solution)/shard_map/while/body/eval_jaxpr/ppermute | solution.py:25
  234.2 3.1 %copy.41 = f32[8,256,256]{2,0,1:T(8,128)} copy(f32[8,256,256]{1,0,2:T(8,128)} %multiply_bitcast_fusion.2) | data formatting | bytes 4194304 | tf_op jit(solution)/shard_map/while/body/eval_jaxpr/sub | solution.py:58
  237.3 15.7 %fusion.64 = f32[2,8,256,256]{3,1,2,0:T(8,128)} fusion(f32[2,8,256,256]{3,1,2,0:T(8,128)} %copy.38, f32[2,1,256,256]{3,1,2,0:T(1,128)S(1)} %get-tuple-element.98, f32[2,1,256,256]{3,1,2,0:T(1,128)S(1)} %get-tuple-element.99, f32[2,8,256,1]{3,1,2,0:T(8,128)S(1)} %copy.39, f32[2,8,256,1]{3,1,2,0:T(8,128)} %copy.40, ...), kind=kLoop, calls=%fused_computation.6.clone.1 | loop fusion | flops 20971520 | bytes 11600136 | tf_op jit(solution)/shard_map/while/body/eval_jaxpr/sub | solution.py:58
  253.1 5.7 %copy.42 = f32[2,8,256,256]{2,1,3,0:T(8,128)} copy(f32[2,8,256,256]{3,1,2,0:T(8,128)} %fusion.64) | data formatting | bytes 8388608 | tf_op jit(solution)/shard_map/while
  264.0 9.6 %collective-permute-start.6 = (f32[32,32]{1,0:T(8,128)S(1)}, f32[32,32]{1,0:T(8,128)S(1)}, u32[]{:S(2)}, u32[]{:S(2)}) collective-permute-start(f32[32,32]{1,0:T(8,128)S(1)} %convolution_multiply_fusion.1), channel_id=1, source_target_pairs={{4,0},{8,4},{12,8},{16,12},{20,16},{24,20},{28,24},{32,28},{36,32}... | collective-permute-start | bytes 12296 | tf_op jit(solution)/shard_map/ppermute | solution.py:33
  273.7 4.8 %collective-permute-start.7 = (f32[32,32]{1,0:T(8,128)S(1)}, f32[32,32]{1,0:T(8,128)S(1)}, u32[]{:S(2)}, u32[]{:S(2)}) collective-permute-start(f32[32,32]{1,0:T(8,128)S(1)} %convolution_multiply_fusion.1), channel_id=1, source_target_pairs={{8,0},{12,4},{16,8},{20,12},{24,16},{28,20},{32,24},{36,28},{40,32... | collective-permute-start | bytes 12296 | tf_op jit(solution)/shard_map/ppermute | solution.py:33
  278.5 5.3 %copy.28 = f32[2,8,256,256]{3,2,1,0:T(8,128)} copy(f32[2,8,256,256]{2,1,3,0:T(8,128)} %get-tuple-element.26) | data formatting | bytes 8388608 | tf_op jit(solution)/shard_map/while | solution.py:81
  288.8 3.6 %collective-permute-start.10 = (f32[32,32]{0,1:T(8,128)S(1)}, f32[32,32]{0,1:T(8,128)S(1)}, u32[]{:S(2)}, u32[]{:S(2)}) collective-permute-start(f32[32,32]{0,1:T(8,128)S(1)} %convolution_divide_fusion.1), channel_id=1, source_target_pairs={{1,0},{2,1},{3,2},{5,4},{6,5},{7,6},{9,8},{10,9},{11,10},{13,12},{... | collective-permute-start | bytes 12296 | tf_op jit(solution)/shard_map/ppermute | solution.py:33
  294.0 3.0 %slice_bitcast_fusion = f32[8,256,256]{2,1,0:T(8,128)} fusion(f32[2,8,256,256]{3,2,1,0:T(8,128)} %copy.28), kind=kLoop, calls=%fused_computation.25 | loop fusion | bytes 4194304 | tf_op jit(solution)/shard_map/squeeze | solution.py:114
  (90 shorter events, 48.1 us)
Async XLA Ops:
  6.7 4.5 %copy-start.3 = (f32[2]{0:T(128)S(1)}, f32[2]{0:T(128)}, u32[]{:S(2)}) copy-start(f32[2]{0:T(128)} %constant.60.clone..sunk.3) | copy-start | bytes 28
  11.9 26.2 %collective-permute-start = (f32[2,8,256,1]{2,1,3,0:T(8,128)S(1)}, f32[2,8,256,1]{2,1,3,0:T(8,128)S(1)}, u32[]{:S(2)}, u32[]{:S(2)}) collective-permute-start(f32[2,8,256,1]{2,1,3,0:T(8,128)S(1)} %get-tuple-element.100), channel_id=1, source_target_pairs={{0,4},{4,8},{8,12},{12,16},{16,20},{20,24},{24,28},{28,32},{32,36}... | collective-permute-start | bytes 49160 | tf_op jit(solution)/shard_map/while/body/eval_jaxpr/ppermute | solution.py:22
  15.8 23.2 %collective-permute-start.1 = (f32[2,8,256,1]{2,1,3,0:T(8,128)S(1)}, f32[2,8,256,1]{2,1,3,0:T(8,128)S(1)}, u32[]{:S(2)}, u32[]{:S(2)}) collective-permute-start(f32[2,8,256,1]{2,1,3,0:T(8,128)S(1)} %get-tuple-element.101), channel_id=1, source_target_pairs={{4,0},{8,4},{12,8},{16,12},{20,16},{24,20},{28,24},{32,28},{36,32}... | collective-permute-start | bytes 49160 | tf_op jit(solution)/shard_map/while/body/eval_jaxpr/ppermute | solution.py:25
  36.8 1.3 copy-start.1
  40.9 6.7 %copy-start = (f32[2,8,256,256]{2,1,3,0:T(8,128)S(1)}, f32[2,8,256,256]{2,1,3,0:T(8,128)}, u32[]{:S(2)}) copy-start(f32[2,8,256,256]{2,1,3,0:T(8,128)} %get-tuple-element.111) | copy-start | bytes 12582916 | tf_op jit(solution)/shard_map/while
  41.9 10.4 %collective-permute-start.2 = (f32[2,8,1,258]{3,1,2,0:T(8,128)S(1)}, f32[2,8,1,258]{3,1,2,0:T(8,128)S(1)}, u32[]{:S(2)}, u32[]{:S(2)}) collective-permute-start(f32[2,8,1,258]{3,1,2,0:T(8,128)S(1)} %get-tuple-element.102), channel_id=1, source_target_pairs={{0,1},{1,2},{2,3},{4,5},{5,6},{6,7},{8,9},{9,10},{10,11},{12,13},{... | collective-permute-start | bytes 49544 | tf_op jit(solution)/shard_map/while/body/eval_jaxpr/ppermute | solution.py:22
  44.0 8.4 %collective-permute-start.3 = (f32[2,8,1,258]{3,1,2,0:T(8,128)S(1)}, f32[2,8,1,258]{3,1,2,0:T(8,128)S(1)}, u32[]{:S(2)}, u32[]{:S(2)}) collective-permute-start(f32[2,8,1,258]{3,1,2,0:T(8,128)S(1)} %get-tuple-element.103), channel_id=1, source_target_pairs={{1,0},{2,1},{3,2},{5,4},{6,5},{7,6},{9,8},{10,9},{11,10},{13,12},{... | collective-permute-start | bytes 49544 | tf_op jit(solution)/shard_map/while/body/eval_jaxpr/ppermute | solution.py:25
  68.1 5.7 %copy-start.2 = (f32[8,256,256]{1,0,2:T(8,128)S(1)}, f32[8,256,256]{1,0,2:T(8,128)}, u32[]{:S(2)}) copy-start(f32[8,256,256]{1,0,2:T(8,128)} %copy-done.1) | copy-start | bytes 6291460 | tf_op jit(solution)/shard_map/while
  74.6 25.2 %collective-permute-start = (f32[2,8,256,1]{2,1,3,0:T(8,128)S(1)}, f32[2,8,256,1]{2,1,3,0:T(8,128)S(1)}, u32[]{:S(2)}, u32[]{:S(2)}) collective-permute-start(f32[2,8,256,1]{2,1,3,0:T(8,128)S(1)} %get-tuple-element.100), channel_id=1, source_target_pairs={{0,4},{4,8},{8,12},{12,16},{16,20},{20,24},{24,28},{28,32},{32,36}... | collective-permute-start | bytes 49160 | tf_op jit(solution)/shard_map/while/body/eval_jaxpr/ppermute | solution.py:22
  76.5 24.1 %collective-permute-start.1 = (f32[2,8,256,1]{2,1,3,0:T(8,128)S(1)}, f32[2,8,256,1]{2,1,3,0:T(8,128)S(1)}, u32[]{:S(2)}, u32[]{:S(2)}) collective-permute-start(f32[2,8,256,1]{2,1,3,0:T(8,128)S(1)} %get-tuple-element.101), channel_id=1, source_target_pairs={{4,0},{8,4},{12,8},{16,12},{20,16},{24,20},{28,24},{32,28},{36,32}... | collective-permute-start | bytes 49160 | tf_op jit(solution)/shard_map/while/body/eval_jaxpr/ppermute | solution.py:25
  98.5 1.3 copy-start.1
  102.6 6.7 %copy-start = (f32[2,8,256,256]{2,1,3,0:T(8,128)S(1)}, f32[2,8,256,256]{2,1,3,0:T(8,128)}, u32[]{:S(2)}) copy-start(f32[2,8,256,256]{2,1,3,0:T(8,128)} %get-tuple-element.111) | copy-start | bytes 12582916 | tf_op jit(solution)/shard_map/while
  103.6 10.4 %collective-permute-start.2 = (f32[2,8,1,258]{3,1,2,0:T(8,128)S(1)}, f32[2,8,1,258]{3,1,2,0:T(8,128)S(1)}, u32[]{:S(2)}, u32[]{:S(2)}) collective-permute-start(f32[2,8,1,258]{3,1,2,0:T(8,128)S(1)} %get-tuple-element.102), channel_id=1, source_target_pairs={{0,1},{1,2},{2,3},{4,5},{5,6},{6,7},{8,9},{9,10},{10,11},{12,13},{... | collective-permute-start | bytes 49544 | tf_op jit(solution)/shard_map/while/body/eval_jaxpr/ppermute | solution.py:22
  105.7 8.4 %collective-permute-start.3 = (f32[2,8,1,258]{3,1,2,0:T(8,128)S(1)}, f32[2,8,1,258]{3,1,2,0:T(8,128)S(1)}, u32[]{:S(2)}, u32[]{:S(2)}) collective-permute-start(f32[2,8,1,258]{3,1,2,0:T(8,128)S(1)} %get-tuple-element.103), channel_id=1, source_target_pairs={{1,0},{2,1},{3,2},{5,4},{6,5},{7,6},{9,8},{10,9},{11,10},{13,12},{... | collective-permute-start | bytes 49544 | tf_op jit(solution)/shard_map/while/body/eval_jaxpr/ppermute | solution.py:25
  129.8 5.7 %copy-start.2 = (f32[8,256,256]{1,0,2:T(8,128)S(1)}, f32[8,256,256]{1,0,2:T(8,128)}, u32[]{:S(2)}) copy-start(f32[8,256,256]{1,0,2:T(8,128)} %copy-done.1) | copy-start | bytes 6291460 | tf_op jit(solution)/shard_map/while
  136.2 25.2 %collective-permute-start = (f32[2,8,256,1]{2,1,3,0:T(8,128)S(1)}, f32[2,8,256,1]{2,1,3,0:T(8,128)S(1)}, u32[]{:S(2)}, u32[]{:S(2)}) collective-permute-start(f32[2,8,256,1]{2,1,3,0:T(8,128)S(1)} %get-tuple-element.100), channel_id=1, source_target_pairs={{0,4},{4,8},{8,12},{12,16},{16,20},{20,24},{24,28},{28,32},{32,36}... | collective-permute-start | bytes 49160 | tf_op jit(solution)/shard_map/while/body/eval_jaxpr/ppermute | solution.py:22
  138.2 24.1 %collective-permute-start.1 = (f32[2,8,256,1]{2,1,3,0:T(8,128)S(1)}, f32[2,8,256,1]{2,1,3,0:T(8,128)S(1)}, u32[]{:S(2)}, u32[]{:S(2)}) collective-permute-start(f32[2,8,256,1]{2,1,3,0:T(8,128)S(1)} %get-tuple-element.101), channel_id=1, source_target_pairs={{4,0},{8,4},{12,8},{16,12},{20,16},{24,20},{28,24},{32,28},{36,32}... | collective-permute-start | bytes 49160 | tf_op jit(solution)/shard_map/while/body/eval_jaxpr/ppermute | solution.py:25
  160.1 1.3 copy-start.1
  164.2 6.7 %copy-start = (f32[2,8,256,256]{2,1,3,0:T(8,128)S(1)}, f32[2,8,256,256]{2,1,3,0:T(8,128)}, u32[]{:S(2)}) copy-start(f32[2,8,256,256]{2,1,3,0:T(8,128)} %get-tuple-element.111) | copy-start | bytes 12582916 | tf_op jit(solution)/shard_map/while
  165.2 10.4 %collective-permute-start.2 = (f32[2,8,1,258]{3,1,2,0:T(8,128)S(1)}, f32[2,8,1,258]{3,1,2,0:T(8,128)S(1)}, u32[]{:S(2)}, u32[]{:S(2)}) collective-permute-start(f32[2,8,1,258]{3,1,2,0:T(8,128)S(1)} %get-tuple-element.102), channel_id=1, source_target_pairs={{0,1},{1,2},{2,3},{4,5},{5,6},{6,7},{8,9},{9,10},{10,11},{12,13},{... | collective-permute-start | bytes 49544 | tf_op jit(solution)/shard_map/while/body/eval_jaxpr/ppermute | solution.py:22
  167.3 8.4 %collective-permute-start.3 = (f32[2,8,1,258]{3,1,2,0:T(8,128)S(1)}, f32[2,8,1,258]{3,1,2,0:T(8,128)S(1)}, u32[]{:S(2)}, u32[]{:S(2)}) collective-permute-start(f32[2,8,1,258]{3,1,2,0:T(8,128)S(1)} %get-tuple-element.103), channel_id=1, source_target_pairs={{1,0},{2,1},{3,2},{5,4},{6,5},{7,6},{9,8},{10,9},{11,10},{13,12},{... | collective-permute-start | bytes 49544 | tf_op jit(solution)/shard_map/while/body/eval_jaxpr/ppermute | solution.py:25
  191.4 5.7 %copy-start.2 = (f32[8,256,256]{1,0,2:T(8,128)S(1)}, f32[8,256,256]{1,0,2:T(8,128)}, u32[]{:S(2)}) copy-start(f32[8,256,256]{1,0,2:T(8,128)} %copy-done.1) | copy-start | bytes 6291460 | tf_op jit(solution)/shard_map/while
  197.9 25.2 %collective-permute-start = (f32[2,8,256,1]{2,1,3,0:T(8,128)S(1)}, f32[2,8,256,1]{2,1,3,0:T(8,128)S(1)}, u32[]{:S(2)}, u32[]{:S(2)}) collective-permute-start(f32[2,8,256,1]{2,1,3,0:T(8,128)S(1)} %get-tuple-element.100), channel_id=1, source_target_pairs={{0,4},{4,8},{8,12},{12,16},{16,20},{20,24},{24,28},{28,32},{32,36}... | collective-permute-start | bytes 49160 | tf_op jit(solution)/shard_map/while/body/eval_jaxpr/ppermute | solution.py:22
  199.8 24.1 %collective-permute-start.1 = (f32[2,8,256,1]{2,1,3,0:T(8,128)S(1)}, f32[2,8,256,1]{2,1,3,0:T(8,128)S(1)}, u32[]{:S(2)}, u32[]{:S(2)}) collective-permute-start(f32[2,8,256,1]{2,1,3,0:T(8,128)S(1)} %get-tuple-element.101), channel_id=1, source_target_pairs={{4,0},{8,4},{12,8},{16,12},{20,16},{24,20},{28,24},{32,28},{36,32}... | collective-permute-start | bytes 49160 | tf_op jit(solution)/shard_map/while/body/eval_jaxpr/ppermute | solution.py:25
  221.8 1.3 copy-start.1
  225.9 6.7 %copy-start = (f32[2,8,256,256]{2,1,3,0:T(8,128)S(1)}, f32[2,8,256,256]{2,1,3,0:T(8,128)}, u32[]{:S(2)}) copy-start(f32[2,8,256,256]{2,1,3,0:T(8,128)} %get-tuple-element.111) | copy-start | bytes 12582916 | tf_op jit(solution)/shard_map/while
  226.9 10.4 %collective-permute-start.2 = (f32[2,8,1,258]{3,1,2,0:T(8,128)S(1)}, f32[2,8,1,258]{3,1,2,0:T(8,128)S(1)}, u32[]{:S(2)}, u32[]{:S(2)}) collective-permute-start(f32[2,8,1,258]{3,1,2,0:T(8,128)S(1)} %get-tuple-element.102), channel_id=1, source_target_pairs={{0,1},{1,2},{2,3},{4,5},{5,6},{6,7},{8,9},{9,10},{10,11},{12,13},{... | collective-permute-start | bytes 49544 | tf_op jit(solution)/shard_map/while/body/eval_jaxpr/ppermute | solution.py:22
  229.0 8.4 %collective-permute-start.3 = (f32[2,8,1,258]{3,1,2,0:T(8,128)S(1)}, f32[2,8,1,258]{3,1,2,0:T(8,128)S(1)}, u32[]{:S(2)}, u32[]{:S(2)}) collective-permute-start(f32[2,8,1,258]{3,1,2,0:T(8,128)S(1)} %get-tuple-element.103), channel_id=1, source_target_pairs={{1,0},{2,1},{3,2},{5,4},{6,5},{7,6},{9,8},{10,9},{11,10},{13,12},{... | collective-permute-start | bytes 49544 | tf_op jit(solution)/shard_map/while/body/eval_jaxpr/ppermute | solution.py:25
  253.1 5.7 %copy-start.2 = (f32[8,256,256]{1,0,2:T(8,128)S(1)}, f32[8,256,256]{1,0,2:T(8,128)}, u32[]{:S(2)}) copy-start(f32[8,256,256]{1,0,2:T(8,128)} %copy-done.1) | copy-start | bytes 6291460 | tf_op jit(solution)/shard_map/while
  260.2 24.3 %collective-permute-start.4 = (f32[32,32]{1,0:T(8,128)S(1)}, f32[32,32]{1,0:T(8,128)S(1)}, u32[]{:S(2)}, u32[]{:S(2)}) collective-permute-start(f32[32,32]{1,0:T(8,128)S(1)} %convolution_multiply_fusion.1), channel_id=1, source_target_pairs={{0,8},{4,12},{8,16},{12,20},{16,24},{20,28},{24,32},{28,36},{32,40... | collective-permute-start | bytes 12296 | tf_op jit(solution)/shard_map/ppermute | solution.py:33
  262.1 22.3 %collective-permute-start.5 = (f32[32,32]{1,0:T(8,128)S(1)}, f32[32,32]{1,0:T(8,128)S(1)}, u32[]{:S(2)}, u32[]{:S(2)}) collective-permute-start(f32[32,32]{1,0:T(8,128)S(1)} %convolution_multiply_fusion.1), channel_id=1, source_target_pairs={{0,4},{4,8},{8,12},{12,16},{16,20},{20,24},{24,28},{28,32},{32,36}... | collective-permute-start | bytes 12296 | tf_op jit(solution)/shard_map/ppermute | solution.py:33
  264.0 20.4 %collective-permute-start.6 = (f32[32,32]{1,0:T(8,128)S(1)}, f32[32,32]{1,0:T(8,128)S(1)}, u32[]{:S(2)}, u32[]{:S(2)}) collective-permute-start(f32[32,32]{1,0:T(8,128)S(1)} %convolution_multiply_fusion.1), channel_id=1, source_target_pairs={{4,0},{8,4},{12,8},{16,12},{20,16},{24,20},{28,24},{32,28},{36,32}... | collective-permute-start | bytes 12296 | tf_op jit(solution)/shard_map/ppermute | solution.py:33
  273.7 10.8 %collective-permute-start.7 = (f32[32,32]{1,0:T(8,128)S(1)}, f32[32,32]{1,0:T(8,128)S(1)}, u32[]{:S(2)}, u32[]{:S(2)}) collective-permute-start(f32[32,32]{1,0:T(8,128)S(1)} %convolution_multiply_fusion.1), channel_id=1, source_target_pairs={{8,0},{12,4},{16,8},{20,12},{24,16},{28,20},{32,24},{36,28},{40,32... | collective-permute-start | bytes 12296 | tf_op jit(solution)/shard_map/ppermute | solution.py:33
  285.6 13.3 %collective-permute-start.8 = (f32[32,32]{0,1:T(8,128)S(1)}, f32[32,32]{0,1:T(8,128)S(1)}, u32[]{:S(2)}, u32[]{:S(2)}) collective-permute-start(f32[32,32]{0,1:T(8,128)S(1)} %convolution_divide_fusion.1), channel_id=1, source_target_pairs={{0,2},{1,3},{4,6},{5,7},{8,10},{9,11},{12,14},{13,15},{16,18},{17,... | collective-permute-start | bytes 12296 | tf_op jit(solution)/shard_map/ppermute | solution.py:33
  286.9 12.0 %collective-permute-start.9 = (f32[32,32]{0,1:T(8,128)S(1)}, f32[32,32]{0,1:T(8,128)S(1)}, u32[]{:S(2)}, u32[]{:S(2)}) collective-permute-start(f32[32,32]{0,1:T(8,128)S(1)} %convolution_divide_fusion.1), channel_id=1, source_target_pairs={{0,1},{1,2},{2,3},{4,5},{5,6},{6,7},{8,9},{9,10},{10,11},{12,13},{... | collective-permute-start | bytes 12296 | tf_op jit(solution)/shard_map/ppermute | solution.py:33
  288.8 10.1 %collective-permute-start.10 = (f32[32,32]{0,1:T(8,128)S(1)}, f32[32,32]{0,1:T(8,128)S(1)}, u32[]{:S(2)}, u32[]{:S(2)}) collective-permute-start(f32[32,32]{0,1:T(8,128)S(1)} %convolution_divide_fusion.1), channel_id=1, source_target_pairs={{1,0},{2,1},{3,2},{5,4},{6,5},{7,6},{9,8},{10,9},{11,10},{13,12},{... | collective-permute-start | bytes 12296 | tf_op jit(solution)/shard_map/ppermute | solution.py:33
  292.4 6.4 %collective-permute-start.11 = (f32[32,32]{0,1:T(8,128)S(1)}, f32[32,32]{0,1:T(8,128)S(1)}, u32[]{:S(2)}, u32[]{:S(2)}) collective-permute-start(f32[32,32]{0,1:T(8,128)S(1)} %convolution_divide_fusion.1), channel_id=1, source_target_pairs={{2,0},{3,1},{6,4},{7,5},{10,8},{11,9},{14,12},{15,13},{18,16},{19,... | collective-permute-start | bytes 12296 | tf_op jit(solution)/shard_map/ppermute | solution.py:33
where the time goes:
time: 305 us; the launch traced here: 302 us
  local copies, waits for them, and re-layouts  110 us (36%)
  starting transfers between devices  96.7 us (32%)
  other arithmetic  89.5 us (29%)
  matrix products  4.67 us (2%)
    sub x8, other arithmetic, advance(): center + rates * (lateral + vertical - 6.0 * center) - reaction[None]  69.3 us
    ppermute x8, starting transfers between devices, padded(): lax.ppermute(lax.slice_in_dim(block, 0, width, axis=dim), axis, backward)  52.2 us
    while x32, local copies, waits for them, and re-layouts  50.5 us
    ppermute x8, starting transfers between devices, from_behind(): return lax.ppermute(block, axis, route)  26.7 us
    ppermute x8, starting transfers between devices, padded(): lax.ppermute(lax.slice_in_dim(block, block.shape[dim] - width, None, axis...  17.7 us
    slice x4, local copies, waits for them, and re-layouts, advance(): edged = jnp.pad(center, ((0, 0), (1, 1), (0, 0), (0, 0)), mode='edge')  16.7 us
    sub x4, local copies, waits for them, and re-layouts, advance(): center + rates * (lateral + vertical - 6.0 * center) - reaction[None]  12.4 us
    mul x4, other arithmetic, single(): return (fields, guarded * jnp.exp(-DEPROTECT * acid_now))  10.3 us
  transfers between devices with their start and end apart: 24, of which 0 were waited for; matrix products, arithmetic and copies ran while one was open for 27% of the time, Pallas kernels for 0%

commit v1 on v0

v1 whole, which is shorter than its diff:
```python
import jax
import jax.numpy as jnp
import numpy as np
from jax import lax
from jax.experimental import pallas as pl
from jax.experimental.pallas import tpu as pltpu
from jax.sharding import PartitionSpec as P

RATE_ACID = 0.15
RATE_QUENCH = 0.05
NEUTRAL = 0.1
DEPROTECT = 0.35
LOADING = 0.8
STEPS = 4
COARSEN = 8
REACH = 64
SPREAD = 25.0

LAYERS = 8
ROWS = 256
COLS = 256
LANES = 128
SUBS = 8
RUN = ROWS // SUBS
HALO = STEPS
EXT = RUN + 2 * HALO
FOLD = EXT // 2
TILE = ROWS // COARSEN

VM = pl.BlockSpec(memory_space=pltpu.VMEM)
HB = pl.BlockSpec(memory_space=pltpu.HBM)
F32 = jnp.float32


def params(mib):
    return pltpu.CompilerParams(vmem_limit_bytes=mib * 1024 * 1024)


def vmem(shape):
    return pltpu.VMEM(shape, F32)


def iota(dim):
    return lax.broadcasted_iota(jnp.int32, (SUBS, LANES), dim)


def row_strips(a_top, a_bot, q_top, q_bot, first_ref, second_ref):
    even = lax.rem(lax.axis_index("gy"), 2) == 0
    low = lax.broadcasted_iota(jnp.int32, (SUBS, COLS), 0) < HALO
    for d in range(LAYERS):
        top = jnp.where(low, a_top[d], pltpu.roll(q_top[d], HALO, 0))
        bot = jnp.where(low, pltpu.roll(a_bot[d], HALO, 0), q_bot[d])
        first_ref[d] = jnp.where(even, bot, top)
        second_ref[d] = jnp.where(even, top, bot)


def pack_rows(acid, quench):
    block = (LAYERS, SUBS, COLS)
    top = pl.BlockSpec(block, lambda i: (0, 0, 0))
    bot = pl.BlockSpec(block, lambda i: (0, RUN - 1, 0))
    out = jax.ShapeDtypeStruct(block, F32)
    return pl.pallas_call(
        row_strips,
        grid=(1,),
        in_specs=[top, bot, top, bot],
        out_specs=[pl.BlockSpec(block, lambda i: (0, 0, 0))] * 2,
        out_shape=[out, out],
        compiler_params=params(4),
        name="pack_rows",
    )(acid, acid, quench, quench)


def spread_rows(acid, quench, state, land, sems):
    copies = []
    for d in range(LAYERS):
        for t in range(4):
            source = (acid, quench)[t // 2].at[d, :, pl.ds((t % 2) * LANES, LANES)]
            copy = pltpu.make_async_copy(source, land.at[d, t], sems.at[d, t])
            copy.start()
            copies.append(copy)
    for d in range(LAYERS):
        for t in range(4):
            copies[d * 4 + t].wait()
            for k in range(RUN):
                state[t, d, HALO + k] = land[d, t, pl.ds(k, SUBS, stride=RUN), :]


def load_state(acid, quench):
    return pl.pallas_call(
        spread_rows,
        in_specs=[HB, HB],
        out_specs=VM,
        out_shape=vmem((4, LAYERS, EXT, SUBS, LANES)),
        scratch_shapes=[
            pltpu.VMEM((LAYERS, 4, ROWS, LANES), F32),
            pltpu.SemaphoreType.DMA((LAYERS, 4)),
        ],
        compiler_params=params(8),
        name="load_state",
    )(acid, quench)


def column_strips(state_in, first_in, second_in, state, first_ref, second_ref):
    del state_in
    even_row = lax.rem(lax.axis_index("gy"), 2) == 0
    even_col = lax.rem(lax.axis_index("gx"), 2) == 0
    sub = iota(0)
    lane = iota(1)
    for d in range(LAYERS):
        for t in range(2):
            cols = pl.ds(t * LANES, LANES)
            one, two = first_in[d, :, cols], second_in[d, :, cols]
            top = jnp.where(even_row, two, one)
            bot = jnp.where(even_row, one, two)
            for f in range(2):
                for j in range(HALO):
                    row = f * HALO + j
                    above = pltpu.roll(state[2 * f + t, d, HALO + RUN - HALO + j], 1, 0)
                    edge = pltpu.roll(top, (SUBS - row) % SUBS, 0)
                    state[2 * f + t, d, j] = jnp.where(sub == 0, edge, above)
                    below = pltpu.roll(state[2 * f + t, d, HALO + j], SUBS - 1, 0)
                    edge = pltpu.roll(bot, SUBS - 1 - row, 0)
                    state[2 * f + t, d, HALO + RUN + j] = jnp.where(sub == SUBS - 1, edge, below)

    def gather(k, _):
        left = jnp.zeros((SUBS, LANES), F32)
        right = jnp.zeros((SUBS, LANES), F32)
        for half in range(2):
            for f in range(2):
                for d in range(LAYERS):
                    at = 64 * f + 32 * half + HALO * d
                    here = (lane >= at) & (lane < at + HALO)
                    first = state[2 * f, d, k + FOLD * half]
                    last = state[2 * f + 1, d, k + FOLD * half]
                    left = jnp.where(here, pltpu.roll(first, at, 1), left)
                    right = jnp.where(here, pltpu.roll(last, (at + HALO) % LANES, 1), right)
        first_ref[k] = jnp.where(even_col, right, left)
        second_ref[k] = jnp.where(even_col, left, right)
        return 0

    lax.fori_loop(0, FOLD, gather, 0)


def pack_columns(state, first, second):
    strip = jax.ShapeDtypeStruct((FOLD, SUBS, LANES), F32)
    return pl.pallas_call(
        column_strips,
        in_specs=[VM, VM, VM],
        out_specs=[VM, VM, VM],
        out_shape=[vmem((4, LAYERS, EXT, SUBS, LANES)), strip, strip],
        input_output_aliases={0: 0},
        compiler_params=params(4),
        name="pack_columns",
    )(state, first, second)


def shifted(x, by):
    return pltpu.roll(x, by % LANES, 1)


def sides(lane, before, x, after):
    return jnp.where(lane == 0, before, shifted(x, 1)) + jnp.where(
        lane == LANES - 1, after, shifted(x, -1)
    )


def bake(state, first_in, second_in, out, edge_out, guard, density, one, two, edge_a, edge_b, total, pooled, coef):
    gx, gy = lax.axis_index("gx"), lax.axis_index("gy")
    even_col = lax.rem(gx, 2) == 0
    lane, sub = iota(1), iota(0)
    at_left = ((lane >= 96) | ((lane >= 32) & (lane < 64)))
    is_acid = (lane < 32) | (lane >= 96)
    wall = jnp.where(at_left, (gx == 0).astype(jnp.int32), (gx == lax.axis_size("gx") - 1).astype(jnp.int32))
    lanes_open = 1.0 - wall.astype(F32)
    for c in range(3):
        closed = jnp.zeros((SUBS, LANES), jnp.int32)
        if c == 0:
            closed = jnp.where(sub == 0, (gy == 0).astype(jnp.int32), 0)
        if c == 2:
            closed = jnp.where(sub == SUBS - 1, (gy == lax.axis_size("gy") - 1).astype(jnp.int32), 0)
        is_open = 1.0 - closed.astype(F32)
        coef[c, 0] = RATE_ACID * is_open
        coef[c, 1] = NEUTRAL * is_open
        coef[c, 2] = RATE_QUENCH * is_open
        coef[c, 3] = (1.0 - 6.0 * RATE_QUENCH) * is_open
        coef[c, 4] = jnp.where(is_acid, RATE_ACID, RATE_QUENCH) * is_open * lanes_open
        coef[c, 5] = NEUTRAL * is_open * lanes_open

    def unpack(k, _):
        a, b = first_in[k], second_in[k]
        left = jnp.where(even_col, b, a)
        right = jnp.where(even_col, a, b)
        for half in range(2):
            for d in range(LAYERS):
                at = 32 * half + HALO * d
                edge_a[d, k + FOLD * half] = jnp.where(
                    at_left, shifted(left, -at - HALO), shifted(right, -at)
                )
        return 0

    lax.fori_loop(0, FOLD, unpack, 0)
    ratio = jnp.where(is_acid, 1.0, (1.0 - 6.0 * RATE_QUENCH) / NEUTRAL)

    def advance(src, src_edge, dst, dst_edge, k, kind, visit):
        c15, c10, c05, c07 = (coef[kind, i] for i in range(4))
        cs, ct = coef[kind, 4], coef[kind, 5]
        load = lambda d, j: [src[t, d, j] for t in range(4)] + [src_edge[d, j]]
        before = center = load(0, k)
        for d in range(LAYERS):
            after = load(d + 1, k) if d + 1 < LAYERS else center
            up, down = load(d, k - 1), load(d, k + 1)
            a0, a1, q0, q1, e = center
            ra0, ra1, re = shifted(a0, 1), shifted(a1, 1), shifted(e, 1)
            la0, la1, le = shifted(a0, -1), shifted(a1, -1), shifted(e, -1)
            rq0, lq1 = shifted(q0, 1), shifted(q1, -1)
            across = [
                jnp.where(lane == 0, re, ra0) + jnp.where(lane == LANES - 1, la1, la0),
                jnp.where(lane == 0, ra0, ra1) + jnp.where(lane == LANES - 1, le, la1),
                jnp.where(lane == 0, shifted(e, 65), rq0)
                + jnp.where(lane == LANES - 1, lq1, shifted(q0, -1)),
                jnp.where(lane == 0, rq0, shifted(q1, 1))
                + jnp.where(lane == LANES - 1, shifted(e, 63), lq1),
                jnp.where(lane == 0, ra1, jnp.where(lane == 64, shifted(q1, 65), re))
                + jnp.where(lane == LANES - 1, la0, jnp.where(lane == 63, shifted(q0, 63), le)),
            ]
            around = [
                (up[i] + down[i]) + (before[i] + after[i]) + across[i] for i in range(5)
            ]
            for t in range(2):
                scaled = c10 * center[t]
                acid = c15 * around[t] + scaled * (1.0 - center[2 + t])
                dst[t, d, k] = acid
                dst[2 + t, d, k] = c05 * around[2 + t] + center[2 + t] * (c07 - scaled)
                visit(t, d, k, center[t], acid)
            dst_edge[d, k] = cs * around[4] + ct * e * (ratio - shifted(e, 64))
            before, center = center, after

    def sweep(src, src_edge, dst, dst_edge, margin, visit):
        def outer(kind):
            def body(k, _):
                advance(src, src_edge, dst, dst_edge, k, kind, lambda *_: None)
                return 0

            return body

        def inner(k, _):
            advance(src, src_edge, dst, dst_edge, k, 1, visit)
            return 0

        lax.fori_loop(HALO - margin, HALO, outer(0), 0)
        lax.fori_loop(HALO, HALO + RUN, inner, 0)
        lax.fori_loop(HALO + RUN, HALO + RUN + margin, outer(2), 0)

    def begin(t, d, k, old, new):
        total[t, d, k - HALO] = old + new

    sweep(state, edge_a, one, edge_b, 3, begin)
    sweep(one, edge_b, two, edge_a, 2, lambda *_: None)

    def protect(t, d, k, old, new):
        left = jnp.exp(-DEPROTECT * (total[t, d, k - HALO] + (old + new)))
        guard[t, d, k - HALO] = left
        pooled[t, k - HALO] = left if d == 0 else pooled[t, k - HALO] + left

    sweep(two, edge_a, out, edge_out, 1, protect)

    fine = jnp.concatenate(
        [
            jnp.concatenate(
                [sum(pooled[t, COARSEN * g + i] for i in range(COARSEN)) for t in range(2)], 1
            )
            for g in range(RUN // COARSEN)
        ],
        0,
    )
    col = lax.broadcasted_iota(jnp.int32, (COLS, LANES), 0)
    block = lax.broadcasted_iota(jnp.int32, (COLS, LANES), 1)
    pool = (col // COARSEN == block).astype(F32)
    sums = jnp.dot(fine, pool, precision=lax.Precision.HIGHEST, preferred_element_type=F32)
    wide = lax.broadcasted_iota(jnp.int32, (TILE, LANES), 1)
    mean = 1.0 - sums * (1.0 / (LAYERS * COARSEN * COARSEN))
    density[...] = jnp.where(wide < TILE, mean, 0.0)


def run_bake(state, first, second):
    grid = (4, LAYERS, EXT, SUBS, LANES)
    edge = (LAYERS, EXT, SUBS, LANES)
    half = (2, LAYERS, RUN, SUBS, LANES)
    return pl.pallas_call(
        bake,
        in_specs=[VM] * 3,
        out_specs=[VM] * 4,
        out_shape=[vmem(grid), vmem(edge), vmem(half), jax.ShapeDtypeStruct((TILE, LANES), F32)],
        scratch_shapes=[
            pltpu.VMEM(grid, F32),
            pltpu.VMEM(grid, F32),
            pltpu.VMEM(edge, F32),
            pltpu.VMEM(edge, F32),
            pltpu.VMEM(half, F32),
            pltpu.VMEM((2, RUN, SUBS, LANES), F32),
            pltpu.VMEM((3, 6, SUBS, LANES), F32),
        ],
        compiler_params=params(20),
        name="bake",
    )(state, first, second)


def last_step(state, edge, guard, acid_out, guard_out, bare, land_a, land_m, sems):
    lane = iota(1)
    copies = []
    for d in range(LAYERS):
        low, high = max(d - 1, 0), min(d + 1, LAYERS - 1)

        def body(k, _, d=d, low=low, high=high):
            j = k + HALO
            e = edge[d, j]
            a0, a1 = state[0, d, j], state[1, d, j]
            ra0, la1 = shifted(a0, 1), shifted(a1, -1)
            across = [
                jnp.where(lane == 0, shifted(e, 1), ra0)
                + jnp.where(lane == LANES - 1, la1, shifted(a0, -1)),
                jnp.where(lane == 0, ra0, shifted(a1, 1))
                + jnp.where(lane == LANES - 1, shifted(e, -1), la1),
            ]
            for t, a in enumerate((a0, a1)):
                around = (
                    (state[t, d, j - 1] + state[t, d, j + 1])
                    + (state[t, low, j] + state[t, high, j])
                    + across[t]
                )
                rows = pl.ds(k, SUBS, stride=RUN)
                land_a[d, t, rows, :] = RATE_ACID * around + (NEUTRAL * a) * (
                    1.0 - state[2 + t, d, j]
                )
                left = guard[t, d, k]
                land_m[d, t, rows, :] = left
                if d == 0:
                    bare[t, rows, :] = 1.0 - left
            return 0

        lax.fori_loop(0, RUN, body, 0, unroll=4)
        for t in range(2):
            for i, (land, target) in enumerate(((land_a, acid_out), (land_m, guard_out))):
                copy = pltpu.make_async_copy(
                    land.at[d, t], target.at[d, :, pl.ds(t * LANES, LANES)], sems.at[d, t, i]
                )
                copy.start()
                copies.append(copy)
    for copy in copies:
        copy.wait()


def run_last(state, edge, guard):
    whole = jax.ShapeDtypeStruct((LAYERS, ROWS, COLS), F32)
    return pl.pallas_call(
        last_step,
        in_specs=[VM] * 3,
        out_specs=[HB, HB, VM],
        out_shape=[whole, whole, vmem((2, ROWS, LANES))],
        scratch_shapes=[
            pltpu.VMEM((LAYERS, 2, ROWS, LANES), F32),
            pltpu.VMEM((LAYERS, 2, ROWS, LANES), F32),
            pltpu.SemaphoreType.DMA((LAYERS, 2, 2)),
        ],
        compiler_params=params(8),
        name="last_step",
    )(state, edge, guard)


def weights(distance):
    offset = np.arange(-REACH, REACH + 1, dtype=np.float64)
    norm = np.exp(-offset * offset / (2.0 * SPREAD * SPREAD)).sum()
    value = np.exp(-(distance.astype(np.float64) ** 2) / (2.0 * SPREAD * SPREAD))
    return np.where(np.abs(distance) <= REACH, value / norm, 0.0).astype(np.float32)


def row_table():
    p = np.arange(TILE)
    coarse = (p % SUBS) * (TILE // SUBS) + p // SUBS
    me = np.arange(4)[:, None, None, None]
    k = np.arange(4)[None, None, :, None]
    i = np.arange(TILE)[None, :, None, None]
    distance = TILE * ((me ^ k) - me) + coarse[None, None, None, :] - i
    return weights(distance).reshape(4, TILE, 4 * TILE)


def column_table():
    c = np.arange(7 * TILE)[:, None] - 3 * TILE
    return weights(c - np.arange(COLS)[None, :] // COARSEN)


def etch(own, mate, near, far, bare, row_ref, col_ref, out, grid, cols):
    gx, gy = lax.axis_index("gx"), lax.axis_index("gy")
    odd = lax.rem(gx, 2)
    upper = lax.rem(lax.div(gx, 2), 2)
    swap = 1 - 2 * odd
    step = 2 - 4 * upper
    tiles = [own[...], mate[...], near[0], near[1], far[0], far[1]]
    offsets = [0 * gx, swap, step, step + swap, -step, -step + swap]
    lane = lax.broadcasted_iota(jnp.int32, (TILE, LANES), 1)
    for k in range(4):
        for half in range(2):
            block = jnp.zeros((TILE, LANES), F32)
            for n in range(4 * half, min(4 * half + 4, 6)):
                at = TILE * (n % 4)
                here = (lane >= at) & (lane < at + TILE)
                block = jnp.where(here, shifted(tiles[n], at - TILE * k), block)
            grid[pl.ds(TILE * k, TILE), pl.ds(LANES * half, LANES)] = block
    for n in range(6):
        start = pl.multiple_of((offsets[n] + 3) * TILE, TILE)
        cols[pl.ds(TILE * n, TILE), :] = col_ref[pl.ds(start, TILE), :]
    cols[pl.ds(6 * TILE, 2 * TILE), :] = jnp.zeros((2 * TILE, COLS), F32)
    across = jnp.dot(
        row_ref[gy], grid[...], precision=lax.Precision.HIGHEST, preferred_element_type=F32
    )
    smooth = jnp.dot(
        across, cols[...], precision=lax.Precision.HIGHEST, preferred_element_type=F32
    )
    factor = 1.0 - LOADING * smooth
    for i in range(TILE):
        rows = pl.ds(COARSEN * i, COARSEN)
        for t in range(2):
            piece = factor[i : i + 1, t * LANES : (t + 1) * LANES]
            out[rows, pl.ds(t * LANES, LANES)] = bare[t, rows, :] * piece


def run_etch(own, mate, near, far, bare):
    return pl.pallas_call(
        etch,
        in_specs=[VM] * 7,
        out_specs=VM,
        out_shape=jax.ShapeDtypeStruct((ROWS, COLS), F32),
        scratch_shapes=[pltpu.VMEM((4 * TILE, COLS), F32), pltpu.VMEM((COLS, COLS), F32)],
        compiler_params=params(4),
        name="etch",
    )(own, mate, near, far, bare, jnp.asarray(row_table()), jnp.asarray(column_table()))


def swap(block, axis, partner):
    count = lax.axis_size(axis)
    route = [(i, partner(i)) for i in range(count) if 0 <= partner(i) < count]
    return lax.ppermute(block, axis, route)


def inside(i):
    return i ^ 1


def outside(i):
    return i - 1 if i % 2 == 0 else i + 1


def shards(acid_field, quencher_field):
    acid_field = pltpu.with_memory_space_constraint(acid_field, pltpu.HBM)
    quencher_field = pltpu.with_memory_space_constraint(quencher_field, pltpu.HBM)
    first, second = pack_rows(acid_field, quencher_field)
    second = swap(second, "gy", outside)
    first = swap(first, "gy", inside)
    state = load_state(acid_field, quencher_field)
    state, first, second = pack_columns(state, first, second)
    second = swap(second, "gx", outside)
    first = swap(first, "gx", inside)
    state, edge, guard, density = run_bake(state, first, second)
    acid_after, inhibitor, bare = run_last(state, edge, guard)
    tile = density[:, :TILE]
    tile = jnp.concatenate([tile, swap(tile, "gy", lambda i: i ^ 1)], 1)
    own = jnp.concatenate([tile, swap(tile, "gy", lambda i: i ^ 2)], 1)
    mate = swap(own, "gx", inside)
    pair = jnp.stack([own, mate], 0)
    far = swap(pair, "gx", lambda i: i - 2 if i // 2 % 2 == 0 else i + 2)
    near = swap(pair, "gx", lambda i: i ^ 2)
    etch_rate = run_etch(own, mate, near, far, bare)
    return acid_after, inhibitor, etch_rate


def solution(mesh):
    in_specs = (P(None, "gy", "gx"), P(None, "gy", "gx"))
    out_specs = (P(None, "gy", "gx"), P(None, "gy", "gx"), P("gy", "gx"))
    return jax.shard_map(shards, mesh=mesh, in_specs=in_specs, out_specs=out_specs, check_vma=False)
```

time: 305 us -> 77.9 us (0.26)
  local copies, waits for them, and re-layouts: 110 us -> 0.01 us
  other arithmetic: 89.5 us -> 0.15 us
  starting transfers between devices: 96.7 us -> 23.4 us
  Pallas kernels: 0 us -> 42 us
  waiting for transfers between devices: 0.06 us -> 11.2 us
  matrix products: 4.67 us -> 0 us
    ppermute x24 -> x9, starting transfers between devices: 96.7 us -> 23.4 us  [swap(): return lax.ppermute(block, axis, route)]
    sub x9 -> x0, other arithmetic: 69.3 us -> none  [the longest x8 69.3 us: advance(): center + rates * (lateral + vertical - 6.0 * center) - reaction[None]]
    while x33 -> x0, local copies, waits for them, and re-layouts: 55.8 us -> none
    pallas_call x0 -> x6, Pallas kernels: none -> 42 us  [the longest x1 23.4 us: run_bake(): pl.pallas_call(bake, in_specs=[VM] * 3, out_specs=[VM] * 4, out_shape=[vm...]
    slice x8 -> x0, local copies, waits for them, and re-layouts: 19.7 us -> none  [the longest x4 16.7 us: advance(): edged = jnp.pad(center, ((0, 0), (1, 1), (0, 0), (0, 0)), mode='edge')]
    sub x4 -> x0, local copies, waits for them, and re-layouts: 12.4 us -> none  [advance(): center + rates * (lateral + vertical - 6.0 * center) - reaction[None]]
    ppermute x24 -> x9, waiting for transfers between devices: 0.06 us -> 11.2 us  [swap(): return lax.ppermute(block, axis, route)]
    ppermute x8 -> x0, local copies, waits for them, and re-layouts: 11 us -> none  [the longest x4 7.89 us: padded(): lax.ppermute(lax.slice_in_dim(block, 0, width, axis=dim), axis, backward)]
  transfers between devices with their start and end apart: 24 -> 9, of which waited for: 0 -> 4; matrix products, arithmetic and copies ran while one was open for 27% -> 0% of each run, Pallas kernels for 0% -> 17%
where the time goes in v1:
time: 77.9 us; the launch traced here: 77.6 us
  Pallas kernels  42 us (54%)
  starting transfers between devices  23.4 us (30%)
  waiting for transfers between devices  11.2 us (14%)
  between operations  0.8 us (1%)
    pallas_call x1, Pallas kernels, run_bake(): pl.pallas_call(bake, in_specs=[VM] * 3, out_specs=[VM] * 4, out_shape=[vm...  23.4 us
    ppermute x9, starting transfers between devices, swap(): return lax.ppermute(block, axis, route)  23.4 us
    ppermute x9, waiting for transfers between devices, swap(): return lax.ppermute(block, axis, route)  11.2 us
    pallas_call x1, Pallas kernels, run_last(): pl.pallas_call(last_step, in_specs=[VM] * 3, out_specs=[HB, HB, VM], out_...  9.66 us
    pallas_call x1, Pallas kernels, load_state(): pl.pallas_call(spread_rows, in_specs=[HB, HB], out_specs=VM, out_shape=vm...  3.8 us
    pallas_call x1, Pallas kernels, pack_columns(): pl.pallas_call(column_strips, in_specs=[VM, VM, VM], out_specs=[VM, VM, V...  2.85 us
  transfers between devices with their start and end apart: 9, of which 4 were waited for; matrix products, arithmetic and copies ran while one was open for 0% of the time, Pallas kernels for 17%

profile of v1, /device:TPU:24, one launch (start us, length us, event | category | flops | bytes accessed | tf_op | source)
XLA Modules:
  0.0 77.6 jit_solution(17431961684452991309)
XLA Ops:
  0.6 1.0 %pack_rows.1 = (f32[8,8,256]{2,1,0:T(8,128)S(1)}, f32[8,8,256]{2,1,0:T(8,128)S(1)}) custom-call(f32[8,256,256]{2,1,0:T(8,128)} %a_bot.1, f32[8,256,256]{2,1,0:T(8,128)} %a_bot.1, f32[8,256,256]{2,1,0:T(8,128)} %q_bot.1, f32[8,256,256]{2,1,0:T(8,128)} %q_bot.1), custom_call_target="tpu_custom_call" | custom-call | tf_op jit(solution)/shard_map/pack_rows/pallas_call | solution.py:62
  1.6 0.1 collective-permute-start
  1.7 2.7 %collective-permute-start.1 = (f32[8,8,256]{2,1,0:T(8,128)S(1)}, f32[8,8,256]{2,1,0:T(8,128)S(1)}, u32[]{:S(2)}, u32[]{:S(2)}) collective-permute-start(f32[8,8,256]{2,1,0:T(8,128)S(1)} %get-tuple-element.16), channel_id=1, source_target_pairs={{1,2},{2,1},{5,6},{6,5},{9,10},{10,9},{13,14},{14,13},{17,18},{18,... | collective-permute-start | bytes 196616 | tf_op jit(solution)/shard_map/ppermute | solution.py:442
  4.4 3.8 %load_state.1.state_in = f32[4,8,40,8,128]{4,3,2,1,0:T(8,128)S(1)} custom-call(f32[8,256,256]{2,1,0:T(8,128)} %a_bot.1, f32[8,256,256]{2,1,0:T(8,128)} %q_bot.1), custom_call_target="tpu_custom_call" | custom-call | tf_op jit(solution)/shard_map/load_state/pallas_call | solution.py:89
  8.3 0.0 collective-permute-done.first_in
  8.3 0.0 collective-permute-done.1.second_in
  8.3 2.8 %pack_columns.1 = (f32[4,8,40,8,128]{4,3,2,1,0:T(8,128)S(1)}, f32[20,8,128]{2,1,0:T(8,128)S(1)}, f32[20,8,128]{2,1,0:T(8,128)S(1)}) custom-call(f32[4,8,40,8,128]{4,3,2,1,0:T(8,128)S(1)} %load_state.1.state_in, f32[8,8,256]{2,1,0:T(8,128)S(1)} %collective-permute-done.first_in, ...), custom_call_target="tpu_custom_call", output_to_operand_aliasing={{0}: (0, {})} | custom-call | tf_op jit(solution)/shard_map/pack_columns/pallas_call | solution.py:146
  11.1 2.0 %collective-permute-start.2 = (f32[20,8,128]{2,1,0:T(8,128)S(1)}, f32[20,8,128]{2,1,0:T(8,128)S(1)}, u32[]{:S(2)}, u32[]{:S(2)}) collective-permute-start(f32[20,8,128]{2,1,0:T(8,128)S(1)} %get-tuple-element.18), channel_id=1, source_target_pairs={{0,4},{4,0},{8,12},{12,8},{16,20},{20,16},{24,28},{28,24},{32,36},... | collective-permute-start | bytes 245768 | tf_op jit(solution)/shard_map/ppermute | solution.py:442
  13.1 9.4 %collective-permute-start.3 = (f32[20,8,128]{2,1,0:T(8,128)S(1)}, f32[20,8,128]{2,1,0:T(8,128)S(1)}, u32[]{:S(2)}, u32[]{:S(2)}) collective-permute-start(f32[20,8,128]{2,1,0:T(8,128)S(1)} %get-tuple-element.19), channel_id=1, source_target_pairs={{4,8},{8,4},{12,16},{16,12},{20,24},{24,20},{28,32},{32,28},{36,40... | collective-permute-start | bytes 245768 | tf_op jit(solution)/shard_map/ppermute | solution.py:442
  22.6 0.0 collective-permute-done.2.first_in
  22.6 2.6 %collective-permute-done.3.second_in = f32[20,8,128]{2,1,0:T(8,128)S(1)} collective-permute-done((f32[20,8,128]{2,1,0:T(8,128)S(1)}, f32[20,8,128]{2,1,0:T(8,128)S(1)}, u32[]{:S(2)}, u32[]{:S(2)}) %collective-permute-start.3) | collective-permute-done | bytes 81952 | tf_op jit(solution)/shard_map/ppermute | solution.py:442
  25.2 23.4 %bake.1 = (f32[4,8,40,8,128]{4,3,2,1,0:T(8,128)S(1)}, f32[8,40,8,128]{3,2,1,0:T(8,128)S(1)}, f32[2,8,32,8,128]{4,3,2,1,0:T(8,128)S(1)}, f32[32,128]{1,0:T(8,128)S(1)}) custom-call(f32[4,8,40,8,128]{4,3,2,1,0:T(8,128)S(1)} %get-tuple-element.17.state, f32[20,8,128]{2,1,0:T(8,128)S(1)} %collective-permute-done.2.first_in, ...), custom_call_target="tpu_custom_call" | custom-call | tf_op jit(solution)/shard_map/bake/pallas_call | solution.py:289
  48.6 0.1 collective-permute-start.4
  48.7 1.2 %collective-permute-done.4 = f32[32,32]{1,0:T(8,128)S(1)} collective-permute-done((f32[32,32]{1,0:T(8,128)S(1)}, f32[32,32]{1,0:T(8,128)S(1)}, u32[]{:S(2)}, u32[]{:S(2)}) %collective-permute-start.4) | collective-permute-done | bytes 4128 | tf_op jit(solution)/shard_map/ppermute | solution.py:442
  49.9 0.1 pad_maximum_fusion.1
  50.0 0.0 collective-permute-start.5
  50.0 3.7 %collective-permute-done.5 = f32[32,64]{1,0:T(8,128)S(1)} collective-permute-done((f32[32,64]{1,0:T(8,128)S(1)}, f32[32,64]{1,0:T(8,128)S(1)}, u32[]{:S(2)}, u32[]{:S(2)}) %collective-permute-start.5) | collective-permute-done | bytes 8224 | tf_op jit(solution)/shard_map/ppermute | solution.py:442
  53.8 0.1 pad_maximum_fusion.2.own
  53.8 0.0 collective-permute-start.6
  53.9 3.7 %collective-permute-done.6.mate = f32[32,128]{1,0:T(8,128)S(1)} collective-permute-done((f32[32,128]{1,0:T(8,128)S(1)}, f32[32,128]{1,0:T(8,128)S(1)}, u32[]{:S(2)}, u32[]{:S(2)}) %collective-permute-start.6) | collective-permute-done | bytes 16416 | tf_op jit(solution)/shard_map/ppermute | solution.py:442
  57.6 8.9 %collective-permute-start.8 = (f32[2,32,128]{2,1,0:T(8,128)S(1)}, f32[2,32,128]{2,1,0:T(8,128)S(1)}, u32[]{:S(2)}, u32[]{:S(2)}) collective-permute-start(f32[2,32,128]{2,1,0:T(8,128)S(1)} %pad_maximum_fusion), channel_id=1, source_target_pairs={{8,16},{12,20},{16,8},{20,12},{24,32},{28,36},{32,24},{36,28},{40,... | collective-permute-start | bytes 98312 | tf_op jit(solution)/shard_map/ppermute | solution.py:442
  66.5 0.1 collective-permute-start.7
  66.6 0.0 copy-start
  66.6 0.0 copy-start.1
  66.6 9.7 %last_step.1 = (f32[8,256,256]{2,1,0:T(8,128)}, f32[8,256,256]{2,1,0:T(8,128)}, f32[2,256,128]{2,1,0:T(8,128)S(1)}) custom-call(f32[4,8,40,8,128]{4,3,2,1,0:T(8,128)S(1)} %get-tuple-element.20.state, f32[8,40,8,128]{3,2,1,0:T(8,128)S(1)} %get-tuple-element.21.edge, f32[2,8,32,8,128]{4,3,2,1,0:T(8,128)S(1)} %get-tuple-element.22.guard), custom_call_target="tpu_custom_call" | custom-call | tf_op jit(solution)/shard_map/last_step/pallas_call | solution.py:355
  76.3 0.0 collective-permute-done.8.far
  76.3 0.0 collective-permute-done.7.near
  76.3 0.0 copy-done
  76.3 0.0 copy-done.1
  76.3 1.3 %etch.1 = f32[256,256]{1,0:T(8,128)} custom-call(f32[32,128]{1,0:T(8,128)S(1)} %pad_maximum_fusion.2.own, f32[32,128]{1,0:T(8,128)S(1)} %collective-permute-done.6.mate, f32[2,32,128]{2,1,0:T(8,128)S(1)} %collective-permute-done.7.near, f32[2,32,128]{2,1,0:T(8,128)S(1)} %collective-permute-done.8.far, f32[2,256,128]{2,1,0:T(8,128)S(1)} %get-tuple-element.26.bare, ...), custom_call_target="tpu_custom_call" | custom-call | tf_op jit(solution)/shard_map/etch/pallas_call | solution.py:428
  (1 shorter events, 0.0 us)
Async XLA Ops:
  1.6 6.7 %collective-permute-start = (f32[8,8,256]{2,1,0:T(8,128)S(1)}, f32[8,8,256]{2,1,0:T(8,128)S(1)}, u32[]{:S(2)}, u32[]{:S(2)}) collective-permute-start(f32[8,8,256]{2,1,0:T(8,128)S(1)} %get-tuple-element.15), channel_id=1, source_target_pairs={{0,1},{1,0},{2,3},{3,2},{4,5},{5,4},{6,7},{7,6},{8,9},{9,8},{10,11... | collective-permute-start | bytes 196616 | tf_op jit(solution)/shard_map/ppermute | solution.py:442
  1.7 6.6 %collective-permute-start.1 = (f32[8,8,256]{2,1,0:T(8,128)S(1)}, f32[8,8,256]{2,1,0:T(8,128)S(1)}, u32[]{:S(2)}, u32[]{:S(2)}) collective-permute-start(f32[8,8,256]{2,1,0:T(8,128)S(1)} %get-tuple-element.16), channel_id=1, source_target_pairs={{1,2},{2,1},{5,6},{6,5},{9,10},{10,9},{13,14},{14,13},{17,18},{18,... | collective-permute-start | bytes 196616 | tf_op jit(solution)/shard_map/ppermute | solution.py:442
  11.1 11.4 %collective-permute-start.2 = (f32[20,8,128]{2,1,0:T(8,128)S(1)}, f32[20,8,128]{2,1,0:T(8,128)S(1)}, u32[]{:S(2)}, u32[]{:S(2)}) collective-permute-start(f32[20,8,128]{2,1,0:T(8,128)S(1)} %get-tuple-element.18), channel_id=1, source_target_pairs={{0,4},{4,0},{8,12},{12,8},{16,20},{20,16},{24,28},{28,24},{32,36},... | collective-permute-start | bytes 245768 | tf_op jit(solution)/shard_map/ppermute | solution.py:442
  13.1 12.0 %collective-permute-start.3 = (f32[20,8,128]{2,1,0:T(8,128)S(1)}, f32[20,8,128]{2,1,0:T(8,128)S(1)}, u32[]{:S(2)}, u32[]{:S(2)}) collective-permute-start(f32[20,8,128]{2,1,0:T(8,128)S(1)} %get-tuple-element.19), channel_id=1, source_target_pairs={{4,8},{8,4},{12,16},{16,12},{20,24},{24,20},{28,32},{32,28},{36,40... | collective-permute-start | bytes 245768 | tf_op jit(solution)/shard_map/ppermute | solution.py:442
  48.6 1.3 %collective-permute-start.4 = (f32[32,32]{1,0:T(8,128)S(1)}, f32[32,32]{1,0:T(8,128)S(1)}, u32[]{:S(2)}, u32[]{:S(2)}) collective-permute-start(f32[32,32]{1,0:T(8,128)S(1)} %bitcast.5), channel_id=1, source_target_pairs={{0,1},{1,0},{2,3},{3,2},{4,5},{5,4},{6,7},{7,6},{8,9},{9,8},{10,11... | collective-permute-start | bytes 12296 | tf_op jit(solution)/shard_map/ppermute | solution.py:442
  50.0 3.8 %collective-permute-start.5 = (f32[32,64]{1,0:T(8,128)S(1)}, f32[32,64]{1,0:T(8,128)S(1)}, u32[]{:S(2)}, u32[]{:S(2)}) collective-permute-start(f32[32,64]{1,0:T(8,128)S(1)} %pad_maximum_fusion.1), channel_id=1, source_target_pairs={{0,2},{1,3},{2,0},{3,1},{4,6},{5,7},{6,4},{7,5},{8,10},{9,11},{10,... | collective-permute-start | bytes 24584 | tf_op jit(solution)/shard_map/ppermute | solution.py:442
  53.8 3.8 %collective-permute-start.6 = (f32[32,128]{1,0:T(8,128)S(1)}, f32[32,128]{1,0:T(8,128)S(1)}, u32[]{:S(2)}, u32[]{:S(2)}) collective-permute-start(f32[32,128]{1,0:T(8,128)S(1)} %pad_maximum_fusion.2.own), channel_id=1, source_target_pairs={{0,4},{4,0},{8,12},{12,8},{16,20},{20,16},{24,28},{28,24},{32,36},... | collective-permute-start | bytes 49160 | tf_op jit(solution)/shard_map/ppermute | solution.py:442
  57.6 18.7 %collective-permute-start.8 = (f32[2,32,128]{2,1,0:T(8,128)S(1)}, f32[2,32,128]{2,1,0:T(8,128)S(1)}, u32[]{:S(2)}, u32[]{:S(2)}) collective-permute-start(f32[2,32,128]{2,1,0:T(8,128)S(1)} %pad_maximum_fusion), channel_id=1, source_target_pairs={{8,16},{12,20},{16,8},{20,12},{24,32},{28,36},{32,24},{36,28},{40,... | collective-permute-start | bytes 98312 | tf_op jit(solution)/shard_map/ppermute | solution.py:442
  66.5 9.8 %collective-permute-start.7 = (f32[2,32,128]{2,1,0:T(8,128)S(1)}, f32[2,32,128]{2,1,0:T(8,128)S(1)}, u32[]{:S(2)}, u32[]{:S(2)}) collective-permute-start(f32[2,32,128]{2,1,0:T(8,128)S(1)} %pad_maximum_fusion), channel_id=1, source_target_pairs={{0,8},{4,12},{8,0},{12,4},{16,24},{20,28},{24,16},{28,20},{32,40},... | collective-permute-start | bytes 98312 | tf_op jit(solution)/shard_map/ppermute | solution.py:442
  66.6 9.7 %copy-start = (f32[224,256]{1,0:T(8,128)S(1)}, f32[224,256]{1,0:T(8,128)}, u32[]{:S(2)}) copy-start(f32[224,256]{1,0:T(8,128)} %constant.5.clone.col_ref) | copy-start | bytes 688132
  66.6 9.7 %copy-start.1 = (f32[4,32,128]{2,1,0:T(8,128)S(1)}, f32[4,32,128]{2,1,0:T(8,128)}, u32[]{:S(2)}) copy-start(f32[4,32,128]{2,1,0:T(8,128)} %constant.4.clone.row_ref) | copy-start | bytes 196612

commit v2 on v1

v2 whole, which is shorter than its diff:
```python
import jax
import jax.numpy as jnp
import numpy as np
from jax import lax
from jax.experimental import pallas as pl
from jax.experimental.pallas import tpu as pltpu
from jax.sharding import PartitionSpec as P

RATE_ACID = 0.15
RATE_QUENCH = 0.05
NEUTRAL = 0.1
DEPROTECT = 0.35
LOADING = 0.8
STEPS = 4
COARSEN = 8
REACH = 64
SPREAD = 25.0

LAYERS = 8
ROWS = 256
COLS = 256
LANES = 128
SUBS = 8
RUN = ROWS // SUBS
HALO = STEPS
BASE = 2 * SUBS
EXT = ROWS + 2 * BASE
LIVE = ROWS + BASE
FOLD = LIVE // SUBS // 2
PARTS = 4
TILE = ROWS // COARSEN
GROUP = 16

VM = pl.BlockSpec(memory_space=pltpu.VMEM)
HB = pl.BlockSpec(memory_space=pltpu.HBM)
F32 = jnp.float32


def params(mib):
    return pltpu.CompilerParams(vmem_limit_bytes=mib * 1024 * 1024)


def vmem(shape):
    return pltpu.VMEM(shape, F32)


def iota(dim):
    return lax.broadcasted_iota(jnp.int32, (SUBS, LANES), dim)


def row_strips(a_top, a_bot, q_top, q_bot, first_ref, second_ref):
    even = lax.rem(lax.axis_index("gy"), 2) == 0
    low = lax.broadcasted_iota(jnp.int32, (SUBS, COLS), 0) < HALO
    for d in range(LAYERS):
        top = jnp.where(low, a_top[d], pltpu.roll(q_top[d], HALO, 0))
        bot = jnp.where(low, pltpu.roll(a_bot[d], HALO, 0), q_bot[d])
        first_ref[d] = jnp.where(even, bot, top)
        second_ref[d] = jnp.where(even, top, bot)


def pack_rows(acid, quench):
    block = (LAYERS, SUBS, COLS)
    top = pl.BlockSpec(block, lambda i: (0, 0, 0))
    bot = pl.BlockSpec(block, lambda i: (0, RUN - 1, 0))
    out = jax.ShapeDtypeStruct(block, F32)
    return pl.pallas_call(
        row_strips,
        grid=(1,),
        in_specs=[top, bot, top, bot],
        out_specs=[pl.BlockSpec(block, lambda i: (0, 0, 0))] * 2,
        out_shape=[out, out],
        compiler_params=params(4),
        name="pack_rows",
    )(acid, acid, quench, quench)


def shifted(x, by):
    return pltpu.roll(x, by % LANES, 1)


def rows_at(i):
    return pl.ds(pl.multiple_of(i * SUBS, SUBS), SUBS)


def own_strips(state, strips, i):
    lane = iota(1)
    rows = rows_at(i)
    for f in range(2):
        left = jnp.zeros((SUBS, LANES), F32)
        right = jnp.zeros((SUBS, LANES), F32)
        for d in range(LAYERS):
            both = jnp.where(lane < LANES // 2, state[2 * f, d, rows, :], state[2 * f + 1, d, rows, :])
            moved = shifted(both, GROUP * d + HALO)
            at = lane - (GROUP * d + HALO)
            left = jnp.where((at >= 0) & (at < 8), moved, left)
            at = (lane + HALO) % LANES - GROUP * d
            right = jnp.where((at >= 0) & (at < 8), moved, right)
        strips[2 * f, rows, :] = left
        strips[2 * f + 1, rows, :] = right


def fill_state(acid, quench, state, strips, sems):
    size = ROWS // PARTS
    copies = []
    for p in range(PARTS):
        for t in range(4):
            source = (acid, quench)[t // 2].at[
                :, pl.ds(size * p, size), pl.ds((t % 2) * LANES, LANES)
            ]
            target = state.at[t, :, pl.ds(BASE + size * p, size), :]
            copy = pltpu.make_async_copy(source, target, sems.at[p, t])
            copy.start()
            copies.append(copy)
    for p in range(PARTS):
        for t in range(4):
            copies[4 * p + t].wait()

        def body(i, _):
            own_strips(state, strips, i)
            return 0

        first = (BASE + size * p) // SUBS
        lax.fori_loop(first, first + size // SUBS, body, 0)


def load_state(acid, quench):
    return pl.pallas_call(
        fill_state,
        in_specs=[HB, HB],
        out_specs=[VM, VM],
        out_shape=[vmem((4, LAYERS, EXT, LANES)), vmem((4, EXT, LANES))],
        scratch_shapes=[pltpu.SemaphoreType.DMA((PARTS, 4))],
        compiler_params=params(4),
        name="load_state",
    )(acid, quench)


def column_strips(state_in, strips_in, first_in, second_in, state, strips, first_ref, second_ref):
    del state_in, strips_in
    even_row = lax.rem(lax.axis_index("gy"), 2) == 0
    even_col = lax.rem(lax.axis_index("gx"), 2) == 0
    sub = iota(0)
    place = iota(1) % GROUP
    for d in range(LAYERS):
        for t in range(2):
            cols = pl.ds(t * LANES, LANES)
            one, two = first_in[d, :, cols], second_in[d, :, cols]
            top = jnp.where(even_row, two, one)
            bot = jnp.where(even_row, one, two)
            above, below = pl.ds(SUBS, SUBS), pl.ds(BASE + ROWS, SUBS)
            state[t, d, above, :] = jnp.where(sub >= HALO, pltpu.roll(top, HALO, 0), 0.0)
            state[2 + t, d, above, :] = jnp.where(sub >= HALO, top, 0.0)
            state[t, d, below, :] = jnp.where(sub < HALO, bot, 0.0)
            state[2 + t, d, below, :] = jnp.where(sub < HALO, pltpu.roll(bot, HALO, 0), 0.0)
    own_strips(state, strips, 1)
    own_strips(state, strips, (BASE + ROWS) // SUBS)
    for j in range(FOLD):
        left = jnp.zeros((SUBS, LANES), F32)
        right = jnp.zeros((SUBS, LANES), F32)
        for m in range(4):
            rows = pl.ds(SUBS * (1 + j + FOLD * (m // 2)), SUBS)
            at = (place - HALO - 4 * m) % GROUP
            left = jnp.where(at < HALO, shifted(strips[2 * (m % 2), rows, :], 4 * m), left)
            at = (place - 4 * m) % GROUP
            right = jnp.where(at < HALO, shifted(strips[2 * (m % 2) + 1, rows, :], 4 * m), right)
        first_ref[j] = jnp.where(even_col, right, left)
        second_ref[j] = jnp.where(even_col, left, right)


def pack_columns(state, strips, first, second):
    strip = jax.ShapeDtypeStruct((FOLD, SUBS, LANES), F32)
    return pl.pallas_call(
        column_strips,
        in_specs=[VM] * 4,
        out_specs=[VM] * 4,
        out_shape=[vmem((4, LAYERS, EXT, LANES)), vmem((4, EXT, LANES)), strip, strip],
        input_output_aliases={0: 0, 1: 1},
        compiler_params=params(4),
        name="pack_columns",
    )(state, strips, first, second)


def halves(x):
    high = x.astype(jnp.bfloat16)
    return high, (x - high.astype(F32)).astype(jnp.bfloat16)


def neighbour_sums(parts, matrix):
    split = [halves(x) for x in parts]
    stacked = jnp.concatenate([h for h, _ in split] + [l for _, l in split], 1)
    return jnp.dot(stacked, matrix, preferred_element_type=F32)


def beside_matrix():
    shape = (2 * COLS, COLS)
    row = lax.broadcasted_iota(jnp.int32, shape, 0) % COLS
    col = lax.broadcasted_iota(jnp.int32, shape, 1)
    return (jnp.abs(row - col) == 1).astype(jnp.bfloat16)


def strip_matrix(offset):
    shape = (2 * LANES, LANES)
    row = lax.broadcasted_iota(jnp.int32, shape, 0) % LANES
    col = lax.broadcasted_iota(jnp.int32, shape, 1)
    layer = ((col + offset) % LANES) // GROUP
    gap = (row - col + LANES) % LANES
    beside = ((gap == 1) | (gap == LANES - 1)).astype(F32)
    lower = (gap == jnp.where(layer == 0, 0, LANES - GROUP)).astype(F32)
    upper = (gap == jnp.where(layer == LAYERS - 1, 0, GROUP)).astype(F32)
    return (beside + lower + upper).astype(jnp.bfloat16)


def row_open(kind):
    gy = lax.axis_index("gy")
    if kind == 1:
        return 1.0
    outside = gy == 0 if kind == 0 else gy == lax.axis_size("gy") - 1
    return 1.0 - outside.astype(jnp.int32).astype(F32)


def sweep(body):
    for kind, low, high in ((0, 1, 2), (1, 2, 2 + RUN), (2, 2 + RUN, 3 + RUN)):

        def step(i, _, kind=kind):
            body(i, kind)
            return 0

        lax.fori_loop(low, high, step, 0)


def main_sums(src, sums, matrix, fields, start, count):
    for f in fields:
        parts = [src[2 * f + t, :, pl.ds(start, count), :].reshape(LAYERS * count, LANES) for t in range(2)]
        total = neighbour_sums(parts, matrix)
        for t in range(2):
            piece = total[:, t * LANES : (t + 1) * LANES].reshape(LAYERS, count, LANES)
            sums[2 * f + t, :, pl.ds(start, count), :] = piece


def main_steps(state, out, guard, one, two, sums, total, matrix):
    matrix[...] = beside_matrix()

    def advance(src, dst, visit):
        main_sums(src, sums, matrix[...], (0, 1), SUBS, LIVE)

        def body(i, kind):
            rows = rows_at(i)
            shut = row_open(kind)
            load = lambda d: [src[t, d, rows, :] for t in range(4)]
            before = center = load(0)
            for d in range(LAYERS):
                after = load(d + 1) if d + 1 < LAYERS else center
                around = []
                for t in range(4):
                    up = src[t, d, pl.ds(i * SUBS - 1, SUBS), :]
                    down = src[t, d, pl.ds(i * SUBS + 1, SUBS), :]
                    around.append((up + down) + (before[t] + after[t]) + sums[t, d, rows, :])
                for t in range(2):
                    scaled = NEUTRAL * center[t]
                    acid = RATE_ACID * around[t] + scaled * (1.0 - center[2 + t])
                    quench = RATE_QUENCH * around[2 + t] + center[2 + t] * (
                        (1.0 - 6.0 * RATE_QUENCH) - scaled
                    )
                    if kind != 1:
                        acid, quench = acid * shut, quench * shut
                    dst[t, d, rows, :] = acid
                    dst[2 + t, d, rows, :] = quench
                    if kind == 1:
                        visit(t, d, i, center[t], acid)
                before, center = center, after

        sweep(body)

    def begin(t, d, i, old, new):
        total[t, d, rows_at(i - 2), :] = old + new

    def protect(t, d, i, old, new):
        rows = rows_at(i - 2)
        guard[d, rows, pl.ds(t * LANES, LANES)] = jnp.exp(
            -DEPROTECT * (total[t, d, rows, :] + (old + new))
        )

    advance(state, one, begin)
    advance(one, two, lambda *_: None)
    advance(two, out, protect)


def run_main(state):
    grid = (4, LAYERS, EXT, LANES)
    return pl.pallas_call(
        main_steps,
        in_specs=[VM],
        out_specs=[VM, VM],
        out_shape=[vmem(grid), vmem((LAYERS, ROWS, COLS))],
        scratch_shapes=[
            pltpu.VMEM(grid, F32),
            pltpu.VMEM(grid, F32),
            pltpu.VMEM(grid, F32),
            pltpu.VMEM((2, LAYERS, ROWS, LANES), F32),
            pltpu.VMEM((2 * COLS, COLS), jnp.bfloat16),
        ],
        compiler_params=params(28),
        cost_estimate=pl.CostEstimate(flops=10**9, bytes_accessed=3 * 10**7, transcendentals=0),
        name="main_steps",
    )(state)


def strip_sums(src, sums, matrices, fields):
    rows = pl.ds(SUBS, LIVE)
    for side in range(2):
        stacked = jnp.concatenate([src[2 * f + side, rows, :] for f in fields], 0)
        total = neighbour_sums([stacked], matrices[side])
        for n, f in enumerate(fields):
            sums[2 * f + side, rows, :] = total[n * LIVE : (n + 1) * LIVE]


def strip_open():
    gx = lax.axis_index("gx")
    place = iota(1) % GROUP
    left = jnp.where((place < HALO) & (gx == 0), 0.0, 1.0)
    right = jnp.where((place >= HALO) & (place < 2 * HALO) & (gx == lax.axis_size("gx") - 1), 0.0, 1.0)
    return left, right


def put_edges(target, i, left, right, visit):
    lane = iota(1)
    rows = rows_at(i - 2)
    place = lane % GROUP
    both = jnp.where((place >= HALO) & (place < 2 * HALO), left, right)
    for d in range(LAYERS):
        moved = shifted(both, -GROUP * d - HALO)
        for t in range(2):
            here = lane < HALO if t == 0 else lane >= LANES - HALO
            cols = pl.ds(t * LANES, LANES)
            value = jnp.where(here, moved, target[d, rows, cols])
            target[d, rows, cols] = value
            visit(d, t, value)


def strip_steps(strips, first_in, second_in, guard_in, out, guard, density, one, two, sums, total, pooled):
    del guard_in
    even_col = lax.rem(lax.axis_index("gx"), 2) == 0
    place = iota(1) % GROUP
    opens = strip_open()
    matrices = strip_matrix(0), strip_matrix(HALO)
    for j in range(FOLD):
        a, b = first_in[j], second_in[j]
        left = jnp.where(even_col, b, a)
        right = jnp.where(even_col, a, b)
        for m in range(4):
            rows = pl.ds(SUBS * (1 + j + FOLD * (m // 2)), SUBS)
            f = m % 2
            one[2 * f, rows, :] = jnp.where(
                place < HALO, shifted(left, -4 * m), strips[2 * f, rows, :]
            )
            one[2 * f + 1, rows, :] = jnp.where(
                (place >= HALO) & (place < 2 * HALO),
                shifted(right, -4 * m),
                strips[2 * f + 1, rows, :],
            )

    def advance(src, dst, visit):
        strip_sums(src, sums, matrices, (0, 1))

        def body(i, kind):
            rows = rows_at(i)
            for side in range(2):
                shut = opens[side] * row_open(kind)
                center = [src[2 * f + side, rows, :] for f in range(2)]
                around = []
                for f in range(2):
                    up = src[2 * f + side, pl.ds(i * SUBS - 1, SUBS), :]
                    down = src[2 * f + side, pl.ds(i * SUBS + 1, SUBS), :]
                    around.append((up + down) + sums[2 * f + side, rows, :])
                scaled = NEUTRAL * center[0]
                acid = RATE_ACID * around[0] + scaled * (1.0 - center[1])
                quench = RATE_QUENCH * around[1] + center[1] * ((1.0 - 6.0 * RATE_QUENCH) - scaled)
                acid = acid * shut
                dst[side, rows, :] = acid
                dst[2 + side, rows, :] = quench * shut
                visit(side, rows, center[0], acid)

        sweep(body)

    def begin(side, rows, old, new):
        total[side, rows, :] = old + new

    def protect(side, rows, old, new):
        total[side, rows, :] = jnp.exp(-DEPROTECT * (total[side, rows, :] + (old + new)))

    advance(one, two, begin)
    advance(two, one, lambda *_: None)
    advance(one, out, protect)

    def merge(i, _):
        kept = [None, None]

        def add(d, t, value):
            kept[t] = value if d == 0 else kept[t] + value

        put_edges(guard, i, total[0, rows_at(i), :], total[1, rows_at(i), :], add)
        for t in range(2):
            pooled[rows_at(i - 2), pl.ds(t * LANES, LANES)] = kept[t]
        return 0

    lax.fori_loop(2, 2 + RUN, merge, 0)
    fine = pooled[...].reshape(TILE, COARSEN, COLS).sum(1)
    col = lax.broadcasted_iota(jnp.int32, (COLS, LANES), 0)
    block = lax.broadcasted_iota(jnp.int32, (COLS, LANES), 1)
    pool = (col // COARSEN == block).astype(F32)
    coarse = jnp.dot(fine, pool, precision=lax.Precision.HIGHEST, preferred_element_type=F32)
    wide = lax.broadcasted_iota(jnp.int32, (TILE, LANES), 1)
    mean = 1.0 - coarse * (1.0 / (LAYERS * COARSEN * COARSEN))
    density[...] = jnp.where(wide < TILE, mean, 0.0)


def run_strips(strips, first, second, guard):
    edge = (4, EXT, LANES)
    whole = (LAYERS, ROWS, COLS)
    return pl.pallas_call(
        strip_steps,
        in_specs=[VM] * 4,
        out_specs=[VM] * 3,
        out_shape=[vmem(edge), vmem(whole), jax.ShapeDtypeStruct((TILE, LANES), F32)],
        input_output_aliases={3: 1},
        scratch_shapes=[
            pltpu.VMEM(edge, F32),
            pltpu.VMEM(edge, F32),
            pltpu.VMEM(edge, F32),
            pltpu.VMEM((2, EXT, LANES), F32),
            pltpu.VMEM((ROWS, COLS), F32),
        ],
        compiler_params=params(8),
        name="strip_steps",
    )(strips, first, second, guard)


def last_step(state, strips, acid_out, sums, edge_sums, matrix, land, sems):
    matrix[...] = beside_matrix()
    main_sums(state, sums, matrix[...], (0,), BASE, ROWS)
    strip_sums(strips, edge_sums, (strip_matrix(0), strip_matrix(HALO)), (0,))

    def body(i, _):
        rows = rows_at(i)
        up_rows, down_rows = pl.ds(i * SUBS - 1, SUBS), pl.ds(i * SUBS + 1, SUBS)
        for t in range(2):
            before = center = state[t, 0, rows, :]
            for d in range(LAYERS):
                after = state[t, d + 1, rows, :] if d + 1 < LAYERS else center
                around = (state[t, d, up_rows, :] + state[t, d, down_rows, :]) + (
                    before + after
                ) + sums[t, d, rows, :]
                land[d, rows_at(i - 2), pl.ds(t * LANES, LANES)] = RATE_ACID * around + (
                    NEUTRAL * center
                ) * (1.0 - state[2 + t, d, rows, :])
                before, center = center, after
        edges = []
        for side in range(2):
            center = strips[side, rows, :]
            around = (strips[side, up_rows, :] + strips[side, down_rows, :]) + edge_sums[side, rows, :]
            edges.append(RATE_ACID * around + (NEUTRAL * center) * (1.0 - strips[2 + side, rows, :]))
        put_edges(land, i, *edges, lambda *_: None)
        return 0

    size = ROWS // PARTS
    copies = []
    for p in range(PARTS):
        first = (BASE + size * p) // SUBS
        lax.fori_loop(first, first + size // SUBS, body, 0)
        part = pl.ds(size * p, size)
        copies.append(pltpu.make_async_copy(land.at[:, part, :], acid_out.at[:, part, :], sems.at[p]))
        copies[p].start()
    for copy in copies:
        copy.wait()


def run_last(state, strips):
    whole = (LAYERS, ROWS, COLS)
    return pl.pallas_call(
        last_step,
        in_specs=[VM] * 2,
        out_specs=HB,
        out_shape=jax.ShapeDtypeStruct(whole, F32),
        scratch_shapes=[
            pltpu.VMEM((2, LAYERS, EXT, LANES), F32),
            pltpu.VMEM((2, EXT, LANES), F32),
            pltpu.VMEM((2 * COLS, COLS), jnp.bfloat16),
            pltpu.VMEM(whole, F32),
            pltpu.SemaphoreType.DMA((PARTS,)),
        ],
        compiler_params=params(12),
        name="last_step",
    )(state, strips)


def weights(distance):
    offset = np.arange(-REACH, REACH + 1, dtype=np.float64)
    norm = np.exp(-offset * offset / (2.0 * SPREAD * SPREAD)).sum()
    value = np.exp(-(distance.astype(np.float64) ** 2) / (2.0 * SPREAD * SPREAD))
    return np.where(np.abs(distance) <= REACH, value / norm, 0.0).astype(np.float32)


def row_table():
    p = np.arange(TILE)
    me = np.arange(4)[:, None, None, None]
    k = np.arange(4)[None, None, :, None]
    i = np.arange(TILE)[None, :, None, None]
    distance = TILE * ((me ^ k) - me) + p[None, None, None, :] - i
    return weights(distance).reshape(4, TILE, 4 * TILE)


def column_table():
    c = np.arange(7 * TILE)[:, None] - 3 * TILE
    return weights(c - np.arange(COLS)[None, :] // COARSEN)


def etch(own, mate, near, far, guard, row_ref, col_ref, out, grid, cols):
    gx, gy = lax.axis_index("gx"), lax.axis_index("gy")
    odd = lax.rem(gx, 2)
    upper = lax.rem(lax.div(gx, 2), 2)
    swap = 1 - 2 * odd
    step = 2 - 4 * upper
    tiles = [own[...], mate[...], near[0], near[1], far[0], far[1]]
    offsets = [0 * gx, swap, step, step + swap, -step, -step + swap]
    lane = lax.broadcasted_iota(jnp.int32, (TILE, LANES), 1)
    for k in range(4):
        for half in range(2):
            block = jnp.zeros((TILE, LANES), F32)
            for n in range(4 * half, min(4 * half + 4, 6)):
                at = TILE * (n % 4)
                here = (lane >= at) & (lane < at + TILE)
                block = jnp.where(here, shifted(tiles[n], at - TILE * k), block)
            grid[pl.ds(TILE * k, TILE), pl.ds(LANES * half, LANES)] = block
    for n in range(6):
        start = pl.multiple_of((offsets[n] + 3) * TILE, TILE)
        cols[pl.ds(TILE * n, TILE), :] = col_ref[pl.ds(start, TILE), :]
    cols[pl.ds(6 * TILE, 2 * TILE), :] = jnp.zeros((2 * TILE, COLS), F32)
    across = jnp.dot(
        row_ref[gy], grid[...], precision=lax.Precision.HIGHEST, preferred_element_type=F32
    )
    smooth = jnp.dot(
        across, cols[...], precision=lax.Precision.HIGHEST, preferred_element_type=F32
    )
    factor = 1.0 - LOADING * smooth
    for i in range(TILE):
        rows = pl.ds(COARSEN * i, COARSEN)
        for t in range(2):
            piece = factor[i : i + 1, t * LANES : (t + 1) * LANES]
            cols_of = pl.ds(t * LANES, LANES)
            out[rows, cols_of] = (1.0 - guard[0, rows, cols_of]) * piece


def run_etch(own, mate, near, far, guard):
    return pl.pallas_call(
        etch,
        in_specs=[VM] * 7,
        out_specs=VM,
        out_shape=jax.ShapeDtypeStruct((ROWS, COLS), F32),
        scratch_shapes=[pltpu.VMEM((4 * TILE, COLS), F32), pltpu.VMEM((COLS, COLS), F32)],
        compiler_params=params(4),
        name="etch",
    )(own, mate, near, far, guard, jnp.asarray(row_table()), jnp.asarray(column_table()))


def swap(block, axis, partner):
    count = lax.axis_size(axis)
    route = [(i, partner(i)) for i in range(count) if 0 <= partner(i) < count]
    return lax.ppermute(block, axis, route)


def inside(i):
    return i ^ 1


def outside(i):
    return i - 1 if i % 2 == 0 else i + 1


def shards(acid_field, quencher_field):
    acid_field = pltpu.with_memory_space_constraint(acid_field, pltpu.HBM)
    quencher_field = pltpu.with_memory_space_constraint(quencher_field, pltpu.HBM)
    first, second = pack_rows(acid_field, quencher_field)
    second = swap(second, "gy", outside)
    first = swap(first, "gy", inside)
    state, strips = load_state(acid_field, quencher_field)
    state, strips, first, second = pack_columns(state, strips, first, second)
    second = swap(second, "gx", outside)
    first = swap(first, "gx", inside)
    state, guard = run_main(state)
    strips, guard, density = run_strips(strips, first, second, guard)
    acid_after = run_last(state, strips)
    tile = density[:, :TILE]
    tile = jnp.concatenate([tile, swap(tile, "gy", lambda i: i ^ 1)], 1)
    own = jnp.concatenate([tile, swap(tile, "gy", lambda i: i ^ 2)], 1)
    mate = swap(own, "gx", inside)
    pair = jnp.stack([own, mate], 0)
    far = swap(pair, "gx", lambda i: i - 2 if i // 2 % 2 == 0 else i + 2)
    near = swap(pair, "gx", lambda i: i ^ 2)
    etch_rate = run_etch(own, mate, near, far, guard)
    return acid_after, guard, etch_rate


def solution(mesh):
    in_specs = (P(None, "gy", "gx"), P(None, "gy", "gx"))
    out_specs = (P(None, "gy", "gx"), P(None, "gy", "gx"), P("gy", "gx"))
    return jax.shard_map(shards, mesh=mesh, in_specs=in_specs, out_specs=out_specs, check_vma=False)
```

time: 77.9 us -> 60.5 us (0.78)
  Pallas kernels: 42 us -> 28.3 us
  starting transfers between devices: 23.4 us -> 17.9 us
  local copies, waits for them, and re-layouts: 0.01 us -> 1.33 us
    pallas_call x4 -> x5, Pallas kernels: 39.8 us -> 26 us  [the longest x1 11.6 us: run_main(): pl.pallas_call(main_steps, in_specs=[VM], out_specs=[VM, VM], out_shape=[...]
    ppermute x9, starting transfers between devices: 23.4 us -> 17.9 us  [swap(): return lax.ppermute(block, axis, route)]
    unnamed x4 -> x5, local copies, waits for them, and re-layouts: 0.01 us -> 1.33 us
  transfers between devices with their start and end apart: 9 -> 9, of which waited for: 4 -> 4; matrix products, arithmetic and copies ran while one was open for 0% -> 2% of each run, Pallas kernels for 17% -> 34%
where the time goes in v2:
time: 60.5 us; the launch traced here: 60.2 us
  Pallas kernels  28.3 us (47%)
  starting transfers between devices  17.9 us (30%)
  waiting for transfers between devices  11.8 us (20%)
  local copies, waits for them, and re-layouts  1.33 us (2%)
  between operations  0.77 us (1%)
    ppermute x9, starting transfers between devices, swap(): return lax.ppermute(block, axis, route)  17.9 us
    ppermute x9, waiting for transfers between devices, swap(): return lax.ppermute(block, axis, route)  11.8 us
    pallas_call x1, Pallas kernels, run_main(): pl.pallas_call(main_steps, in_specs=[VM], out_specs=[VM, VM], out_shape=[...  11.6 us
    pallas_call x1, Pallas kernels, run_strips(): pl.pallas_call(strip_steps, in_specs=[VM] * 4, out_specs=[VM] * 3, out_sh...  5.6 us
    pallas_call x1, Pallas kernels, run_last(): pl.pallas_call(last_step, in_specs=[VM] * 2, out_specs=HB, out_shape=jax....  4.44 us
    pallas_call x1, Pallas kernels, load_state(): pl.pallas_call(fill_state, in_specs=[HB, HB], out_specs=[VM, VM], out_sha...  4.16 us
    unnamed x5, local copies, waits for them, and re-layouts  1.33 us
    pallas_call x1, Pallas kernels, run_etch(): pl.pallas_call(etch, in_specs=[VM] * 7, out_specs=VM, out_shape=jax.Shape...  1.3 us
  transfers between devices with their start and end apart: 9, of which 4 were waited for; matrix products, arithmetic and copies ran while one was open for 2% of the time, Pallas kernels for 34%

profile of v2, /device:TPU:24, one launch (start us, length us, event | category | flops | bytes accessed | tf_op | source)
XLA Modules:
  0.0 60.2 jit_solution(6959623609966876804)
XLA Ops:
  0.6 1.0 %pack_rows.1 = (f32[8,8,256]{2,1,0:T(8,128)S(1)}, f32[8,8,256]{2,1,0:T(8,128)S(1)}) custom-call(f32[8,256,256]{2,1,0:T(8,128)} %a_bot.1, f32[8,256,256]{2,1,0:T(8,128)} %a_bot.1, f32[8,256,256]{2,1,0:T(8,128)} %q_bot.1, f32[8,256,256]{2,1,0:T(8,128)} %q_bot.1), custom_call_target="tpu_custom_call" | custom-call | tf_op jit(solution)/shard_map/pack_rows/pallas_call | solution.py:66
  1.6 0.1 collective-permute-start
  1.7 2.7 %collective-permute-start.1 = (f32[8,8,256]{2,1,0:T(8,128)S(1)}, f32[8,8,256]{2,1,0:T(8,128)S(1)}, u32[]{:S(2)}, u32[]{:S(2)}) collective-permute-start(f32[8,8,256]{2,1,0:T(8,128)S(1)} %get-tuple-element.19), channel_id=1, source_target_pairs={{1,2},{2,1},{5,6},{6,5},{9,10},{10,9},{13,14},{14,13},{17,18},{18,... | collective-permute-start | bytes 196616 | tf_op jit(solution)/shard_map/ppermute | solution.py:568
  4.4 4.2 %load_state.1 = (f32[4,8,288,128]{3,2,1,0:T(8,128)S(1)}, f32[4,288,128]{2,1,0:T(8,128)S(1)}) custom-call(f32[8,256,256]{2,1,0:T(8,128)} %a_bot.1, f32[8,256,256]{2,1,0:T(8,128)} %q_bot.1), custom_call_target="tpu_custom_call" | custom-call | tf_op jit(solution)/shard_map/load_state/pallas_call | solution.py:127
  8.6 0.0 collective-permute-done.first_in
  8.6 0.0 collective-permute-done.1.second_in
  8.6 0.2 pack_columns.1
  8.9 2.0 %collective-permute-start.2 = (f32[17,8,128]{2,1,0:T(8,128)S(1)}, f32[17,8,128]{2,1,0:T(8,128)S(1)}, u32[]{:S(2)}, u32[]{:S(2)}) collective-permute-start(f32[17,8,128]{2,1,0:T(8,128)S(1)} %get-tuple-element.23), channel_id=1, source_target_pairs={{0,4},{4,0},{8,12},{12,8},{16,20},{20,16},{24,28},{28,24},{32,36},... | collective-permute-start | bytes 208904 | tf_op jit(solution)/shard_map/ppermute | solution.py:568
  10.9 9.4 %collective-permute-start.3 = (f32[17,8,128]{2,1,0:T(8,128)S(1)}, f32[17,8,128]{2,1,0:T(8,128)S(1)}, u32[]{:S(2)}, u32[]{:S(2)}) collective-permute-start(f32[17,8,128]{2,1,0:T(8,128)S(1)} %get-tuple-element.24), channel_id=1, source_target_pairs={{4,8},{8,4},{12,16},{16,12},{20,24},{24,20},{28,32},{32,28},{36,40... | collective-permute-start | bytes 208904 | tf_op jit(solution)/shard_map/ppermute | solution.py:568
  20.3 11.6 %main_steps.1 = (f32[4,8,288,128]{3,2,1,0:T(8,128)S(1)}, f32[8,256,256]{2,1,0:T(8,128)S(1)}) custom-call(f32[4,8,288,128]{3,2,1,0:T(8,128)S(1)} %get-tuple-element.20.state), custom_call_target="tpu_custom_call" | custom-call | flops 1000000000 | bytes 30000000 | tf_op jit(solution)/shard_map/main_steps/pallas_call | solution.py:290
  31.9 0.0 collective-permute-done.2.first_in
  31.9 0.0 collective-permute-done.3.second_in
  31.9 5.6 %strip_steps.1 = (f32[4,288,128]{2,1,0:T(8,128)S(1)}, f32[8,256,256]{2,1,0:T(8,128)S(1)}, f32[32,128]{1,0:T(8,128)S(1)}) custom-call(f32[4,288,128]{2,1,0:T(8,128)S(1)} %get-tuple-element.22.strips, f32[17,8,128]{2,1,0:T(8,128)S(1)} %collective-permute-done.2.first_in, ...), custom_call_target="tpu_custom_call", output_to_operand_aliasing={{1}: (3, {})} | custom-call | tf_op jit(solution)/shard_map/strip_steps/pallas_call | solution.py:420
  37.5 0.1 collective-permute-start.4
  37.6 1.2 %collective-permute-done.4 = f32[32,32]{1,0:T(8,128)S(1)} collective-permute-done((f32[32,32]{1,0:T(8,128)S(1)}, f32[32,32]{1,0:T(8,128)S(1)}, u32[]{:S(2)}, u32[]{:S(2)}) %collective-permute-start.4) | collective-permute-done | bytes 4128 | tf_op jit(solution)/shard_map/ppermute | solution.py:568
  38.8 0.1 pad_maximum_fusion.1
  38.9 0.1 collective-permute-start.5
  39.0 3.6 %collective-permute-done.5 = f32[32,64]{1,0:T(8,128)S(1)} collective-permute-done((f32[32,64]{1,0:T(8,128)S(1)}, f32[32,64]{1,0:T(8,128)S(1)}, u32[]{:S(2)}, u32[]{:S(2)}) %collective-permute-start.5) | collective-permute-done | bytes 8224 | tf_op jit(solution)/shard_map/ppermute | solution.py:568
  42.7 0.1 pad_maximum_fusion.2.own
  42.7 0.0 collective-permute-start.6
  42.8 3.7 %collective-permute-done.6.mate = f32[32,128]{1,0:T(8,128)S(1)} collective-permute-done((f32[32,128]{1,0:T(8,128)S(1)}, f32[32,128]{1,0:T(8,128)S(1)}, u32[]{:S(2)}, u32[]{:S(2)}) %collective-permute-start.6) | collective-permute-done | bytes 16416 | tf_op jit(solution)/shard_map/ppermute | solution.py:568
  46.5 3.3 %collective-permute-start.8 = (f32[2,32,128]{2,1,0:T(8,128)S(1)}, f32[2,32,128]{2,1,0:T(8,128)S(1)}, u32[]{:S(2)}, u32[]{:S(2)}) collective-permute-start(f32[2,32,128]{2,1,0:T(8,128)S(1)} %pad_maximum_fusion), channel_id=1, source_target_pairs={{8,16},{12,20},{16,8},{20,12},{24,32},{28,36},{32,24},{36,28},{40,... | collective-permute-start | bytes 98312 | tf_op jit(solution)/shard_map/ppermute | solution.py:568
  49.9 0.1 collective-permute-start.7
  50.0 1.3 %copy.13 = f32[8,256,256]{2,1,0:T(8,128)} copy(f32[8,256,256]{2,1,0:T(8,128)S(1)} %get-tuple-element.30.guard) | data formatting | bytes 4194304
  51.3 0.0 copy-start
  51.3 0.0 copy-start.1
  51.3 4.4 %last_step.1 = f32[8,256,256]{2,1,0:T(8,128)} custom-call(f32[4,8,288,128]{3,2,1,0:T(8,128)S(1)} %get-tuple-element.21.state, f32[4,288,128]{2,1,0:T(8,128)S(1)} %get-tuple-element.26.strips), custom_call_target="tpu_custom_call" | custom-call | tf_op jit(solution)/shard_map/last_step/pallas_call | solution.py:479
  55.7 3.2 %collective-permute-done.8.far = f32[2,32,128]{2,1,0:T(8,128)S(1)} collective-permute-done((f32[2,32,128]{2,1,0:T(8,128)S(1)}, f32[2,32,128]{2,1,0:T(8,128)S(1)}, u32[]{:S(2)}, u32[]{:S(2)}) %collective-permute-start.8) | collective-permute-done | bytes 32800 | tf_op jit(solution)/shard_map/ppermute | solution.py:568
  58.9 0.0 collective-permute-done.7.near
  58.9 0.0 copy-done
  58.9 0.0 copy-done.1
  58.9 1.3 %etch.1 = f32[256,256]{1,0:T(8,128)} custom-call(f32[32,128]{1,0:T(8,128)S(1)} %pad_maximum_fusion.2.own, f32[32,128]{1,0:T(8,128)S(1)} %collective-permute-done.6.mate, f32[2,32,128]{2,1,0:T(8,128)S(1)} %collective-permute-done.7.near, f32[2,32,128]{2,1,0:T(8,128)S(1)} %collective-permute-done.8.far, f32[8,256,256]{2,1,0:T(8,128)S(1)} %get-tuple-element.30.guard, ...), custom_call_target="tpu_custom_call" | custom-call | tf_op jit(solution)/shard_map/etch/pallas_call | solution.py:554
  (1 shorter events, 0.0 us)
Async XLA Ops:
  1.6 7.0 %collective-permute-start = (f32[8,8,256]{2,1,0:T(8,128)S(1)}, f32[8,8,256]{2,1,0:T(8,128)S(1)}, u32[]{:S(2)}, u32[]{:S(2)}) collective-permute-start(f32[8,8,256]{2,1,0:T(8,128)S(1)} %get-tuple-element.18), channel_id=1, source_target_pairs={{0,1},{1,0},{2,3},{3,2},{4,5},{5,4},{6,7},{7,6},{8,9},{9,8},{10,11... | collective-permute-start | bytes 196616 | tf_op jit(solution)/shard_map/ppermute | solution.py:568
  1.7 6.9 %collective-permute-start.1 = (f32[8,8,256]{2,1,0:T(8,128)S(1)}, f32[8,8,256]{2,1,0:T(8,128)S(1)}, u32[]{:S(2)}, u32[]{:S(2)}) collective-permute-start(f32[8,8,256]{2,1,0:T(8,128)S(1)} %get-tuple-element.19), channel_id=1, source_target_pairs={{1,2},{2,1},{5,6},{6,5},{9,10},{10,9},{13,14},{14,13},{17,18},{18,... | collective-permute-start | bytes 196616 | tf_op jit(solution)/shard_map/ppermute | solution.py:568
  8.9 23.1 %collective-permute-start.2 = (f32[17,8,128]{2,1,0:T(8,128)S(1)}, f32[17,8,128]{2,1,0:T(8,128)S(1)}, u32[]{:S(2)}, u32[]{:S(2)}) collective-permute-start(f32[17,8,128]{2,1,0:T(8,128)S(1)} %get-tuple-element.23), channel_id=1, source_target_pairs={{0,4},{4,0},{8,12},{12,8},{16,20},{20,16},{24,28},{28,24},{32,36},... | collective-permute-start | bytes 208904 | tf_op jit(solution)/shard_map/ppermute | solution.py:568
  10.9 21.1 %collective-permute-start.3 = (f32[17,8,128]{2,1,0:T(8,128)S(1)}, f32[17,8,128]{2,1,0:T(8,128)S(1)}, u32[]{:S(2)}, u32[]{:S(2)}) collective-permute-start(f32[17,8,128]{2,1,0:T(8,128)S(1)} %get-tuple-element.24), channel_id=1, source_target_pairs={{4,8},{8,4},{12,16},{16,12},{20,24},{24,20},{28,32},{32,28},{36,40... | collective-permute-start | bytes 208904 | tf_op jit(solution)/shard_map/ppermute | solution.py:568
  37.5 1.3 %collective-permute-start.4 = (f32[32,32]{1,0:T(8,128)S(1)}, f32[32,32]{1,0:T(8,128)S(1)}, u32[]{:S(2)}, u32[]{:S(2)}) collective-permute-start(f32[32,32]{1,0:T(8,128)S(1)} %bitcast.5), channel_id=1, source_target_pairs={{0,1},{1,0},{2,3},{3,2},{4,5},{5,4},{6,7},{7,6},{8,9},{9,8},{10,11... | collective-permute-start | bytes 12296 | tf_op jit(solution)/shard_map/ppermute | solution.py:568
  38.9 3.8 %collective-permute-start.5 = (f32[32,64]{1,0:T(8,128)S(1)}, f32[32,64]{1,0:T(8,128)S(1)}, u32[]{:S(2)}, u32[]{:S(2)}) collective-permute-start(f32[32,64]{1,0:T(8,128)S(1)} %pad_maximum_fusion.1), channel_id=1, source_target_pairs={{0,2},{1,3},{2,0},{3,1},{4,6},{5,7},{6,4},{7,5},{8,10},{9,11},{10,... | collective-permute-start | bytes 24584 | tf_op jit(solution)/shard_map/ppermute | solution.py:568
  42.7 3.8 %collective-permute-start.6 = (f32[32,128]{1,0:T(8,128)S(1)}, f32[32,128]{1,0:T(8,128)S(1)}, u32[]{:S(2)}, u32[]{:S(2)}) collective-permute-start(f32[32,128]{1,0:T(8,128)S(1)} %pad_maximum_fusion.2.own), channel_id=1, source_target_pairs={{0,4},{4,0},{8,12},{12,8},{16,20},{20,16},{24,28},{28,24},{32,36},... | collective-permute-start | bytes 49160 | tf_op jit(solution)/shard_map/ppermute | solution.py:568
  46.5 12.4 %collective-permute-start.8 = (f32[2,32,128]{2,1,0:T(8,128)S(1)}, f32[2,32,128]{2,1,0:T(8,128)S(1)}, u32[]{:S(2)}, u32[]{:S(2)}) collective-permute-start(f32[2,32,128]{2,1,0:T(8,128)S(1)} %pad_maximum_fusion), channel_id=1, source_target_pairs={{8,16},{12,20},{16,8},{20,12},{24,32},{28,36},{32,24},{36,28},{40,... | collective-permute-start | bytes 98312 | tf_op jit(solution)/shard_map/ppermute | solution.py:568
  49.9 9.1 %collective-permute-start.7 = (f32[2,32,128]{2,1,0:T(8,128)S(1)}, f32[2,32,128]{2,1,0:T(8,128)S(1)}, u32[]{:S(2)}, u32[]{:S(2)}) collective-permute-start(f32[2,32,128]{2,1,0:T(8,128)S(1)} %pad_maximum_fusion), channel_id=1, source_target_pairs={{0,8},{4,12},{8,0},{12,4},{16,24},{20,28},{24,16},{28,20},{32,40},... | collective-permute-start | bytes 98312 | tf_op jit(solution)/shard_map/ppermute | solution.py:568
  51.3 7.7 %copy-start = (f32[224,256]{1,0:T(8,128)S(1)}, f32[224,256]{1,0:T(8,128)}, u32[]{:S(2)}) copy-start(f32[224,256]{1,0:T(8,128)} %constant.5.clone.col_ref) | copy-start | bytes 688132
  51.3 7.7 %copy-start.1 = (f32[4,32,128]{2,1,0:T(8,128)S(1)}, f32[4,32,128]{2,1,0:T(8,128)}, u32[]{:S(2)}) copy-start(f32[4,32,128]{2,1,0:T(8,128)} %constant.4.clone.row_ref) | copy-start | bytes 196612

commit v3 on v2

v3 whole, which is shorter than its diff:
```python
import functools

import jax
import jax.numpy as jnp
import numpy as np
from jax import lax
from jax.experimental import pallas as pl
from jax.experimental.pallas import tpu as pltpu
from jax.sharding import PartitionSpec as P

RATE_ACID = 0.15
RATE_QUENCH = 0.05
NEUTRAL = 0.1
DEPROTECT = 0.35
LOADING = 0.8
STEPS = 4
COARSEN = 8
REACH = 64
SPREAD = 25.0

LAYERS = 8
ROWS = 256
COLS = 256
LANES = 128
SUBS = 8
RUN = ROWS // SUBS
HALO = STEPS
BASE = 2 * SUBS
EXT = ROWS + 2 * BASE
LIVE = ROWS + BASE
FOLD = LIVE // SUBS // 2
PARTS = 4
TILE = ROWS // COARSEN
BATCH = 4
GROUP = 16

VM = pl.BlockSpec(memory_space=pltpu.VMEM)
HB = pl.BlockSpec(memory_space=pltpu.HBM)
F32 = jnp.float32


def params(mib):
    return pltpu.CompilerParams(vmem_limit_bytes=mib * 1024 * 1024)


def vmem(shape):
    return pltpu.VMEM(shape, F32)


def iota(dim):
    return lax.broadcasted_iota(jnp.int32, (SUBS, LANES), dim)


def row_strips(a_top, a_bot, q_top, q_bot, first_ref, second_ref):
    even = lax.rem(lax.axis_index("gy"), 2) == 0
    low = lax.broadcasted_iota(jnp.int32, (SUBS, COLS), 0) < HALO
    for d in range(LAYERS):
        top = jnp.where(low, a_top[d], pltpu.roll(q_top[d], HALO, 0))
        bot = jnp.where(low, pltpu.roll(a_bot[d], HALO, 0), q_bot[d])
        first_ref[d] = jnp.where(even, bot, top)
        second_ref[d] = jnp.where(even, top, bot)


def pack_rows(acid, quench):
    block = (LAYERS, SUBS, COLS)
    top = pl.BlockSpec(block, lambda i: (0, 0, 0))
    bot = pl.BlockSpec(block, lambda i: (0, RUN - 1, 0))
    out = jax.ShapeDtypeStruct(block, F32)
    return pl.pallas_call(
        row_strips,
        grid=(1,),
        in_specs=[top, bot, top, bot],
        out_specs=[pl.BlockSpec(block, lambda i: (0, 0, 0))] * 2,
        out_shape=[out, out],
        compiler_params=params(4),
        name="pack_rows",
    )(acid, acid, quench, quench)


def shifted(x, by):
    return pltpu.roll(x, by % LANES, 1)


def rows_at(i):
    return pl.ds(pl.multiple_of(i * SUBS, SUBS), SUBS)


def own_edges(state, edges, i):
    lane = iota(1)
    rows = rows_at(i)
    for f in range(2):
        total = None
        for d in range(LAYERS):
            first = jnp.where(lane < 2 * HALO, state[2 * f, d, rows, :], 0.0)
            both = jnp.where(lane >= LANES - 2 * HALO, state[2 * f + 1, d, rows, :], first)
            moved = shifted(both, GROUP * d + HALO)
            total = moved if d == 0 else total + moved
        edges[f, rows, :] = total


def fill_state(acid, quench, state, edges, sems):
    size = ROWS // PARTS
    copies = []
    for p in range(PARTS):
        for t in range(4):
            source = (acid, quench)[t // 2].at[
                :, pl.ds(size * p, size), pl.ds((t % 2) * LANES, LANES)
            ]
            target = state.at[t, :, pl.ds(BASE + size * p, size), :]
            copy = pltpu.make_async_copy(source, target, sems.at[p, t])
            copy.start()
            copies.append(copy)
    for p in range(PARTS):
        for t in range(4):
            copies[4 * p + t].wait()

        def body(i, _):
            own_edges(state, edges, i)
            return 0

        first = (BASE + size * p) // SUBS
        lax.fori_loop(first, first + size // SUBS, body, 0, unroll=2)


def load_state(acid, quench):
    return pl.pallas_call(
        fill_state,
        in_specs=[HB, HB],
        out_specs=[VM, VM],
        out_shape=[vmem((4, LAYERS, EXT, LANES)), vmem((2, EXT, LANES))],
        scratch_shapes=[pltpu.SemaphoreType.DMA((PARTS, 4))],
        compiler_params=params(4),
        name="load_state",
    )(acid, quench)


def column_strips(state_in, edges_in, second_in, first_in, state, edges, second_ref, first_ref):
    del state_in, edges_in
    even_row = lax.rem(lax.axis_index("gy"), 2) == 0
    even_col = lax.rem(lax.axis_index("gx"), 2) == 0
    sub = iota(0)
    place = iota(1) % GROUP
    for d in range(LAYERS):
        for t in range(2):
            cols = pl.ds(t * LANES, LANES)
            one, two = first_in[d, :, cols], second_in[d, :, cols]
            top = jnp.where(even_row, two, one)
            bot = jnp.where(even_row, one, two)
            above, below = pl.ds(SUBS, SUBS), pl.ds(BASE + ROWS, SUBS)
            state[t, d, above, :] = jnp.where(sub >= HALO, pltpu.roll(top, HALO, 0), 0.0)
            state[2 + t, d, above, :] = jnp.where(sub >= HALO, top, 0.0)
            state[t, d, below, :] = jnp.where(sub < HALO, bot, 0.0)
            state[2 + t, d, below, :] = jnp.where(sub < HALO, pltpu.roll(bot, HALO, 0), 0.0)
    own_edges(state, edges, 1)
    own_edges(state, edges, (BASE + ROWS) // SUBS)
    for j in range(FOLD):
        left = jnp.zeros((SUBS, LANES), F32)
        right = jnp.zeros((SUBS, LANES), F32)
        for m in range(4):
            rows = pl.ds(SUBS * (1 + j + FOLD * (m // 2)), SUBS)
            moved = shifted(edges[m % 2, rows, :], 4 * m)
            left = jnp.where((place - HALO - 4 * m) % GROUP < HALO, moved, left)
            right = jnp.where((place - 4 * m) % GROUP < HALO, moved, right)
        first_ref[j] = jnp.where(even_col, right, left)
        second_ref[j] = jnp.where(even_col, left, right)


def pack_columns(state, edges, second, first):
    strip = jax.ShapeDtypeStruct((FOLD, SUBS, LANES), F32)
    return pl.pallas_call(
        column_strips,
        in_specs=[VM] * 4,
        out_specs=[VM] * 4,
        out_shape=[vmem((4, LAYERS, EXT, LANES)), vmem((2, EXT, LANES)), strip, strip],
        input_output_aliases={0: 0, 1: 1},
        compiler_params=params(4),
        name="pack_columns",
    )(state, edges, second, first)


def halves(x):
    high = x.astype(jnp.bfloat16)
    return high, (x - high.astype(F32)).astype(jnp.bfloat16)


def neighbour_sums(parts, matrix):
    split = [halves(x) for x in parts]
    stacked = jnp.concatenate([h for h, _ in split] + [l for _, l in split], 1)
    return jnp.dot(stacked, matrix, preferred_element_type=F32)


def beside_matrix():
    shape = (2 * COLS, COLS)
    row = lax.broadcasted_iota(jnp.int32, shape, 0) % COLS
    col = lax.broadcasted_iota(jnp.int32, shape, 1)
    return (jnp.abs(row - col) == 1).astype(jnp.bfloat16)


def strip_matrix(offset):
    shape = (2 * LANES, LANES)
    row = lax.broadcasted_iota(jnp.int32, shape, 0) % LANES
    col = lax.broadcasted_iota(jnp.int32, shape, 1)
    layer = ((col + offset) % LANES) // GROUP
    gap = (row - col + LANES) % LANES
    beside = ((gap == 1) | (gap == LANES - 1)).astype(F32)
    lower = (gap == jnp.where(layer == 0, 0, LANES - GROUP)).astype(F32)
    upper = (gap == jnp.where(layer == LAYERS - 1, 0, GROUP)).astype(F32)
    return (beside + lower + upper).astype(jnp.bfloat16)


def row_open(kind):
    gy = lax.axis_index("gy")
    if kind == 1:
        return 1.0
    outside = gy == 0 if kind == 0 else gy == lax.axis_size("gy") - 1
    return 1.0 - outside.astype(jnp.int32).astype(F32)


def sweep(body):
    def step(p, _):
        body(2 + p * BATCH, BATCH, 1)
        return 0

    body(1, 1, 0)
    lax.fori_loop(0, RUN // BATCH, step, 0)
    body(2 + RUN, 1, 2)


def beside_rows(read, center, i, mixed):
    n = len(center)
    above = [read(pl.ds((i + j) * SUBS - 1, SUBS)) for j in range(n)]
    if not mixed:
        return [above[j] + read(pl.ds((i + j) * SUBS + 1, SUBS)) for j in range(n)]
    last = iota(0) == SUBS - 1
    up = [pltpu.roll(x, SUBS - 1, 0) for x in center + [read(rows_at(i + n))]]
    return [above[j] + jnp.where(last, up[j + 1], up[j]) for j in range(n)]


def main_sums(src, sums, matrix, fields, start, count):
    for f in fields:
        parts = [src[2 * f + t, :, pl.ds(start, count), :].reshape(LAYERS * count, LANES) for t in range(2)]
        total = neighbour_sums(parts, matrix)
        for t in range(2):
            piece = total[:, t * LANES : (t + 1) * LANES].reshape(LAYERS, count, LANES)
            sums[2 * f + t, :, pl.ds(start, count), :] = piece


def main_steps(role, state, *refs):
    out, guard, one, two, sums, total, matrix = refs[-7:]

    @pl.when(lax.rem(lax.axis_index("gx"), 2) == role)
    def _():
        main_part(state, out, guard, one, two, sums, total, matrix)


def main_part(state, out, guard, one, two, sums, total, matrix):
    matrix[...] = beside_matrix()

    def advance(src, dst, visit):
        main_sums(src, sums, matrix[...], (0, 1), SUBS, LIVE)

        def body(i, n, kind):
            shut = row_open(kind)
            load = lambda d: [[src[t, d, rows_at(i + j), :] for j in range(n)] for t in range(4)]
            before = center = load(0)
            for d in range(LAYERS):
                after = load(d + 1) if d + 1 < LAYERS else center
                around = []
                for t in range(4):
                    rows = beside_rows(lambda r, t=t, d=d: src[t, d, r, :], center[t], i, t % 2 == 1)
                    around.append(
                        [
                            (rows[j] + (before[t][j] + after[t][j])) + sums[t, d, rows_at(i + j), :]
                            for j in range(n)
                        ]
                    )
                for t in range(2):
                    for j in range(n):
                        at = rows_at(i + j)
                        scaled = NEUTRAL * center[t][j]
                        acid = RATE_ACID * around[t][j] + scaled * (1.0 - center[2 + t][j])
                        quench = RATE_QUENCH * around[2 + t][j] + center[2 + t][j] * (
                            (1.0 - 6.0 * RATE_QUENCH) - scaled
                        )
                        if kind != 1:
                            acid, quench = acid * shut, quench * shut
                        dst[t, d, at, :] = acid
                        dst[2 + t, d, at, :] = quench
                        if kind == 1:
                            visit(t, d, i + j, center[t][j], acid)
                before, center = center, after

        sweep(body)

    def begin(t, d, i, old, new):
        total[t, d, rows_at(i - 2), :] = old + new

    def protect(t, d, i, old, new):
        rows = rows_at(i - 2)
        guard[d, rows, pl.ds(t * LANES, LANES)] = jnp.exp(
            -DEPROTECT * (total[t, d, rows, :] + (old + new))
        )

    advance(state, one, begin)
    advance(one, two, lambda *_: None)
    advance(two, out, protect)


def run_main(role, state, *earlier):
    grid = (4, LAYERS, EXT, LANES)
    return pl.pallas_call(
        functools.partial(main_steps, role),
        in_specs=[VM] * (1 + len(earlier)),
        out_specs=[VM, VM],
        out_shape=[vmem(grid), vmem((LAYERS, ROWS, COLS))],
        input_output_aliases={1: 0, 2: 1} if earlier else {},
        scratch_shapes=[
            pltpu.VMEM(grid, F32),
            pltpu.VMEM(grid, F32),
            pltpu.VMEM(grid, F32),
            pltpu.VMEM((2, LAYERS, ROWS, LANES), F32),
            pltpu.VMEM((2 * COLS, COLS), jnp.bfloat16),
        ],
        compiler_params=params(28),
        cost_estimate=pl.CostEstimate(
            flops=(10**9, 1)[role], bytes_accessed=(3 * 10**7, 1)[role], transcendentals=0
        ),
        name=("main_even", "main_odd")[role],
    )(state, *earlier)


def strip_sums(src, sums, matrices, fields):
    rows = pl.ds(SUBS, LIVE)
    for side in range(2):
        stacked = jnp.concatenate([src[2 * f + side, rows, :] for f in fields], 0)
        total = neighbour_sums([stacked], matrices[side])
        for n, f in enumerate(fields):
            sums[2 * f + side, rows, :] = total[n * LIVE : (n + 1) * LIVE]


def strip_open():
    gx = lax.axis_index("gx")
    place = iota(1) % GROUP
    left = jnp.where((place < HALO) & (gx == 0), 0.0, 1.0)
    right = jnp.where((place >= HALO) & (place < 2 * HALO) & (gx == lax.axis_size("gx") - 1), 0.0, 1.0)
    return left, right


def put_edges(target, i, left, right, visit):
    lane = iota(1)
    rows = rows_at(i - 2)
    place = lane % GROUP
    both = jnp.where((place >= HALO) & (place < 2 * HALO), left, right)
    for d in range(LAYERS):
        moved = shifted(both, -GROUP * d - HALO)
        for t in range(2):
            here = lane < HALO if t == 0 else lane >= LANES - HALO
            cols = pl.ds(t * LANES, LANES)
            value = jnp.where(here, moved, target[d, rows, cols])
            target[d, rows, cols] = value
            visit(d, t, value)


def strip_steps(edges, inner_in, up_in, down_in, guard_in, out, guard, density, one, two, sums, total, pooled):
    del guard_in
    even_col = lax.rem(lax.axis_index("gx"), 2) == 0
    place = iota(1) % GROUP
    opens = strip_open()
    matrices = strip_matrix(0), strip_matrix(HALO)
    for j in range(FOLD):
        left = jnp.where(even_col, up_in[j], inner_in[j])
        right = jnp.where(even_col, inner_in[j], down_in[j])
        for m in range(4):
            rows = pl.ds(SUBS * (1 + j + FOLD * (m // 2)), SUBS)
            f = m % 2
            own = edges[f, rows, :]
            near = (place >= HALO) & (place < 2 * HALO)
            kept = jnp.where((place >= HALO) & (place < 3 * HALO), own, 0.0)
            one[2 * f, rows, :] = jnp.where(place < HALO, shifted(left, -4 * m), kept)
            kept = jnp.where((place < HALO) | (place >= 3 * HALO), own, 0.0)
            one[2 * f + 1, rows, :] = jnp.where(near, shifted(right, -4 * m), kept)

    def advance(src, dst, visit):
        strip_sums(src, sums, matrices, (0, 1))

        def body(i, n, kind):
            for side in range(2):
                shut = opens[side] * row_open(kind)
                for j in range(n):
                    rows = rows_at(i + j)
                    center = [src[2 * f + side, rows, :] for f in range(2)]
                    around = []
                    for f in range(2):
                        read = lambda r, f=f, side=side: src[2 * f + side, r, :]
                        beside = beside_rows(read, [center[f]], i + j, False)
                        around.append(beside[0] + sums[2 * f + side, rows, :])
                    scaled = NEUTRAL * center[0]
                    acid = RATE_ACID * around[0] + scaled * (1.0 - center[1])
                    quench = RATE_QUENCH * around[1] + center[1] * (
                        (1.0 - 6.0 * RATE_QUENCH) - scaled
                    )
                    acid = acid * shut
                    dst[side, rows, :] = acid
                    dst[2 + side, rows, :] = quench * shut
                    visit(side, rows, center[0], acid)

        sweep(body)

    def begin(side, rows, old, new):
        total[side, rows, :] = old + new

    def protect(side, rows, old, new):
        total[side, rows, :] = jnp.exp(-DEPROTECT * (total[side, rows, :] + (old + new)))

    advance(one, two, begin)
    advance(two, one, lambda *_: None)
    advance(one, out, protect)

    def merge(i, _):
        kept = [None, None]

        def add(d, t, value):
            kept[t] = value if d == 0 else kept[t] + value

        put_edges(guard, i, total[0, rows_at(i), :], total[1, rows_at(i), :], add)
        for t in range(2):
            pooled[rows_at(i - 2), pl.ds(t * LANES, LANES)] = kept[t]
        return 0

    lax.fori_loop(2, 2 + RUN, merge, 0, unroll=2)
    fine = pooled[...].reshape(TILE, COARSEN, COLS).sum(1)
    col = lax.broadcasted_iota(jnp.int32, (COLS, LANES), 0)
    block = lax.broadcasted_iota(jnp.int32, (COLS, LANES), 1)
    pool = (col // COARSEN == block).astype(F32)
    coarse = jnp.dot(fine, pool, precision=lax.Precision.HIGHEST, preferred_element_type=F32)
    wide = lax.broadcasted_iota(jnp.int32, (TILE, LANES), 1)
    mean = 1.0 - coarse * (1.0 / (LAYERS * COARSEN * COARSEN))
    density[...] = jnp.where(wide < TILE, mean, 0.0)


def run_strips(edges, inner, up, down, guard):
    edge = (4, EXT, LANES)
    whole = (LAYERS, ROWS, COLS)
    return pl.pallas_call(
        strip_steps,
        in_specs=[VM] * 5,
        out_specs=[VM] * 3,
        out_shape=[vmem(edge), vmem(whole), jax.ShapeDtypeStruct((TILE, LANES), F32)],
        input_output_aliases={4: 1},
        scratch_shapes=[
            pltpu.VMEM(edge, F32),
            pltpu.VMEM(edge, F32),
            pltpu.VMEM(edge, F32),
            pltpu.VMEM((2, EXT, LANES), F32),
            pltpu.VMEM((ROWS, COLS), F32),
        ],
        compiler_params=params(8),
        name="strip_steps",
    )(edges, inner, up, down, guard)


def last_step(
    state, strips, guard, col_ref, acid_out, guard_out, cols, sums, edge_sums, matrix, land, sems
):
    kept = pltpu.make_async_copy(guard, guard_out, sems.at[PARTS])
    kept.start()
    matrix[...] = beside_matrix()
    main_sums(state, sums, matrix[...], (0,), BASE, ROWS)
    strip_sums(strips, edge_sums, (strip_matrix(0), strip_matrix(HALO)), (0,))
    n = BATCH

    def body(p, _):
        i = 2 + p * n
        for t in range(2):
            load = lambda d, t=t: [state[t, d, rows_at(i + j), :] for j in range(n)]
            before = center = load(0)
            for d in range(LAYERS):
                after = load(d + 1) if d + 1 < LAYERS else center
                rows = beside_rows(lambda r, t=t, d=d: state[t, d, r, :], center, i, t == 1)
                for j in range(n):
                    at = rows_at(i + j)
                    around = (rows[j] + (before[j] + after[j])) + sums[t, d, at, :]
                    land[d, rows_at(i + j - 2), pl.ds(t * LANES, LANES)] = RATE_ACID * around + (
                        NEUTRAL * center[j]
                    ) * (1.0 - state[2 + t, d, at, :])
                before, center = center, after
        for j in range(n):
            at = rows_at(i + j)
            edges = []
            for side in range(2):
                center = strips[side, at, :]
                beside = beside_rows(lambda r, side=side: strips[side, r, :], [center], i + j, False)
                around = beside[0] + edge_sums[side, at, :]
                edges.append(
                    RATE_ACID * around + (NEUTRAL * center) * (1.0 - strips[2 + side, at, :])
                )
            put_edges(land, i + j, *edges, lambda *_: None)
        return 0

    size = ROWS // PARTS
    copies = []
    for p in range(PARTS):
        count = size // SUBS // n
        lax.fori_loop(p * count, (p + 1) * count, body, 0)
        part = pl.ds(size * p, size)
        copies.append(pltpu.make_async_copy(land.at[:, part, :], acid_out.at[:, part, :], sems.at[p]))
        copies[p].start()
    for m, offset in enumerate(tile_offsets()):
        start = pl.multiple_of((offset + 3) * TILE, TILE)
        cols[pl.ds(TILE * m, TILE), :] = col_ref[pl.ds(start, TILE), :]
    for copy in copies:
        copy.wait()
    kept.wait()


def run_last(state, strips, guard):
    whole = jax.ShapeDtypeStruct((LAYERS, ROWS, COLS), F32)
    return pl.pallas_call(
        last_step,
        in_specs=[VM] * 4,
        out_specs=[HB, HB, VM],
        out_shape=[whole, whole, vmem((6 * TILE, COLS))],
        scratch_shapes=[
            pltpu.VMEM((2, LAYERS, EXT, LANES), F32),
            pltpu.VMEM((2, EXT, LANES), F32),
            pltpu.VMEM((2 * COLS, COLS), jnp.bfloat16),
            pltpu.VMEM((LAYERS, ROWS, COLS), F32),
            pltpu.SemaphoreType.DMA((PARTS + 1,)),
        ],
        compiler_params=params(12),
        cost_estimate=pl.CostEstimate(flops=10**9, bytes_accessed=10**7, transcendentals=0),
        name="last_step",
    )(state, strips, guard, jnp.asarray(column_table()))


def weights(distance):
    offset = np.arange(-REACH, REACH + 1, dtype=np.float64)
    norm = np.exp(-offset * offset / (2.0 * SPREAD * SPREAD)).sum()
    value = np.exp(-(distance.astype(np.float64) ** 2) / (2.0 * SPREAD * SPREAD))
    return np.where(np.abs(distance) <= REACH, value / norm, 0.0).astype(np.float32)


def row_table():
    p = np.arange(TILE)
    me = np.arange(4)[:, None, None, None]
    k = np.arange(4)[None, None, :, None]
    i = np.arange(TILE)[None, :, None, None]
    distance = TILE * ((me ^ k) - me) + p[None, None, None, :] - i
    return weights(distance).reshape(4, TILE, 4 * TILE)


def column_table():
    c = np.arange(7 * TILE)[:, None] - 3 * TILE
    return weights(c - np.arange(COLS)[None, :] // COARSEN)


def tile_offsets():
    gx = lax.axis_index("gx")
    beside = 1 - 2 * lax.rem(gx, 2)
    step = 2 - 4 * lax.rem(lax.div(gx, 2), 2)
    return [0 * gx, beside, step, step + beside, -step, -step + beside]


def etch(low, high, guard, row_ref, cols, out):
    gy = lax.axis_index("gy")
    across = sum(
        jnp.dot(
            row_ref[gy, :, pl.ds(2 * TILE * n, 2 * TILE)],
            part[...],
            precision=lax.Precision.HIGHEST,
            preferred_element_type=F32,
        )
        for n, part in enumerate((low, high))
    )
    smooth = jnp.dot(across, cols[...], precision=lax.Precision.HIGHEST, preferred_element_type=F32)
    factor = 1.0 - LOADING * smooth
    for i in range(TILE):
        rows = pl.ds(COARSEN * i, COARSEN)
        for t in range(2):
            piece = factor[i : i + 1, t * LANES : (t + 1) * LANES]
            cols_of = pl.ds(t * LANES, LANES)
            out[rows, cols_of] = (1.0 - guard[0, rows, cols_of]) * piece


def run_etch(low, high, guard, cols):
    return pl.pallas_call(
        etch,
        in_specs=[VM] * 5,
        out_specs=VM,
        out_shape=jax.ShapeDtypeStruct((ROWS, COLS), F32),
        compiler_params=params(4),
        name="etch",
    )(low, high, guard, jnp.asarray(row_table()), cols)


def swap(block, axis, partner):
    count = lax.axis_size(axis)
    route = [(i, partner(i)) for i in range(count) if 0 <= partner(i) < count]
    return lax.ppermute(block, axis, route)


def shift(block, axis, odd):
    count = lax.axis_size(axis)
    route = [(i, i + 2 * odd - 1) for i in range(count) if i % 2 == odd]
    return lax.ppermute(block, axis, [(i, k) for i, k in route if 0 <= k < count])


def inside(i):
    return i ^ 1


def outside(i):
    return i - 1 if i % 2 == 0 else i + 1


def shards(acid_field, quencher_field):
    acid_field = pltpu.with_memory_space_constraint(acid_field, pltpu.HBM)
    quencher_field = pltpu.with_memory_space_constraint(quencher_field, pltpu.HBM)
    first, second = pack_rows(acid_field, quencher_field)
    second = swap(second, "gy", outside)
    first = swap(first, "gy", inside)
    state, edges = load_state(acid_field, quencher_field)
    state, edges, second, first = pack_columns(state, edges, second, first)
    inner = swap(first, "gx", inside)
    up = shift(second, "gx", 1)
    state_even, guard = run_main(0, state)
    second, state_even = lax.optimization_barrier((second, state_even))
    down = shift(second, "gx", 0)
    up, state_even = lax.optimization_barrier((up, state_even))
    state, guard = run_main(1, state, state_even, guard)
    strips, guard, density = run_strips(edges, inner, up, down, guard)
    tile = density[:, :TILE]
    pair = jnp.concatenate([tile, swap(tile, "gx", inside)], 1)
    far = swap(pair, "gx", lambda i: i - 2 if i // 2 % 2 == 0 else i + 2)
    near = swap(pair, "gx", lambda i: i ^ 2)
    acid_after, inhibitor, cols = run_last(state, strips, guard)
    near, far, cols = lax.optimization_barrier((near, far, cols))
    six = jnp.concatenate([pair, near, far], 1)
    low = jnp.concatenate([six, swap(six, "gy", lambda i: i ^ 1)], 0)
    high = swap(low, "gy", lambda i: i ^ 2)
    etch_rate = run_etch(low, high, guard, cols)
    return acid_after, inhibitor, etch_rate


def solution(mesh):
    in_specs = (P(None, "gy", "gx"), P(None, "gy", "gx"))
    out_specs = (P(None, "gy", "gx"), P(None, "gy", "gx"), P("gy", "gx"))
    return jax.shard_map(shards, mesh=mesh, in_specs=in_specs, out_specs=out_specs, check_vma=False)
```

time: 60.5 us -> 53 us (0.88)
  Pallas kernels: 28.3 us -> 20.9 us
  starting transfers between devices: 17.9 us -> 20.4 us
  waiting for transfers between devices: 11.8 us -> 9.87 us
  local copies, waits for them, and re-layouts: 1.33 us -> 0.01 us
    pallas_call x4 -> x5, Pallas kernels: 23 us -> 16.8 us  [the longest x2 9.1 us: run_main(): pl.pallas_call(functools.partial(main_steps, role), in_specs=[VM] * (1 +...]
    ppermute x9 -> x8, waiting for transfers between devices: 11.8 us -> 7.97 us  [swap(): return lax.ppermute(block, axis, route)]
    ppermute x0 -> x2, starting transfers between devices: none -> 2.57 us  [shift(): lax.ppermute(block, axis, [(i, k) for i, k in route if 0 <= k < count])]
    ppermute x0 -> x2, waiting for transfers between devices: none -> 1.9 us  [shift(): lax.ppermute(block, axis, [(i, k) for i, k in route if 0 <= k < count])]
    unnamed x5 -> x4, local copies, waits for them, and re-layouts: 1.33 us -> 0.01 us
    pallas_call x1, Pallas kernels: 4.16 us -> 3.03 us  [load_state(): pl.pallas_call(fill_state, in_specs=[HB, HB], out_specs=[VM, VM], out_sha...]
    ppermute x9 -> x8, starting transfers between devices: 17.9 us -> 17.9 us  [swap(): return lax.ppermute(block, axis, route)]
  transfers between devices with their start and end apart: 9 -> 10, of which waited for: 4 -> 8; matrix products, arithmetic and copies ran while one was open for 2% -> 0% of each run, Pallas kernels for 34% -> 29%
where the time goes in v3:
time: 53 us; the launch traced here: 52.3 us
  Pallas kernels  20.9 us (39%)
  starting transfers between devices  20.4 us (38%)
  waiting for transfers between devices  9.87 us (19%)
  between operations  0.78 us (1%)
    ppermute x8, starting transfers between devices, swap(): return lax.ppermute(block, axis, route)  17.9 us
    pallas_call x2, Pallas kernels, run_main(): pl.pallas_call(functools.partial(main_steps, role), in_specs=[VM] * (1 +...  9.1 us
    ppermute x8, waiting for transfers between devices, swap(): return lax.ppermute(block, axis, route)  7.97 us
    pallas_call x1, Pallas kernels, run_strips(): pl.pallas_call(strip_steps, in_specs=[VM] * 5, out_specs=[VM] * 3, out_sh...  3.38 us
    pallas_call x1, Pallas kernels, run_last(): pl.pallas_call(last_step, in_specs=[VM] * 4, out_specs=[HB, HB, VM], out_...  3.04 us
    pallas_call x1, Pallas kernels, load_state(): pl.pallas_call(fill_state, in_specs=[HB, HB], out_specs=[VM, VM], out_sha...  3.03 us
    ppermute x2, starting transfers between devices, shift(): lax.ppermute(block, axis, [(i, k) for i, k in route if 0 <= k < count])  2.57 us
    ppermute x2, waiting for transfers between devices, shift(): lax.ppermute(block, axis, [(i, k) for i, k in route if 0 <= k < count])  1.9 us
  transfers between devices with their start and end apart: 10, of which 8 were waited for; matrix products, arithmetic and copies ran while one was open for 0% of the time, Pallas kernels for 29%

profile of v3, /device:TPU:24, one launch (start us, length us, event | category | flops | bytes accessed | tf_op | source)
XLA Modules:
  0.0 52.3 jit_solution(2084875141095308878)
XLA Ops:
  0.6 1.0 %pack_rows.1 = (f32[8,8,256]{2,1,0:T(8,128)S(1)}, f32[8,8,256]{2,1,0:T(8,128)S(1)}) custom-call(f32[8,256,256]{2,1,0:T(8,128)} %a_bot.1, f32[8,256,256]{2,1,0:T(8,128)} %a_bot.1, f32[8,256,256]{2,1,0:T(8,128)} %q_bot.1, f32[8,256,256]{2,1,0:T(8,128)} %q_bot.1), custom_call_target="tpu_custom_call" | custom-call | tf_op jit(solution)/shard_map/pack_rows/pallas_call | solution.py:69
  1.6 2.1 %collective-permute-start = (f32[8,8,256]{2,1,0:T(8,128)S(1)}, f32[8,8,256]{2,1,0:T(8,128)S(1)}, u32[]{:S(2)}, u32[]{:S(2)}) collective-permute-start(f32[8,8,256]{2,1,0:T(8,128)S(1)} %get-tuple-element.30), channel_id=1, source_target_pairs={{1,2},{2,1},{5,6},{6,5},{9,10},{10,9},{13,14},{14,13},{17,18},{18,... | collective-permute-start | bytes 196616 | tf_op jit(solution)/shard_map/ppermute | solution.py:599
  3.7 0.1 collective-permute-start.1
  3.8 3.0 %load_state.1 = (f32[4,8,288,128]{3,2,1,0:T(8,128)S(1)}, f32[2,288,128]{2,1,0:T(8,128)S(1)}) custom-call(f32[8,256,256]{2,1,0:T(8,128)} %a_bot.1, f32[8,256,256]{2,1,0:T(8,128)} %q_bot.1), custom_call_target="tpu_custom_call" | custom-call | tf_op jit(solution)/shard_map/load_state/pallas_call | solution.py:126
  6.8 0.3 collective-permute-done.second_in
  7.2 0.0 collective-permute-done.1.first_in
  7.2 0.2 pack_columns.1
  7.4 2.0 %collective-permute-start.3 = (f32[17,8,128]{2,1,0:T(8,128)S(1)}, f32[17,8,128]{2,1,0:T(8,128)S(1)}, u32[]{:S(2)}, u32[]{:S(2)}) collective-permute-start(f32[17,8,128]{2,1,0:T(8,128)S(1)} %get-tuple-element.40), channel_id=1, source_target_pairs={{0,4},{4,0},{8,12},{12,8},{16,20},{20,16},{24,28},{28,24},{32,36},... | collective-permute-start | bytes 208904 | tf_op jit(solution)/shard_map/ppermute | solution.py:599
  9.4 1.3 %collective-permute-start.2 = (f32[17,8,128]{2,1,0:T(8,128)S(1)}, f32[17,8,128]{2,1,0:T(8,128)S(1)}, u32[]{:S(2)}, u32[]{:S(2)}) collective-permute-start(f32[17,8,128]{2,1,0:T(8,128)S(1)} %get-tuple-element.42), channel_id=1, source_target_pairs={{4,8},{12,16},{20,24},{28,32},{36,40},{44,48},{52,56},{60,64},{68,... | collective-permute-start | bytes 208904 | tf_op jit(solution)/shard_map/ppermute | solution.py:605
  10.7 9.1 %main_even.1 = (f32[4,8,288,128]{3,2,1,0:T(8,128)S(1)}, f32[8,256,256]{2,1,0:T(8,128)S(1)}) custom-call(f32[4,8,288,128]{3,2,1,0:T(8,128)S(1)} %get-tuple-element.32.state), custom_call_target="tpu_custom_call" | custom-call | flops 1000000000 | bytes 30000000 | tf_op jit(solution)/shard_map/main_even/pallas_call | solution.py:311
  19.8 1.3 %collective-permute-start.4 = (f32[17,8,128]{2,1,0:T(8,128)S(1)}, f32[17,8,128]{2,1,0:T(8,128)S(1)}, u32[]{:S(2)}, u32[]{:S(2)}) collective-permute-start(f32[17,8,128]{2,1,0:T(8,128)S(1)} %get-tuple-element.42), channel_id=1, source_target_pairs={{8,4},{16,12},{24,20},{32,28},{40,36},{48,44},{56,52},{64,60},{72,... | collective-permute-start | bytes 208904 | tf_op jit(solution)/shard_map/ppermute | solution.py:605
  21.1 0.2 collective-permute-done.2.up_in
  21.3 0.0 copy-start
  21.3 0.0 collective-permute-done.3.inner_in
  21.3 1.7 %collective-permute-done.4.down_in = f32[17,8,128]{2,1,0:T(8,128)S(1)} collective-permute-done((f32[17,8,128]{2,1,0:T(8,128)S(1)}, f32[17,8,128]{2,1,0:T(8,128)S(1)}, u32[]{:S(2)}, u32[]{:S(2)}) %collective-permute-start.4) | collective-permute-done | bytes 69664 | tf_op jit(solution)/shard_map/ppermute | solution.py:605
  23.0 3.4 %strip_steps.1 = (f32[4,288,128]{2,1,0:T(8,128)S(1)}, f32[8,256,256]{2,1,0:T(8,128)S(1)}, f32[32,128]{1,0:T(8,128)S(1)}) custom-call(f32[2,288,128]{2,1,0:T(8,128)S(1)} %get-tuple-element.39.edges, f32[17,8,128]{2,1,0:T(8,128)S(1)} %collective-permute-done.3.inner_in, ...), custom_call_target="tpu_custom_call", output_to_operand_aliasing={{1}: (4, {})} | custom-call | tf_op jit(solution)/shard_map/strip_steps/pallas_call | solution.py:444
  26.4 4.3 %collective-permute-start.5 = (f32[32,32]{1,0:T(8,128)S(1)}, f32[32,32]{1,0:T(8,128)S(1)}, u32[]{:S(2)}, u32[]{:S(2)}) collective-permute-start(f32[32,32]{1,0:T(8,128)S(1)} %bitcast.1), channel_id=1, source_target_pairs={{0,4},{4,0},{8,12},{12,8},{16,20},{20,16},{24,28},{28,24},{32,36},... | collective-permute-start | bytes 12296 | tf_op jit(solution)/shard_map/ppermute | solution.py:599
  30.6 1.7 %collective-permute-done.5 = f32[32,32]{1,0:T(8,128)S(1)} collective-permute-done((f32[32,32]{1,0:T(8,128)S(1)}, f32[32,32]{1,0:T(8,128)S(1)}, u32[]{:S(2)}, u32[]{:S(2)}) %collective-permute-start.5) | collective-permute-done | bytes 4128 | tf_op jit(solution)/shard_map/ppermute | solution.py:599
  32.4 0.1 pad_maximum_fusion.2
  32.4 8.0 %collective-permute-start.7 = (f32[32,64]{1,0:T(8,128)S(1)}, f32[32,64]{1,0:T(8,128)S(1)}, u32[]{:S(2)}, u32[]{:S(2)}) collective-permute-start(f32[32,64]{1,0:T(8,128)S(1)} %pad_maximum_fusion.2), channel_id=1, source_target_pairs={{8,16},{12,20},{16,8},{20,12},{24,32},{28,36},{32,24},{36,28},{40,... | collective-permute-start | bytes 24584 | tf_op jit(solution)/shard_map/ppermute | solution.py:599
  40.5 0.1 collective-permute-start.6
  40.6 0.0 copy-done
  40.6 0.0 copy-start.1
  40.6 3.0 %last_step.1 = (f32[8,256,256]{2,1,0:T(8,128)}, f32[8,256,256]{2,1,0:T(8,128)}, f32[192,256]{1,0:T(8,128)S(1)}) custom-call(f32[4,8,288,128]{3,2,1,0:T(8,128)S(1)} %get-tuple-element.38.state, f32[4,288,128]{2,1,0:T(8,128)S(1)} %get-tuple-element.44.strips, f32[8,256,256]{2,1,0:T(8,128)S(1)} %get-tuple-element.45.guard, f32[224,256]{1,0:T(8,128)S(1)} %copy-done), custom_call_target="tpu_custom_call" | custom-call | flops 1000000000 | bytes 10000000 | tf_op jit(solution)/shard_map/last_step/pallas_call | solution.py:518
  43.6 1.1 %collective-permute-done.7 = f32[32,64]{1,0:T(8,128)S(1)} collective-permute-done((f32[32,64]{1,0:T(8,128)S(1)}, f32[32,64]{1,0:T(8,128)S(1)}, u32[]{:S(2)}, u32[]{:S(2)}) %collective-permute-start.7) | collective-permute-done | bytes 8224 | tf_op jit(solution)/shard_map/ppermute | solution.py:599
  44.7 0.5 collective-permute-done.6
  45.2 0.1 pad_maximum_fusion.1
  45.3 0.1 collective-permute-start.8
  45.4 1.2 %collective-permute-done.8 = f32[32,192]{1,0:T(8,128)S(1)} collective-permute-done((f32[32,192]{1,0:T(8,128)S(1)}, f32[32,192]{1,0:T(8,128)S(1)}, u32[]{:S(2)}, u32[]{:S(2)}) %collective-permute-start.8) | collective-permute-done | bytes 24608 | tf_op jit(solution)/shard_map/ppermute | solution.py:599
  46.6 0.1 pad_maximum_fusion.low
  46.7 1.2 %collective-permute-start.9 = (f32[64,192]{1,0:T(8,128)S(1)}, f32[64,192]{1,0:T(8,128)S(1)}, u32[]{:S(2)}, u32[]{:S(2)}) collective-permute-start(f32[64,192]{1,0:T(8,128)S(1)} %pad_maximum_fusion.low), channel_id=1, source_target_pairs={{0,2},{1,3},{2,0},{3,1},{4,6},{5,7},{6,4},{7,5},{8,10},{9,11},{10,... | collective-permute-start | bytes 147464 | tf_op jit(solution)/shard_map/ppermute | solution.py:599
  47.9 3.1 %collective-permute-done.9.high = f32[64,192]{1,0:T(8,128)S(1)} collective-permute-done((f32[64,192]{1,0:T(8,128)S(1)}, f32[64,192]{1,0:T(8,128)S(1)}, u32[]{:S(2)}, u32[]{:S(2)}) %collective-permute-start.9) | collective-permute-done | bytes 49184 | tf_op jit(solution)/shard_map/ppermute | solution.py:599
  51.0 0.0 copy-done.1
  51.0 1.3 %etch.1 = f32[256,256]{1,0:T(8,128)} custom-call(f32[64,192]{1,0:T(8,128)S(1)} %pad_maximum_fusion.low, f32[64,192]{1,0:T(8,128)S(1)} %collective-permute-done.9.high, f32[8,256,256]{2,1,0:T(8,128)S(1)} %get-tuple-element.45.guard, f32[4,32,128]{2,1,0:T(8,128)S(1)} %copy-done.1, f32[192,256]{1,0:T(8,128)S(1)} %get-tuple-element.52.cols), custom_call_target="tpu_custom_call" | custom-call | tf_op jit(solution)/shard_map/etch/pallas_call | solution.py:586
  (1 shorter events, 0.0 us)
Async XLA Ops:
  1.6 5.6 %collective-permute-start = (f32[8,8,256]{2,1,0:T(8,128)S(1)}, f32[8,8,256]{2,1,0:T(8,128)S(1)}, u32[]{:S(2)}, u32[]{:S(2)}) collective-permute-start(f32[8,8,256]{2,1,0:T(8,128)S(1)} %get-tuple-element.30), channel_id=1, source_target_pairs={{1,2},{2,1},{5,6},{6,5},{9,10},{10,9},{13,14},{14,13},{17,18},{18,... | collective-permute-start | bytes 196616 | tf_op jit(solution)/shard_map/ppermute | solution.py:599
  3.7 3.5 %collective-permute-start.1 = (f32[8,8,256]{2,1,0:T(8,128)S(1)}, f32[8,8,256]{2,1,0:T(8,128)S(1)}, u32[]{:S(2)}, u32[]{:S(2)}) collective-permute-start(f32[8,8,256]{2,1,0:T(8,128)S(1)} %get-tuple-element.31), channel_id=1, source_target_pairs={{0,1},{1,0},{2,3},{3,2},{4,5},{5,4},{6,7},{7,6},{8,9},{9,8},{10,11... | collective-permute-start | bytes 196616 | tf_op jit(solution)/shard_map/ppermute | solution.py:599
  7.4 13.9 %collective-permute-start.3 = (f32[17,8,128]{2,1,0:T(8,128)S(1)}, f32[17,8,128]{2,1,0:T(8,128)S(1)}, u32[]{:S(2)}, u32[]{:S(2)}) collective-permute-start(f32[17,8,128]{2,1,0:T(8,128)S(1)} %get-tuple-element.40), channel_id=1, source_target_pairs={{0,4},{4,0},{8,12},{12,8},{16,20},{20,16},{24,28},{28,24},{32,36},... | collective-permute-start | bytes 208904 | tf_op jit(solution)/shard_map/ppermute | solution.py:599
  9.4 11.9 %collective-permute-start.2 = (f32[17,8,128]{2,1,0:T(8,128)S(1)}, f32[17,8,128]{2,1,0:T(8,128)S(1)}, u32[]{:S(2)}, u32[]{:S(2)}) collective-permute-start(f32[17,8,128]{2,1,0:T(8,128)S(1)} %get-tuple-element.42), channel_id=1, source_target_pairs={{4,8},{12,16},{20,24},{28,32},{36,40},{44,48},{52,56},{60,64},{68,... | collective-permute-start | bytes 208904 | tf_op jit(solution)/shard_map/ppermute | solution.py:605
  19.8 3.2 %collective-permute-start.4 = (f32[17,8,128]{2,1,0:T(8,128)S(1)}, f32[17,8,128]{2,1,0:T(8,128)S(1)}, u32[]{:S(2)}, u32[]{:S(2)}) collective-permute-start(f32[17,8,128]{2,1,0:T(8,128)S(1)} %get-tuple-element.42), channel_id=1, source_target_pairs={{8,4},{16,12},{24,20},{32,28},{40,36},{48,44},{56,52},{64,60},{72,... | collective-permute-start | bytes 208904 | tf_op jit(solution)/shard_map/ppermute | solution.py:605
  21.3 19.3 %copy-start = (f32[224,256]{1,0:T(8,128)S(1)}, f32[224,256]{1,0:T(8,128)}, u32[]{:S(2)}) copy-start(f32[224,256]{1,0:T(8,128)} %constant.4.clone.col_ref) | copy-start | bytes 688132
  26.4 6.0 %collective-permute-start.5 = (f32[32,32]{1,0:T(8,128)S(1)}, f32[32,32]{1,0:T(8,128)S(1)}, u32[]{:S(2)}, u32[]{:S(2)}) collective-permute-start(f32[32,32]{1,0:T(8,128)S(1)} %bitcast.1), channel_id=1, source_target_pairs={{0,4},{4,0},{8,12},{12,8},{16,20},{20,16},{24,28},{28,24},{32,36},... | collective-permute-start | bytes 12296 | tf_op jit(solution)/shard_map/ppermute | solution.py:599
  32.4 12.2 %collective-permute-start.7 = (f32[32,64]{1,0:T(8,128)S(1)}, f32[32,64]{1,0:T(8,128)S(1)}, u32[]{:S(2)}, u32[]{:S(2)}) collective-permute-start(f32[32,64]{1,0:T(8,128)S(1)} %pad_maximum_fusion.2), channel_id=1, source_target_pairs={{8,16},{12,20},{16,8},{20,12},{24,32},{28,36},{32,24},{36,28},{40,... | collective-permute-start | bytes 24584 | tf_op jit(solution)/shard_map/ppermute | solution.py:599
  40.5 4.7 %collective-permute-start.6 = (f32[32,64]{1,0:T(8,128)S(1)}, f32[32,64]{1,0:T(8,128)S(1)}, u32[]{:S(2)}, u32[]{:S(2)}) collective-permute-start(f32[32,64]{1,0:T(8,128)S(1)} %pad_maximum_fusion.2), channel_id=1, source_target_pairs={{0,8},{4,12},{8,0},{12,4},{16,24},{20,28},{24,16},{28,20},{32,40},... | collective-permute-start | bytes 24584 | tf_op jit(solution)/shard_map/ppermute | solution.py:599
  40.6 10.4 %copy-start.1 = (f32[4,32,128]{2,1,0:T(8,128)S(1)}, f32[4,32,128]{2,1,0:T(8,128)}, u32[]{:S(2)}) copy-start(f32[4,32,128]{2,1,0:T(8,128)} %constant.5.clone.row_ref) | copy-start | bytes 196612
  45.3 1.3 %collective-permute-start.8 = (f32[32,192]{1,0:T(8,128)S(1)}, f32[32,192]{1,0:T(8,128)S(1)}, u32[]{:S(2)}, u32[]{:S(2)}) collective-permute-start(f32[32,192]{1,0:T(8,128)S(1)} %pad_maximum_fusion.1), channel_id=1, source_target_pairs={{0,1},{1,0},{2,3},{3,2},{4,5},{5,4},{6,7},{7,6},{8,9},{9,8},{10,11... | collective-permute-start | bytes 73736 | tf_op jit(solution)/shard_map/ppermute | solution.py:599
  46.7 4.4 %collective-permute-start.9 = (f32[64,192]{1,0:T(8,128)S(1)}, f32[64,192]{1,0:T(8,128)S(1)}, u32[]{:S(2)}, u32[]{:S(2)}) collective-permute-start(f32[64,192]{1,0:T(8,128)S(1)} %pad_maximum_fusion.low), channel_id=1, source_target_pairs={{0,2},{1,3},{2,0},{3,1},{4,6},{5,7},{6,4},{7,5},{8,10},{9,11},{10,... | collective-permute-start | bytes 147464 | tf_op jit(solution)/shard_map/ppermute | solution.py:599

commit v4 on v3

--- a/solution.py
+++ b/solution.py
@@ -43,6 +43,19 @@
     return pltpu.CompilerParams(vmem_limit_bytes=mib * 1024 * 1024)
 
 
+EARLY_COLUMNS = (0, 1, 4, 6)
+PERIOD = 8
+
+
+def early_column(i):
+    return sum((i % PERIOD == k) * 1 for k in EARLY_COLUMNS)
+
+
+def is_early():
+    place = lax.rem(lax.axis_index("gx"), PERIOD)
+    return functools.reduce(jnp.logical_or, [place == k for k in EARLY_COLUMNS])
+
+
 def vmem(shape):
     return pltpu.VMEM(shape, F32)
 
@@ -119,7 +132,7 @@
             return 0
 
         first = (BASE + size * p) // SUBS
-        lax.fori_loop(first, first + size // SUBS, body, 0, unroll=2)
+        lax.fori_loop(first, first + size // SUBS, body, 0, unroll=4)
 
 
 def load_state(acid, quench):
@@ -248,7 +261,7 @@
 def main_steps(role, state, *refs):
     out, guard, one, two, sums, total, matrix = refs[-7:]
 
-    @pl.when(lax.rem(lax.axis_index("gx"), 2) == role)
+    @pl.when(is_early() == (role == 0))
     def _():
         main_part(state, out, guard, one, two, sums, total, matrix)
 
@@ -325,7 +338,7 @@
         cost_estimate=pl.CostEstimate(
             flops=(10**9, 1)[role], bytes_accessed=(3 * 10**7, 1)[role], transcendentals=0
         ),
-        name=("main_even", "main_odd")[role],
+        name=("main_early", "main_late")[role],
     )(state, *earlier)
 
 
@@ -364,12 +377,14 @@
 def strip_steps(edges, inner_in, up_in, down_in, guard_in, out, guard, density, one, two, sums, total, pooled):
     del guard_in
     even_col = lax.rem(lax.axis_index("gx"), 2) == 0
+    early = is_early()
     place = iota(1) % GROUP
     opens = strip_open()
     matrices = strip_matrix(0), strip_matrix(HALO)
     for j in range(FOLD):
-        left = jnp.where(even_col, up_in[j], inner_in[j])
-        right = jnp.where(even_col, inner_in[j], down_in[j])
+        outer = jnp.where(early, up_in[j], down_in[j])
+        left = jnp.where(even_col, outer, inner_in[j])
+        right = jnp.where(even_col, inner_in[j], outer)
         for m in range(4):
             rows = pl.ds(SUBS * (1 + j + FOLD * (m // 2)), SUBS)
             f = m % 2
@@ -427,7 +442,7 @@
             pooled[rows_at(i - 2), pl.ds(t * LANES, LANES)] = kept[t]
         return 0
 
-    lax.fori_loop(2, 2 + RUN, merge, 0, unroll=2)
+    lax.fori_loop(2, 2 + RUN, merge, 0, unroll=8)
     fine = pooled[...].reshape(TILE, COARSEN, COLS).sum(1)
     col = lax.broadcasted_iota(jnp.int32, (COLS, LANES), 0)
     block = lax.broadcasted_iota(jnp.int32, (COLS, LANES), 1)
@@ -519,7 +534,7 @@
         last_step,
         in_specs=[VM] * 4,
         out_specs=[HB, HB, VM],
-        out_shape=[whole, whole, vmem((6 * TILE, COLS))],
+        out_shape=[whole, whole, vmem((6 * TILE, LANES))],
         scratch_shapes=[
             pltpu.VMEM((2, LAYERS, EXT, LANES), F32),
             pltpu.VMEM((2, EXT, LANES), F32),
@@ -541,17 +556,17 @@
 
 
 def row_table():
-    p = np.arange(TILE)
     me = np.arange(4)[:, None, None, None]
-    k = np.arange(4)[None, None, :, None]
-    i = np.arange(TILE)[None, :, None, None]
-    distance = TILE * ((me ^ k) - me) + p[None, None, None, :] - i
-    return weights(distance).reshape(4, TILE, 4 * TILE)
+    k = np.arange(4)[None, :, None, None]
+    i = np.arange(TILE)[None, None, :, None]
+    p = np.arange(TILE)[None, None, None, :]
+    return weights(TILE * ((me ^ k) - me) + p - i).reshape(4, 4 * TILE, TILE)
 
 
 def column_table():
     c = np.arange(7 * TILE)[:, None] - 3 * TILE
-    return weights(c - np.arange(COLS)[None, :] // COARSEN)
+    j = np.arange(LANES)[None, :]
+    return np.where(j < TILE, weights(c - j), np.float32(0.0))
 
 
 def tile_offsets():
@@ -561,18 +576,37 @@
     return [0 * gx, beside, step, step + beside, -step, -step + beside]
 
 
-def etch(low, high, guard, row_ref, cols, out):
+def product(a, b):
+    return jnp.dot(a, b, precision=lax.Precision.HIGHEST, preferred_element_type=F32)
+
+
+def mix_columns(pair, near, far, cols, out):
+    total = product(pair[...], cols[pl.ds(0, 2 * TILE), :])
+    total += product(near[...], cols[pl.ds(2 * TILE, 2 * TILE), :])
+    out[...] = total + product(far[...], cols[pl.ds(4 * TILE, 2 * TILE), :])
+
+
+def run_mix(pair, near, far, cols):
+    return pl.pallas_call(
+        mix_columns,
+        in_specs=[VM] * 4,
+        out_specs=VM,
+        out_shape=jax.ShapeDtypeStruct((TILE, LANES), F32),
+        compiler_params=params(4),
+        name="mix_columns",
+    )(pair, near, far, cols)
+
+
+def etch(low, high, guard, row_ref, out):
     gy = lax.axis_index("gy")
-    across = sum(
-        jnp.dot(
-            row_ref[gy, :, pl.ds(2 * TILE * n, 2 * TILE)],
-            part[...],
-            precision=lax.Precision.HIGHEST,
-            preferred_element_type=F32,
-        )
-        for n, part in enumerate((low, high))
-    )
-    smooth = jnp.dot(across, cols[...], precision=lax.Precision.HIGHEST, preferred_element_type=F32)
+    every = jnp.concatenate([low[...], high[...]], 1)
+    rows = product(row_ref[gy], every)
+    k = lax.broadcasted_iota(jnp.int32, rows.shape, 0) // TILE
+    rows = jnp.where(k == lax.broadcasted_iota(jnp.int32, rows.shape, 1) // TILE, rows, 0.0)
+    rows = sum(rows[TILE * n : TILE * (n + 1)] for n in range(4))
+    j = lax.broadcasted_iota(jnp.int32, (LANES, COLS), 0) % TILE
+    widen = (j == lax.broadcasted_iota(jnp.int32, (LANES, COLS), 1) // COARSEN).astype(F32)
+    smooth = product(rows, widen)
     factor = 1.0 - LOADING * smooth
     for i in range(TILE):
         rows = pl.ds(COARSEN * i, COARSEN)
@@ -582,15 +616,15 @@
             out[rows, cols_of] = (1.0 - guard[0, rows, cols_of]) * piece
 
 
-def run_etch(low, high, guard, cols):
+def run_etch(low, high, guard):
     return pl.pallas_call(
         etch,
-        in_specs=[VM] * 5,
+        in_specs=[VM] * 4,
         out_specs=VM,
         out_shape=jax.ShapeDtypeStruct((ROWS, COLS), F32),
         compiler_params=params(4),
         name="etch",
-    )(low, high, guard, jnp.asarray(row_table()), cols)
+    )(low, high, guard, jnp.asarray(row_table()))
 
 
 def swap(block, axis, partner):
@@ -599,18 +633,18 @@
     return lax.ppermute(block, axis, route)
 
 
-def shift(block, axis, odd):
-    count = lax.axis_size(axis)
-    route = [(i, i + 2 * odd - 1) for i in range(count) if i % 2 == odd]
-    return lax.ppermute(block, axis, [(i, k) for i, k in route if 0 <= k < count])
-
-
 def inside(i):
     return i ^ 1
 
 
 def outside(i):
     return i - 1 if i % 2 == 0 else i + 1
+
+
+def shift(block, axis, early):
+    count = lax.axis_size(axis)
+    route = [(i, outside(i)) for i in range(count) if early_column(i) == early]
+    return lax.ppermute(block, axis, [(i, k) for i, k in route if 0 <= k < count])
 
 
 def shards(acid_field, quencher_field):
@@ -622,12 +656,12 @@
     state, edges = load_state(acid_field, quencher_field)
     state, edges, second, first = pack_columns(state, edges, second, first)
     inner = swap(first, "gx", inside)
-    up = shift(second, "gx", 1)
-    state_even, guard = run_main(0, state)
-    second, state_even = lax.optimization_barrier((second, state_even))
-    down = shift(second, "gx", 0)
-    up, state_even = lax.optimization_barrier((up, state_even))
-    state, guard = run_main(1, state, state_even, guard)
+    up = shift(second, "gx", 0)
+    state_early, guard = run_main(0, state)
+    second, state_early = lax.optimization_barrier((second, state_early))
+    down = shift(second, "gx", 1)
+    up, inner, state_early = lax.optimization_barrier((up, inner, state_early))
+    state, guard = run_main(1, state, state_early, guard)
     strips, guard, density = run_strips(edges, inner, up, down, guard)
     tile = density[:, :TILE]
     pair = jnp.concatenate([tile, swap(tile, "gx", inside)], 1)
@@ -635,10 +669,10 @@
     near = swap(pair, "gx", lambda i: i ^ 2)
     acid_after, inhibitor, cols = run_last(state, strips, guard)
     near, far, cols = lax.optimization_barrier((near, far, cols))
-    six = jnp.concatenate([pair, near, far], 1)
-    low = jnp.concatenate([six, swap(six, "gy", lambda i: i ^ 1)], 0)
+    mixed = run_mix(pair, near, far, cols)[:, :TILE]
+    low = jnp.concatenate([mixed, swap(mixed, "gy", lambda i: i ^ 1)], 1)
     high = swap(low, "gy", lambda i: i ^ 2)
-    etch_rate = run_etch(low, high, guard, cols)
+    etch_rate = run_etch(low, high, guard)
     return acid_after, inhibitor, etch_rate
 
 

time: 53 us -> 51 us (0.962)
  starting transfers between devices: 20.4 us -> 17.8 us
  waiting for transfers between devices: 9.87 us -> 12.1 us
  Pallas kernels: 20.9 us -> 19.8 us
    ppermute x8, starting transfers between devices: 17.9 us -> 15.3 us  [swap(): return lax.ppermute(block, axis, route)]
    ppermute x8, waiting for transfers between devices: 7.97 us -> 10.2 us  [swap(): return lax.ppermute(block, axis, route)]
    pallas_call x1, Pallas kernels: 3.38 us -> 2.51 us  [run_strips(): pl.pallas_call(strip_steps, in_specs=[VM] * 5, out_specs=[VM] * 3, out_sh...]
    pallas_call x1 -> x2, Pallas kernels: 1.25 us -> 1.42 us  [the longest x1 1.22 us: run_etch(): pl.pallas_call(etch, in_specs=[VM] * 4, out_specs=VM, out_shape=jax.Shape...]
  transfers between devices with their start and end apart: 10 -> 10, of which waited for: 8 -> 7; matrix products, arithmetic and copies ran while one was open for 0% -> 0% of each run, Pallas kernels for 29% -> 29%
where the time goes in v4:
time: 51 us; the launch traced here: 50.8 us
  Pallas kernels  19.8 us (39%)
  starting transfers between devices  17.8 us (35%)
  waiting for transfers between devices  12.1 us (24%)
  between operations  0.77 us (2%)
    ppermute x8, starting transfers between devices, swap(): return lax.ppermute(block, axis, route)  15.3 us
    ppermute x8, waiting for transfers between devices, swap(): return lax.ppermute(block, axis, route)  10.2 us
    pallas_call x2, Pallas kernels, run_main(): pl.pallas_call(functools.partial(main_steps, role), in_specs=[VM] * (1 +...  9.11 us
    pallas_call x1, Pallas kernels, run_last(): pl.pallas_call(last_step, in_specs=[VM] * 4, out_specs=[HB, HB, VM], out_...  3.04 us
    pallas_call x1, Pallas kernels, load_state(): pl.pallas_call(fill_state, in_specs=[HB, HB], out_specs=[VM, VM], out_sha...  2.64 us
    ppermute x2, starting transfers between devices, shift(): lax.ppermute(block, axis, [(i, k) for i, k in route if 0 <= k < count])  2.57 us
    pallas_call x1, Pallas kernels, run_strips(): pl.pallas_call(strip_steps, in_specs=[VM] * 5, out_specs=[VM] * 3, out_sh...  2.51 us
    ppermute x2, waiting for transfers between devices, shift(): lax.ppermute(block, axis, [(i, k) for i, k in route if 0 <= k < count])  1.88 us
  transfers between devices with their start and end apart: 10, of which 7 were waited for; matrix products, arithmetic and copies ran while one was open for 0% of the time, Pallas kernels for 29%

profile of v4, /device:TPU:24, one launch (start us, length us, event | category | flops | bytes accessed | tf_op | source)
XLA Modules:
  0.0 50.8 jit_solution(4479158586485681240)
XLA Ops:
  0.6 1.0 %pack_rows.1 = (f32[8,8,256]{2,1,0:T(8,128)S(1)}, f32[8,8,256]{2,1,0:T(8,128)S(1)}) custom-call(f32[8,256,256]{2,1,0:T(8,128)} %a_bot.1, f32[8,256,256]{2,1,0:T(8,128)} %a_bot.1, f32[8,256,256]{2,1,0:T(8,128)} %q_bot.1, f32[8,256,256]{2,1,0:T(8,128)} %q_bot.1), custom_call_target="tpu_custom_call" | custom-call | tf_op jit(solution)/shard_map/pack_rows/pallas_call | solution.py:82
  1.6 2.1 %collective-permute-start = (f32[8,8,256]{2,1,0:T(8,128)S(1)}, f32[8,8,256]{2,1,0:T(8,128)S(1)}, u32[]{:S(2)}, u32[]{:S(2)}) collective-permute-start(f32[8,8,256]{2,1,0:T(8,128)S(1)} %get-tuple-element.31), channel_id=1, source_target_pairs={{1,2},{2,1},{5,6},{6,5},{9,10},{10,9},{13,14},{14,13},{17,18},{18,... | collective-permute-start | bytes 196616 | tf_op jit(solution)/shard_map/ppermute | solution.py:633
  3.7 0.1 collective-permute-start.1
  3.8 2.6 %load_state.1 = (f32[4,8,288,128]{3,2,1,0:T(8,128)S(1)}, f32[2,288,128]{2,1,0:T(8,128)S(1)}) custom-call(f32[8,256,256]{2,1,0:T(8,128)} %a_bot.1, f32[8,256,256]{2,1,0:T(8,128)} %q_bot.1), custom_call_target="tpu_custom_call" | custom-call | tf_op jit(solution)/shard_map/load_state/pallas_call | solution.py:139
  6.4 0.7 %collective-permute-done.second_in = f32[8,8,256]{2,1,0:T(8,128)S(1)} collective-permute-done((f32[8,8,256]{2,1,0:T(8,128)S(1)}, f32[8,8,256]{2,1,0:T(8,128)S(1)}, u32[]{:S(2)}, u32[]{:S(2)}) %collective-permute-start) | collective-permute-done | bytes 65568 | tf_op jit(solution)/shard_map/ppermute | solution.py:633
  7.2 0.0 collective-permute-done.1.first_in
  7.2 0.2 pack_columns.1
  7.4 2.0 %collective-permute-start.3 = (f32[17,8,128]{2,1,0:T(8,128)S(1)}, f32[17,8,128]{2,1,0:T(8,128)S(1)}, u32[]{:S(2)}, u32[]{:S(2)}) collective-permute-start(f32[17,8,128]{2,1,0:T(8,128)S(1)} %get-tuple-element.35), channel_id=1, source_target_pairs={{0,4},{4,0},{8,12},{12,8},{16,20},{20,16},{24,28},{28,24},{32,36},... | collective-permute-start | bytes 208904 | tf_op jit(solution)/shard_map/ppermute | solution.py:633
  9.4 1.3 %collective-permute-start.2 = (f32[17,8,128]{2,1,0:T(8,128)S(1)}, f32[17,8,128]{2,1,0:T(8,128)S(1)}, u32[]{:S(2)}, u32[]{:S(2)}) collective-permute-start(f32[17,8,128]{2,1,0:T(8,128)S(1)} %get-tuple-element.44), channel_id=1, source_target_pairs={{8,4},{12,16},{20,24},{28,32},{40,36},{44,48},{52,56},{60,64},{72,... | collective-permute-start | bytes 208904 | tf_op jit(solution)/shard_map/ppermute | solution.py:647
  10.7 9.1 %main_early.1 = (f32[4,8,288,128]{3,2,1,0:T(8,128)S(1)}, f32[8,256,256]{2,1,0:T(8,128)S(1)}) custom-call(f32[4,8,288,128]{3,2,1,0:T(8,128)S(1)} %get-tuple-element.33.state), custom_call_target="tpu_custom_call" | custom-call | flops 1000000000 | bytes 30000000 | tf_op jit(solution)/shard_map/main_early/pallas_call | solution.py:324
  19.8 1.3 %collective-permute-start.4 = (f32[17,8,128]{2,1,0:T(8,128)S(1)}, f32[17,8,128]{2,1,0:T(8,128)S(1)}, u32[]{:S(2)}, u32[]{:S(2)}) collective-permute-start(f32[17,8,128]{2,1,0:T(8,128)S(1)} %get-tuple-element.44), channel_id=1, source_target_pairs={{4,8},{16,12},{24,20},{32,28},{36,40},{48,44},{56,52},{64,60},{68,... | collective-permute-start | bytes 208904 | tf_op jit(solution)/shard_map/ppermute | solution.py:647
  21.1 0.0 collective-permute-done.3.inner_in
  21.1 0.2 collective-permute-done.2.up_in
  21.3 0.0 copy-start.1
  21.3 1.7 %collective-permute-done.4.down_in = f32[17,8,128]{2,1,0:T(8,128)S(1)} collective-permute-done((f32[17,8,128]{2,1,0:T(8,128)S(1)}, f32[17,8,128]{2,1,0:T(8,128)S(1)}, u32[]{:S(2)}, u32[]{:S(2)}) %collective-permute-start.4) | collective-permute-done | bytes 69664 | tf_op jit(solution)/shard_map/ppermute | solution.py:647
  23.0 2.5 %strip_steps.1 = (f32[4,288,128]{2,1,0:T(8,128)S(1)}, f32[8,256,256]{2,1,0:T(8,128)S(1)}, f32[32,128]{1,0:T(8,128)S(1)}) custom-call(f32[2,288,128]{2,1,0:T(8,128)S(1)} %get-tuple-element.41.edges, f32[17,8,128]{2,1,0:T(8,128)S(1)} %collective-permute-done.3.inner_in, ...), custom_call_target="tpu_custom_call", output_to_operand_aliasing={{1}: (4, {})} | custom-call | tf_op jit(solution)/shard_map/strip_steps/pallas_call | solution.py:459
  25.5 0.2 collective-permute-start.5
  25.7 3.6 %collective-permute-done.5 = f32[32,32]{1,0:T(8,128)S(1)} collective-permute-done((f32[32,32]{1,0:T(8,128)S(1)}, f32[32,32]{1,0:T(8,128)S(1)}, u32[]{:S(2)}, u32[]{:S(2)}) %collective-permute-start.5) | collective-permute-done | bytes 4128 | tf_op jit(solution)/shard_map/ppermute | solution.py:633
  29.3 0.1 pad_maximum_fusion.pair
  29.4 10.2 %collective-permute-start.7 = (f32[32,64]{1,0:T(8,128)S(1)}, f32[32,64]{1,0:T(8,128)S(1)}, u32[]{:S(2)}, u32[]{:S(2)}) collective-permute-start(f32[32,64]{1,0:T(8,128)S(1)} %pad_maximum_fusion.pair), channel_id=1, source_target_pairs={{8,16},{12,20},{16,8},{20,12},{24,32},{28,36},{32,24},{36,28},{40,... | collective-permute-start | bytes 24584 | tf_op jit(solution)/shard_map/ppermute | solution.py:633
  39.6 0.1 collective-permute-start.6
  39.7 0.0 copy-done.1
  39.7 0.0 copy-start
  39.7 3.0 %last_step.1 = (f32[8,256,256]{2,1,0:T(8,128)}, f32[8,256,256]{2,1,0:T(8,128)}, f32[192,128]{1,0:T(8,128)S(1)}) custom-call(f32[4,8,288,128]{3,2,1,0:T(8,128)S(1)} %get-tuple-element.40.state, f32[4,288,128]{2,1,0:T(8,128)S(1)} %get-tuple-element.46.strips, f32[8,256,256]{2,1,0:T(8,128)S(1)} %get-tuple-element.47.guard, f32[224,128]{1,0:T(8,128)S(1)} %copy-done.1), custom_call_target="tpu_custom_call" | custom-call | flops 1000000000 | bytes 10000000 | tf_op jit(solution)/shard_map/last_step/pallas_call | solution.py:533
  42.7 0.0 collective-permute-done.7.far
  42.8 1.5 %collective-permute-done.6.near = f32[32,64]{1,0:T(8,128)S(1)} collective-permute-done((f32[32,64]{1,0:T(8,128)S(1)}, f32[32,64]{1,0:T(8,128)S(1)}, u32[]{:S(2)}, u32[]{:S(2)}) %collective-permute-start.6) | collective-permute-done | bytes 8224 | tf_op jit(solution)/shard_map/ppermute | solution.py:633
  44.3 0.2 mix_columns.1
  44.5 0.0 collective-permute-start.8
  44.5 1.2 %collective-permute-done.8 = f32[32,32]{1,0:T(8,128)S(1)} collective-permute-done((f32[32,32]{1,0:T(8,128)S(1)}, f32[32,32]{1,0:T(8,128)S(1)}, u32[]{:S(2)}, u32[]{:S(2)}) %collective-permute-start.8) | collective-permute-done | bytes 4128 | tf_op jit(solution)/shard_map/ppermute | solution.py:633
  45.7 0.1 pad_maximum_fusion.1.low
  45.8 0.6 %collective-permute-start.9 = (f32[32,64]{1,0:T(8,128)S(1)}, f32[32,64]{1,0:T(8,128)S(1)}, u32[]{:S(2)}, u32[]{:S(2)}) collective-permute-start(f32[32,64]{1,0:T(8,128)S(1)} %pad_maximum_fusion.1.low), channel_id=1, source_target_pairs={{0,2},{1,3},{2,0},{3,1},{4,6},{5,7},{6,4},{7,5},{8,10},{9,11},{10,... | collective-permute-start | bytes 24584 | tf_op jit(solution)/shard_map/ppermute | solution.py:633
  46.4 3.1 %collective-permute-done.9.high = f32[32,64]{1,0:T(8,128)S(1)} collective-permute-done((f32[32,64]{1,0:T(8,128)S(1)}, f32[32,64]{1,0:T(8,128)S(1)}, u32[]{:S(2)}, u32[]{:S(2)}) %collective-permute-start.9) | collective-permute-done | bytes 8224 | tf_op jit(solution)/shard_map/ppermute | solution.py:633
  49.5 0.0 copy-done
  49.5 1.2 %etch.1 = f32[256,256]{1,0:T(8,128)} custom-call(f32[32,64]{1,0:T(8,128)S(1)} %pad_maximum_fusion.1.low, f32[32,64]{1,0:T(8,128)S(1)} %collective-permute-done.9.high, f32[8,256,256]{2,1,0:T(8,128)S(1)} %get-tuple-element.47.guard, f32[4,128,32]{2,1,0:T(8,128)S(1)} %copy-done), custom_call_target="tpu_custom_call" | custom-call | tf_op jit(solution)/shard_map/etch/pallas_call | solution.py:620
  (1 shorter events, 0.0 us)
Async XLA Ops:
  1.6 5.6 %collective-permute-start = (f32[8,8,256]{2,1,0:T(8,128)S(1)}, f32[8,8,256]{2,1,0:T(8,128)S(1)}, u32[]{:S(2)}, u32[]{:S(2)}) collective-permute-start(f32[8,8,256]{2,1,0:T(8,128)S(1)} %get-tuple-element.31), channel_id=1, source_target_pairs={{1,2},{2,1},{5,6},{6,5},{9,10},{10,9},{13,14},{14,13},{17,18},{18,... | collective-permute-start | bytes 196616 | tf_op jit(solution)/shard_map/ppermute | solution.py:633
  3.7 3.5 %collective-permute-start.1 = (f32[8,8,256]{2,1,0:T(8,128)S(1)}, f32[8,8,256]{2,1,0:T(8,128)S(1)}, u32[]{:S(2)}, u32[]{:S(2)}) collective-permute-start(f32[8,8,256]{2,1,0:T(8,128)S(1)} %get-tuple-element.32), channel_id=1, source_target_pairs={{0,1},{1,0},{2,3},{3,2},{4,5},{5,4},{6,7},{7,6},{8,9},{9,8},{10,11... | collective-permute-start | bytes 196616 | tf_op jit(solution)/shard_map/ppermute | solution.py:633
  7.4 13.7 %collective-permute-start.3 = (f32[17,8,128]{2,1,0:T(8,128)S(1)}, f32[17,8,128]{2,1,0:T(8,128)S(1)}, u32[]{:S(2)}, u32[]{:S(2)}) collective-permute-start(f32[17,8,128]{2,1,0:T(8,128)S(1)} %get-tuple-element.35), channel_id=1, source_target_pairs={{0,4},{4,0},{8,12},{12,8},{16,20},{20,16},{24,28},{28,24},{32,36},... | collective-permute-start | bytes 208904 | tf_op jit(solution)/shard_map/ppermute | solution.py:633
  9.4 11.9 %collective-permute-start.2 = (f32[17,8,128]{2,1,0:T(8,128)S(1)}, f32[17,8,128]{2,1,0:T(8,128)S(1)}, u32[]{:S(2)}, u32[]{:S(2)}) collective-permute-start(f32[17,8,128]{2,1,0:T(8,128)S(1)} %get-tuple-element.44), channel_id=1, source_target_pairs={{8,4},{12,16},{20,24},{28,32},{40,36},{44,48},{52,56},{60,64},{72,... | collective-permute-start | bytes 208904 | tf_op jit(solution)/shard_map/ppermute | solution.py:647
  19.8 3.2 %collective-permute-start.4 = (f32[17,8,128]{2,1,0:T(8,128)S(1)}, f32[17,8,128]{2,1,0:T(8,128)S(1)}, u32[]{:S(2)}, u32[]{:S(2)}) collective-permute-start(f32[17,8,128]{2,1,0:T(8,128)S(1)} %get-tuple-element.44), channel_id=1, source_target_pairs={{4,8},{16,12},{24,20},{32,28},{36,40},{48,44},{56,52},{64,60},{68,... | collective-permute-start | bytes 208904 | tf_op jit(solution)/shard_map/ppermute | solution.py:647
  21.3 18.4 %copy-start.1 = (f32[224,128]{1,0:T(8,128)S(1)}, f32[224,128]{1,0:T(8,128)}, u32[]{:S(2)}) copy-start(f32[224,128]{1,0:T(8,128)} %constant.4.clone.col_ref) | copy-start | bytes 344068
  25.5 3.8 %collective-permute-start.5 = (f32[32,32]{1,0:T(8,128)S(1)}, f32[32,32]{1,0:T(8,128)S(1)}, u32[]{:S(2)}, u32[]{:S(2)}) collective-permute-start(f32[32,32]{1,0:T(8,128)S(1)} %bitcast.4), channel_id=1, source_target_pairs={{0,4},{4,0},{8,12},{12,8},{16,20},{20,16},{24,28},{28,24},{32,36},... | collective-permute-start | bytes 12296 | tf_op jit(solution)/shard_map/ppermute | solution.py:633
  29.4 13.3 %collective-permute-start.7 = (f32[32,64]{1,0:T(8,128)S(1)}, f32[32,64]{1,0:T(8,128)S(1)}, u32[]{:S(2)}, u32[]{:S(2)}) collective-permute-start(f32[32,64]{1,0:T(8,128)S(1)} %pad_maximum_fusion.pair), channel_id=1, source_target_pairs={{8,16},{12,20},{16,8},{20,12},{24,32},{28,36},{32,24},{36,28},{40,... | collective-permute-start | bytes 24584 | tf_op jit(solution)/shard_map/ppermute | solution.py:633
  39.6 4.7 %collective-permute-start.6 = (f32[32,64]{1,0:T(8,128)S(1)}, f32[32,64]{1,0:T(8,128)S(1)}, u32[]{:S(2)}, u32[]{:S(2)}) collective-permute-start(f32[32,64]{1,0:T(8,128)S(1)} %pad_maximum_fusion.pair), channel_id=1, source_target_pairs={{0,8},{4,12},{8,0},{12,4},{16,24},{20,28},{24,16},{28,20},{32,40},... | collective-permute-start | bytes 24584 | tf_op jit(solution)/shard_map/ppermute | solution.py:633
  39.7 9.8 %copy-start = (f32[4,128,32]{2,1,0:T(8,128)S(1)}, f32[4,128,32]{2,1,0:T(8,128)}, u32[]{:S(2)}) copy-start(f32[4,128,32]{2,1,0:T(8,128)} %constant.5.clone.row_ref) | copy-start | bytes 196612
  44.5 1.2 %collective-permute-start.8 = (f32[32,32]{1,0:T(8,128)S(1)}, f32[32,32]{1,0:T(8,128)S(1)}, u32[]{:S(2)}, u32[]{:S(2)}) collective-permute-start(f32[32,32]{1,0:T(8,128)S(1)} %bitcast.2), channel_id=1, source_target_pairs={{0,1},{1,0},{2,3},{3,2},{4,5},{5,4},{6,7},{7,6},{8,9},{9,8},{10,11... | collective-permute-start | bytes 12296 | tf_op jit(solution)/shard_map/ppermute | solution.py:633
  45.8 3.8 %collective-permute-start.9 = (f32[32,64]{1,0:T(8,128)S(1)}, f32[32,64]{1,0:T(8,128)S(1)}, u32[]{:S(2)}, u32[]{:S(2)}) collective-permute-start(f32[32,64]{1,0:T(8,128)S(1)} %pad_maximum_fusion.1.low), channel_id=1, source_target_pairs={{0,2},{1,3},{2,0},{3,1},{4,6},{5,7},{6,4},{7,5},{8,10},{9,11},{10,... | collective-permute-start | bytes 24584 | tf_op jit(solution)/shard_map/ppermute | solution.py:633

commit v5 on v4

--- a/solution.py
+++ b/solution.py
@@ -446,8 +446,11 @@
     fine = pooled[...].reshape(TILE, COARSEN, COLS).sum(1)
     col = lax.broadcasted_iota(jnp.int32, (COLS, LANES), 0)
     block = lax.broadcasted_iota(jnp.int32, (COLS, LANES), 1)
-    pool = (col // COARSEN == block).astype(F32)
-    coarse = jnp.dot(fine, pool, precision=lax.Precision.HIGHEST, preferred_element_type=F32)
+    pool = (col // COARSEN == block).astype(jnp.bfloat16)
+    high, low = halves(fine)
+    coarse = jnp.dot(high, pool, preferred_element_type=F32) + jnp.dot(
+        low, pool, preferred_element_type=F32
+    )
     wide = lax.broadcasted_iota(jnp.int32, (TILE, LANES), 1)
     mean = 1.0 - coarse * (1.0 / (LAYERS * COARSEN * COARSEN))
     density[...] = jnp.where(wide < TILE, mean, 0.0)
@@ -577,7 +580,10 @@
 
 
 def product(a, b):
-    return jnp.dot(a, b, precision=lax.Precision.HIGHEST, preferred_element_type=F32)
+    a_high, a_low = halves(a)
+    b_high, b_low = halves(b)
+    dot = functools.partial(jnp.dot, preferred_element_type=F32)
+    return dot(a_high, b_high) + (dot(a_low, b_high) + dot(a_high, b_low))
 
 
 def mix_columns(pair, near, far, cols, out):
@@ -597,16 +603,20 @@
     )(pair, near, far, cols)
 
 
-def etch(low, high, guard, row_ref, out):
+def etch(near_in, far_in, guard, row_ref, out):
     gy = lax.axis_index("gy")
-    every = jnp.concatenate([low[...], high[...]], 1)
+    every = jnp.concatenate([near_in[...], far_in[...]], 1)
     rows = product(row_ref[gy], every)
     k = lax.broadcasted_iota(jnp.int32, rows.shape, 0) // TILE
     rows = jnp.where(k == lax.broadcasted_iota(jnp.int32, rows.shape, 1) // TILE, rows, 0.0)
     rows = sum(rows[TILE * n : TILE * (n + 1)] for n in range(4))
     j = lax.broadcasted_iota(jnp.int32, (LANES, COLS), 0) % TILE
     widen = (j == lax.broadcasted_iota(jnp.int32, (LANES, COLS), 1) // COARSEN).astype(F32)
-    smooth = product(rows, widen)
+    high, low = halves(rows)
+    widen = widen.astype(jnp.bfloat16)
+    smooth = jnp.dot(high, widen, preferred_element_type=F32) + jnp.dot(
+        low, widen, preferred_element_type=F32
+    )
     factor = 1.0 - LOADING * smooth
     for i in range(TILE):
         rows = pl.ds(COARSEN * i, COARSEN)

time: 51 us -> 50.8 us (level)
  no operation moved by 1% of the time
where the time goes in v5:
time: 50.8 us; the launch traced here: 50.5 us
  Pallas kernels  19.7 us (39%)
  starting transfers between devices  17.8 us (35%)
  waiting for transfers between devices  12.1 us (24%)
  between operations  0.76 us (1%)
    ppermute x8, starting transfers between devices, swap(): return lax.ppermute(block, axis, route)  15.3 us
    ppermute x8, waiting for transfers between devices, swap(): return lax.ppermute(block, axis, route)  10.3 us
    pallas_call x2, Pallas kernels, run_main(): pl.pallas_call(functools.partial(main_steps, role), in_specs=[VM] * (1 +...  9.11 us
    pallas_call x1, Pallas kernels, run_last(): pl.pallas_call(last_step, in_specs=[VM] * 4, out_specs=[HB, HB, VM], out_...  3.04 us
    pallas_call x1, Pallas kernels, load_state(): pl.pallas_call(fill_state, in_specs=[HB, HB], out_specs=[VM, VM], out_sha...  2.64 us
    ppermute x2, starting transfers between devices, shift(): lax.ppermute(block, axis, [(i, k) for i, k in route if 0 <= k < count])  2.57 us
    pallas_call x1, Pallas kernels, run_strips(): pl.pallas_call(strip_steps, in_specs=[VM] * 5, out_specs=[VM] * 3, out_sh...  2.49 us
    ppermute x2, waiting for transfers between devices, shift(): lax.ppermute(block, axis, [(i, k) for i, k in route if 0 <= k < count])  1.88 us
  transfers between devices with their start and end apart: 10, of which 7 were waited for; matrix products, arithmetic and copies ran while one was open for 0% of the time, Pallas kernels for 29%

profile of v5, /device:TPU:24, one launch (start us, length us, event | category | flops | bytes accessed | tf_op | source)
XLA Modules:
  0.0 50.5 jit_solution(2922785913422268967)
XLA Ops:
  0.6 1.0 %pack_rows.1 = (f32[8,8,256]{2,1,0:T(8,128)S(1)}, f32[8,8,256]{2,1,0:T(8,128)S(1)}) custom-call(f32[8,256,256]{2,1,0:T(8,128)} %a_bot.1, f32[8,256,256]{2,1,0:T(8,128)} %a_bot.1, f32[8,256,256]{2,1,0:T(8,128)} %q_bot.1, f32[8,256,256]{2,1,0:T(8,128)} %q_bot.1), custom_call_target="tpu_custom_call" | custom-call | tf_op jit(solution)/shard_map/pack_rows/pallas_call | solution.py:82
  1.6 2.1 %collective-permute-start = (f32[8,8,256]{2,1,0:T(8,128)S(1)}, f32[8,8,256]{2,1,0:T(8,128)S(1)}, u32[]{:S(2)}, u32[]{:S(2)}) collective-permute-start(f32[8,8,256]{2,1,0:T(8,128)S(1)} %get-tuple-element.31), channel_id=1, source_target_pairs={{1,2},{2,1},{5,6},{6,5},{9,10},{10,9},{13,14},{14,13},{17,18},{18,... | collective-permute-start | bytes 196616 | tf_op jit(solution)/shard_map/ppermute | solution.py:643
  3.7 0.1 collective-permute-start.1
  3.8 2.6 %load_state.1 = (f32[4,8,288,128]{3,2,1,0:T(8,128)S(1)}, f32[2,288,128]{2,1,0:T(8,128)S(1)}) custom-call(f32[8,256,256]{2,1,0:T(8,128)} %a_bot.1, f32[8,256,256]{2,1,0:T(8,128)} %q_bot.1), custom_call_target="tpu_custom_call" | custom-call | tf_op jit(solution)/shard_map/load_state/pallas_call | solution.py:139
  6.4 0.7 %collective-permute-done.second_in = f32[8,8,256]{2,1,0:T(8,128)S(1)} collective-permute-done((f32[8,8,256]{2,1,0:T(8,128)S(1)}, f32[8,8,256]{2,1,0:T(8,128)S(1)}, u32[]{:S(2)}, u32[]{:S(2)}) %collective-permute-start) | collective-permute-done | bytes 65568 | tf_op jit(solution)/shard_map/ppermute | solution.py:643
  7.2 0.0 collective-permute-done.1.first_in
  7.2 0.2 pack_columns.1
  7.4 2.0 %collective-permute-start.3 = (f32[17,8,128]{2,1,0:T(8,128)S(1)}, f32[17,8,128]{2,1,0:T(8,128)S(1)}, u32[]{:S(2)}, u32[]{:S(2)}) collective-permute-start(f32[17,8,128]{2,1,0:T(8,128)S(1)} %get-tuple-element.35), channel_id=1, source_target_pairs={{0,4},{4,0},{8,12},{12,8},{16,20},{20,16},{24,28},{28,24},{32,36},... | collective-permute-start | bytes 208904 | tf_op jit(solution)/shard_map/ppermute | solution.py:643
  9.4 1.3 %collective-permute-start.2 = (f32[17,8,128]{2,1,0:T(8,128)S(1)}, f32[17,8,128]{2,1,0:T(8,128)S(1)}, u32[]{:S(2)}, u32[]{:S(2)}) collective-permute-start(f32[17,8,128]{2,1,0:T(8,128)S(1)} %get-tuple-element.44), channel_id=1, source_target_pairs={{8,4},{12,16},{20,24},{28,32},{40,36},{44,48},{52,56},{60,64},{72,... | collective-permute-start | bytes 208904 | tf_op jit(solution)/shard_map/ppermute | solution.py:657
  10.7 9.1 %main_early.1 = (f32[4,8,288,128]{3,2,1,0:T(8,128)S(1)}, f32[8,256,256]{2,1,0:T(8,128)S(1)}) custom-call(f32[4,8,288,128]{3,2,1,0:T(8,128)S(1)} %get-tuple-element.33.state), custom_call_target="tpu_custom_call" | custom-call | flops 1000000000 | bytes 30000000 | tf_op jit(solution)/shard_map/main_early/pallas_call | solution.py:324
  19.8 1.3 %collective-permute-start.4 = (f32[17,8,128]{2,1,0:T(8,128)S(1)}, f32[17,8,128]{2,1,0:T(8,128)S(1)}, u32[]{:S(2)}, u32[]{:S(2)}) collective-permute-start(f32[17,8,128]{2,1,0:T(8,128)S(1)} %get-tuple-element.44), channel_id=1, source_target_pairs={{4,8},{16,12},{24,20},{32,28},{36,40},{48,44},{56,52},{64,60},{68,... | collective-permute-start | bytes 208904 | tf_op jit(solution)/shard_map/ppermute | solution.py:657
  21.1 0.0 collective-permute-done.3.inner_in
  21.1 0.2 collective-permute-done.2.up_in
  21.3 0.0 copy-start.1
  21.3 1.7 %collective-permute-done.4.down_in = f32[17,8,128]{2,1,0:T(8,128)S(1)} collective-permute-done((f32[17,8,128]{2,1,0:T(8,128)S(1)}, f32[17,8,128]{2,1,0:T(8,128)S(1)}, u32[]{:S(2)}, u32[]{:S(2)}) %collective-permute-start.4) | collective-permute-done | bytes 69664 | tf_op jit(solution)/shard_map/ppermute | solution.py:657
  23.0 2.5 %strip_steps.1 = (f32[4,288,128]{2,1,0:T(8,128)S(1)}, f32[8,256,256]{2,1,0:T(8,128)S(1)}, f32[32,128]{1,0:T(8,128)S(1)}) custom-call(f32[2,288,128]{2,1,0:T(8,128)S(1)} %get-tuple-element.41.edges, f32[17,8,128]{2,1,0:T(8,128)S(1)} %collective-permute-done.3.inner_in, ...), custom_call_target="tpu_custom_call", output_to_operand_aliasing={{1}: (4, {})} | custom-call | tf_op jit(solution)/shard_map/strip_steps/pallas_call | solution.py:462
  25.5 0.2 collective-permute-start.5
  25.7 3.6 %collective-permute-done.5 = f32[32,32]{1,0:T(8,128)S(1)} collective-permute-done((f32[32,32]{1,0:T(8,128)S(1)}, f32[32,32]{1,0:T(8,128)S(1)}, u32[]{:S(2)}, u32[]{:S(2)}) %collective-permute-start.5) | collective-permute-done | bytes 4128 | tf_op jit(solution)/shard_map/ppermute | solution.py:643
  29.3 0.1 pad_maximum_fusion.pair
  29.4 10.2 %collective-permute-start.7 = (f32[32,64]{1,0:T(8,128)S(1)}, f32[32,64]{1,0:T(8,128)S(1)}, u32[]{:S(2)}, u32[]{:S(2)}) collective-permute-start(f32[32,64]{1,0:T(8,128)S(1)} %pad_maximum_fusion.pair), channel_id=1, source_target_pairs={{8,16},{12,20},{16,8},{20,12},{24,32},{28,36},{32,24},{36,28},{40,... | collective-permute-start | bytes 24584 | tf_op jit(solution)/shard_map/ppermute | solution.py:643
  39.5 0.1 collective-permute-start.6
  39.6 0.0 copy-done.1
  39.6 0.0 copy-start
  39.7 3.0 %last_step.1 = (f32[8,256,256]{2,1,0:T(8,128)}, f32[8,256,256]{2,1,0:T(8,128)}, f32[192,128]{1,0:T(8,128)S(1)}) custom-call(f32[4,8,288,128]{3,2,1,0:T(8,128)S(1)} %get-tuple-element.40.state, f32[4,288,128]{2,1,0:T(8,128)S(1)} %get-tuple-element.46.strips, f32[8,256,256]{2,1,0:T(8,128)S(1)} %get-tuple-element.47.guard, f32[224,128]{1,0:T(8,128)S(1)} %copy-done.1), custom_call_target="tpu_custom_call" | custom-call | flops 1000000000 | bytes 10000000 | tf_op jit(solution)/shard_map/last_step/pallas_call | solution.py:536
  42.7 0.0 collective-permute-done.7.far
  42.7 1.5 %collective-permute-done.6.near = f32[32,64]{1,0:T(8,128)S(1)} collective-permute-done((f32[32,64]{1,0:T(8,128)S(1)}, f32[32,64]{1,0:T(8,128)S(1)}, u32[]{:S(2)}, u32[]{:S(2)}) %collective-permute-start.6) | collective-permute-done | bytes 8224 | tf_op jit(solution)/shard_map/ppermute | solution.py:643
  44.3 0.2 mix_columns.1
  44.4 0.0 collective-permute-start.8
  44.4 1.2 %collective-permute-done.8 = f32[32,32]{1,0:T(8,128)S(1)} collective-permute-done((f32[32,32]{1,0:T(8,128)S(1)}, f32[32,32]{1,0:T(8,128)S(1)}, u32[]{:S(2)}, u32[]{:S(2)}) %collective-permute-start.8) | collective-permute-done | bytes 4128 | tf_op jit(solution)/shard_map/ppermute | solution.py:643
  45.6 0.1 pad_maximum_fusion.1.near_in
  45.7 0.6 %collective-permute-start.9 = (f32[32,64]{1,0:T(8,128)S(1)}, f32[32,64]{1,0:T(8,128)S(1)}, u32[]{:S(2)}, u32[]{:S(2)}) collective-permute-start(f32[32,64]{1,0:T(8,128)S(1)} %pad_maximum_fusion.1.near_in), channel_id=1, source_target_pairs={{0,2},{1,3},{2,0},{3,1},{4,6},{5,7},{6,4},{7,5},{8,10},{9,11},{10,... | collective-permute-start | bytes 24584 | tf_op jit(solution)/shard_map/ppermute | solution.py:643
  46.3 3.1 %collective-permute-done.9.far_in = f32[32,64]{1,0:T(8,128)S(1)} collective-permute-done((f32[32,64]{1,0:T(8,128)S(1)}, f32[32,64]{1,0:T(8,128)S(1)}, u32[]{:S(2)}, u32[]{:S(2)}) %collective-permute-start.9) | collective-permute-done | bytes 8224 | tf_op jit(solution)/shard_map/ppermute | solution.py:643
  49.5 0.0 copy-done
  49.5 1.1 %etch.1 = f32[256,256]{1,0:T(8,128)} custom-call(f32[32,64]{1,0:T(8,128)S(1)} %pad_maximum_fusion.1.near_in, f32[32,64]{1,0:T(8,128)S(1)} %collective-permute-done.9.far_in, f32[8,256,256]{2,1,0:T(8,128)S(1)} %get-tuple-element.47.guard, f32[4,128,32]{2,1,0:T(8,128)S(1)} %copy-done), custom_call_target="tpu_custom_call" | custom-call | tf_op jit(solution)/shard_map/etch/pallas_call | solution.py:630
  (1 shorter events, 0.0 us)
Async XLA Ops:
  1.6 5.6 %collective-permute-start = (f32[8,8,256]{2,1,0:T(8,128)S(1)}, f32[8,8,256]{2,1,0:T(8,128)S(1)}, u32[]{:S(2)}, u32[]{:S(2)}) collective-permute-start(f32[8,8,256]{2,1,0:T(8,128)S(1)} %get-tuple-element.31), channel_id=1, source_target_pairs={{1,2},{2,1},{5,6},{6,5},{9,10},{10,9},{13,14},{14,13},{17,18},{18,... | collective-permute-start | bytes 196616 | tf_op jit(solution)/shard_map/ppermute | solution.py:643
  3.7 3.5 %collective-permute-start.1 = (f32[8,8,256]{2,1,0:T(8,128)S(1)}, f32[8,8,256]{2,1,0:T(8,128)S(1)}, u32[]{:S(2)}, u32[]{:S(2)}) collective-permute-start(f32[8,8,256]{2,1,0:T(8,128)S(1)} %get-tuple-element.32), channel_id=1, source_target_pairs={{0,1},{1,0},{2,3},{3,2},{4,5},{5,4},{6,7},{7,6},{8,9},{9,8},{10,11... | collective-permute-start | bytes 196616 | tf_op jit(solution)/shard_map/ppermute | solution.py:643
  7.4 13.7 %collective-permute-start.3 = (f32[17,8,128]{2,1,0:T(8,128)S(1)}, f32[17,8,128]{2,1,0:T(8,128)S(1)}, u32[]{:S(2)}, u32[]{:S(2)}) collective-permute-start(f32[17,8,128]{2,1,0:T(8,128)S(1)} %get-tuple-element.35), channel_id=1, source_target_pairs={{0,4},{4,0},{8,12},{12,8},{16,20},{20,16},{24,28},{28,24},{32,36},... | collective-permute-start | bytes 208904 | tf_op jit(solution)/shard_map/ppermute | solution.py:643
  9.4 11.9 %collective-permute-start.2 = (f32[17,8,128]{2,1,0:T(8,128)S(1)}, f32[17,8,128]{2,1,0:T(8,128)S(1)}, u32[]{:S(2)}, u32[]{:S(2)}) collective-permute-start(f32[17,8,128]{2,1,0:T(8,128)S(1)} %get-tuple-element.44), channel_id=1, source_target_pairs={{8,4},{12,16},{20,24},{28,32},{40,36},{44,48},{52,56},{60,64},{72,... | collective-permute-start | bytes 208904 | tf_op jit(solution)/shard_map/ppermute | solution.py:657
  19.8 3.2 %collective-permute-start.4 = (f32[17,8,128]{2,1,0:T(8,128)S(1)}, f32[17,8,128]{2,1,0:T(8,128)S(1)}, u32[]{:S(2)}, u32[]{:S(2)}) collective-permute-start(f32[17,8,128]{2,1,0:T(8,128)S(1)} %get-tuple-element.44), channel_id=1, source_target_pairs={{4,8},{16,12},{24,20},{32,28},{36,40},{48,44},{56,52},{64,60},{68,... | collective-permute-start | bytes 208904 | tf_op jit(solution)/shard_map/ppermute | solution.py:657
  21.3 18.3 %copy-start.1 = (f32[224,128]{1,0:T(8,128)S(1)}, f32[224,128]{1,0:T(8,128)}, u32[]{:S(2)}) copy-start(f32[224,128]{1,0:T(8,128)} %constant.4.clone.col_ref) | copy-start | bytes 344068
  25.5 3.8 %collective-permute-start.5 = (f32[32,32]{1,0:T(8,128)S(1)}, f32[32,32]{1,0:T(8,128)S(1)}, u32[]{:S(2)}, u32[]{:S(2)}) collective-permute-start(f32[32,32]{1,0:T(8,128)S(1)} %bitcast.4), channel_id=1, source_target_pairs={{0,4},{4,0},{8,12},{12,8},{16,20},{20,16},{24,28},{28,24},{32,36},... | collective-permute-start | bytes 12296 | tf_op jit(solution)/shard_map/ppermute | solution.py:643
  29.4 13.3 %collective-permute-start.7 = (f32[32,64]{1,0:T(8,128)S(1)}, f32[32,64]{1,0:T(8,128)S(1)}, u32[]{:S(2)}, u32[]{:S(2)}) collective-permute-start(f32[32,64]{1,0:T(8,128)S(1)} %pad_maximum_fusion.pair), channel_id=1, source_target_pairs={{8,16},{12,20},{16,8},{20,12},{24,32},{28,36},{32,24},{36,28},{40,... | collective-permute-start | bytes 24584 | tf_op jit(solution)/shard_map/ppermute | solution.py:643
  39.5 4.7 %collective-permute-start.6 = (f32[32,64]{1,0:T(8,128)S(1)}, f32[32,64]{1,0:T(8,128)S(1)}, u32[]{:S(2)}, u32[]{:S(2)}) collective-permute-start(f32[32,64]{1,0:T(8,128)S(1)} %pad_maximum_fusion.pair), channel_id=1, source_target_pairs={{0,8},{4,12},{8,0},{12,4},{16,24},{20,28},{24,16},{28,20},{32,40},... | collective-permute-start | bytes 24584 | tf_op jit(solution)/shard_map/ppermute | solution.py:643
  39.6 9.8 %copy-start = (f32[4,128,32]{2,1,0:T(8,128)S(1)}, f32[4,128,32]{2,1,0:T(8,128)}, u32[]{:S(2)}) copy-start(f32[4,128,32]{2,1,0:T(8,128)} %constant.5.clone.row_ref) | copy-start | bytes 196612
  44.4 1.2 %collective-permute-start.8 = (f32[32,32]{1,0:T(8,128)S(1)}, f32[32,32]{1,0:T(8,128)S(1)}, u32[]{:S(2)}, u32[]{:S(2)}) collective-permute-start(f32[32,32]{1,0:T(8,128)S(1)} %bitcast.2), channel_id=1, source_target_pairs={{0,1},{1,0},{2,3},{3,2},{4,5},{5,4},{6,7},{7,6},{8,9},{9,8},{10,11... | collective-permute-start | bytes 12296 | tf_op jit(solution)/shard_map/ppermute | solution.py:643
  45.7 3.8 %collective-permute-start.9 = (f32[32,64]{1,0:T(8,128)S(1)}, f32[32,64]{1,0:T(8,128)S(1)}, u32[]{:S(2)}, u32[]{:S(2)}) collective-permute-start(f32[32,64]{1,0:T(8,128)S(1)} %pad_maximum_fusion.1.near_in), channel_id=1, source_target_pairs={{0,2},{1,3},{2,0},{3,1},{4,6},{5,7},{6,4},{7,5},{8,10},{9,11},{10,... | collective-permute-start | bytes 24584 | tf_op jit(solution)/shard_map/ppermute | solution.py:643
